TPU v7x, 1024 devices: a whole 4x4x32 slice. The times are simulated.
1024 devices in a mesh: dp: 128 (over x_lo, z, core), fsdp: 8 (over y, x_hi).
Axes of the slice: x: 4 (x_hi: 2, x_lo: 2; x = x_hi * 2 + x_lo), y: 4, z: 32, core: 2. Of those that a mesh axis runs over, the one named last changes fastest.
Arguments:
- activations: bfloat16 [32768, 4096], P('dp', 'fsdp'), may hold values from -6 to 6
- proj_basis: bfloat16 [4096, 512], replicated, may hold values from -0.09375 to 0.09375
- out_grad: bfloat16 [32768, 6144], P('dp', 'fsdp')
- master_weight: float32 [4096, 6144], P('dp', 'fsdp'), may hold values from -4 to 4
- first_moment: float32 [512, 6144], P('dp', 'fsdp'), may hold values from -3 to 3
- second_moment: float32 [512, 6144], P('dp', 'fsdp'), may hold values from 0.0001 to 0.01
Outputs:
- new_weight: float32 [4096, 6144], P('dp')
- new_first: float32 [512, 6144], P('dp', 'fsdp')
- new_second: float32 [512, 6144], P('dp', 'fsdp')
All inputs are finite; a program needn't handle non-finite values.
Results may differ from a plain program's by a relative error of at most 0.0024.
Values may be sent and summed in bfloat16 or wider, within the bound.
No kernel may reach another device: no remote copies, remote signals or barrier semaphores. Data moves between devices by JAX's collectives and lax.ppermute only.
A program may use at most 32 MiB of HBM per device.

v0:
```python
import jax
import jax.numpy as jnp
from jax import lax
from jax.sharding import PartitionSpec as P

beta_one = 0.9
beta_two = 0.999
adam_step = 2
eps_value = 1e-08
step_size = 1.0


def body(activations, proj_basis, out_grad, master_weight, first_moment, second_moment):
    summed = jnp.dot(
        lax.all_gather(activations, "fsdp", axis=1, tiled=True),
        proj_basis,
        preferred_element_type=jnp.float32,
    )
    coords = summed.astype(jnp.bfloat16)
    partial_grad = lax.dot_general(
        coords, out_grad, (((0,), (0,)), ((), ())), preferred_element_type=jnp.float32
    )
    grad_share = lax.psum_scatter(partial_grad, "dp", scatter_dimension=0, tiled=True)
    new_first = beta_one * first_moment + (1.0 - beta_one) * grad_share
    new_second = beta_two * second_moment + (1.0 - beta_two) * grad_share * grad_share
    correct_one = 1.0 - beta_one**adam_step
    correct_two = 1.0 - beta_two**adam_step
    update = (new_first / correct_one / (jnp.sqrt(new_second / correct_two) + eps_value)).astype(
        jnp.bfloat16
    )
    full_rank = lax.all_gather(update, "dp", axis=0, tiled=True)
    height = master_weight.shape[0]
    basis_rows = lax.dynamic_slice_in_dim(proj_basis, lax.axis_index("dp") * height, height, 0)
    delta = jnp.dot(basis_rows, full_rank, preferred_element_type=jnp.float32)
    fresh_part = master_weight - step_size * delta
    new_weight = lax.all_gather(fresh_part, "fsdp", axis=1, tiled=True)
    return (new_weight, new_first, new_second)


def solution(mesh):
    in_specs = (
        P("dp", "fsdp"),
        P(),
        P("dp", "fsdp"),
        P("dp", "fsdp"),
        P("dp", "fsdp"),
        P("dp", "fsdp"),
    )
    out_specs = (P("dp", None), P("dp", "fsdp"), P("dp", "fsdp"))
    return jax.shard_map(body, mesh=mesh, in_specs=in_specs, out_specs=out_specs, check_vma=False)
```

profile of v0, /device:TPU:1, one launch (start us, length us, event | category | flops | bytes accessed | tf_op | source)
XLA Modules:
  0.0 1088.3 jit_solution(11714671539541467116)
XLA Ops:
  7.2 0.0 copy-start
  7.2 0.0 all-gather.3.cloned.1.call-start
  7.2 0.7 all-gather.3.cloned.1.call-update
  7.9 0.0 copy-start.2
  7.9 0.0 copy-start.3
  7.9 0.0 all-reduce.3.cloned.1.call-start
  8.0 102.5 %all-gather.3.cloned.1.call-done = bf16[256,4096]{1,0:T(8,128)(2,1)} async-done(((bf16[256,512]{1,0:T(8,128)(2,1)}), bf16[256,4096]{1,0:T(8,128)(2,1)}) %all-gather.3.cloned.1.call-update) | async-done | bytes 2097168 | tf_op jit(solution)/shard_map/all_gather | solution.py:15
  110.5 0.0 copy-done
  110.5 5.7 fusion
  116.2 0.0 copy-start.1
  116.2 0.0 all-reduce.3.cloned.1.call-update
  116.2 1.3 dynamic-slice
  118.2 808.2 %all-reduce.3.cloned.1.call-done = f32[512,768]{1,0:T(8,128)} async-done(((f32[512,768]{1,0:T(8,128)}), f32[512,768]{1,0:T(8,128)}) %all-reduce.3.cloned.1.call-update) | async-done | bytes 1572880
  926.4 0.0 copy-done.2
  926.4 0.0 copy-done.3
  926.4 1.4 fusion.4
  927.8 119.4 %all-gather = bf16[128,4,768]{2,1,0:T(4,128)(2,1)S(1)} all-gather(bf16[1,4,768]{2,1,0:T(4,128)(2,1)S(1)} %get-tuple-element.3), channel_id=1, replica_groups=mesh['dp'=128,'fsdp'=8] {'dp'}, dimensions={0}, use_global_device_ids=true | all-gather | bytes 792576 | tf_op jit(solution)/shard_map/all_gather | solution.py:31
  1047.2 0.2 reshape.7
  1047.4 0.0 copy-done.1
  1047.4 1.0 convolution_subtract_fusion
  1048.4 32.2 %all_gather.11 = f32[32,6144]{1,0:T(8,128)S(1)} all-gather(f32[32,768]{1,0:T(8,128)S(1)} %convolution_subtract_fusion), channel_id=1, replica_groups=mesh['dp'=128,'fsdp'=8] {'fsdp'}, dimensions={1}, use_global_device_ids=true | all-gather | bytes 884736 | tf_op jit(solution)/shard_map/all_gather | solution.py:36
  1080.5 0.9 copy.11
Async XLA Ops:
  7.2 103.3 %copy-start = (bf16[256,768]{1,0:T(8,128)(2,1)S(1)}, bf16[256,768]{1,0:T(8,128)(2,1)}, u32[]{:S(2)}) copy-start(bf16[256,768]{1,0:T(8,128)(2,1)} %param.8) | copy-start | bytes 1179652
  7.2 103.3 %all-gather.3.cloned.1.call-start = ((), (), s32[]{:S(2)}) async-start(), calls=%async_computation | async-start | bytes 2359296 | tf_op jit(solution)/shard_map/all_gather | solution.py:15
  7.9 918.5 %copy-start.2 = (f32[4,768]{1,0:T(4,128)S(1)}, f32[4,768]{1,0:T(4,128)}, u32[]{:S(2)}) copy-start(f32[4,768]{1,0:T(4,128)} %param.10) | copy-start | bytes 36868
  7.9 918.5 %copy-start.3 = (f32[4,768]{1,0:T(4,128)S(1)}, f32[4,768]{1,0:T(4,128)}, u32[]{:S(2)}) copy-start(f32[4,768]{1,0:T(4,128)} %param.11) | copy-start | bytes 36868
  7.9 918.5 %all-reduce.3.cloned.1.call-start = ((), (), s32[]{:S(2)}) async-start(), calls=%async_computation.1 | async-start | bytes 3145728
  116.2 931.2 %copy-start.1 = (f32[32,768]{1,0:T(8,128)S(1)}, f32[32,768]{1,0:T(8,128)}, u32[]{:S(2)}) copy-start(f32[32,768]{1,0:T(8,128)} %param.9) | copy-start | bytes 294916
Sparse Core Ops, SparseCore 0:
  12.2 98.2 all-gather.2
  116.3 810.0 all-reduce.2
where the time goes:
time: 1090 us
  waiting for transfers between devices  911 us (84%)
  blocking collectives  152 us (14%)
  between operations  14.7 us (1%)
    unnamed x3, waiting for transfers between devices  809 us
    all_gather x1, blocking collectives, body(): full_rank = lax.all_gather(update, 'dp', axis=0, tiled=True)  119 us
    all_gather x1, waiting for transfers between devices, body(): lax.all_gather(activations, 'fsdp', axis=1, tiled=True)  103 us
    all_gather x1, blocking collectives, body(): new_weight = lax.all_gather(fresh_part, 'fsdp', axis=1, tiled=True)  32.2 us
  transfers between devices with their start and end apart: 2, of which 2 were waited for; matrix products, arithmetic and copies ran while one was open for 0% of the time, Pallas kernels for 0%

commit v1 on v0

v1 whole, which is shorter than its diff:
```python
import jax
import jax.numpy as jnp
from jax import lax
from jax.sharding import Mesh, PartitionSpec as P

beta_one = 0.9
beta_two = 0.999
adam_step = 2
eps_value = 1e-08
step_size = 1.0

f32 = jnp.float32
bf16 = jnp.bfloat16
DP = ("xl", "zh", "zl", "c")
FS = ("y", "xh")


def swap(x, axis):
    return lax.ppermute(x, axis, [(0, 1), (1, 0)])


def exchange(x, axis):
    return lax.all_to_all(x, axis, 0, 0, tiled=False)


def spread(x, axis, n):
    return exchange(jnp.broadcast_to(x[None], (n,) + x.shape), axis)


def pair_sum(x, axis, kind):
    me = lax.axis_index(axis)
    mine = lax.dynamic_index_in_dim(x, me, 0, keepdims=False)
    other = lax.dynamic_index_in_dim(x, 1 - me, 0, keepdims=False)
    return mine + swap(other.astype(kind), axis).astype(f32)


def pair_gather(x, axis):
    me = lax.axis_index(axis)
    other = swap(x, axis)
    first = jnp.where(me == 0, x, other)
    second = jnp.where(me == 0, other, x)
    return jnp.stack([first, second])


def rank_order(sizes, total):
    xl, zh, zl, c = (sizes[a] for a in DP)
    depth = total // (xl * zh * zl * c)
    new = lax.broadcasted_iota(jnp.int32, (total, total), 1)
    j = new % depth
    rest = new // depth
    izh = rest % zh
    rest = rest // zh
    izl = rest % zl
    rest = rest // zl
    ixl = rest % xl
    ic = rest // xl
    old = (((ixl * zh + izh) * zl + izl) * c + ic) * depth + j
    return (lax.broadcasted_iota(jnp.int32, (total, total), 0) == old).astype(bf16)


def build(sizes):
    xl, zh, zl, c = (sizes[a] for a in DP)
    nf = sizes["y"] * sizes["xh"]

    def body(activations, proj_basis, out_grad, master_weight, first_moment, second_moment):
        tokens, feats = activations.shape
        ranks = proj_basis.shape[1]
        width = out_grad.shape[1]
        depth = first_moment.shape[0]
        height = master_weight.shape[0]
        order = rank_order(sizes, ranks)

        part_basis = lax.dynamic_slice_in_dim(proj_basis, lax.axis_index(FS) * feats, feats, 0)
        part = jnp.dot(activations, part_basis, preferred_element_type=f32)
        part = exchange(part.reshape(nf, tokens // nf, ranks), FS)
        own = jnp.sum(part, axis=0).astype(bf16)
        own = jnp.dot(own, order, preferred_element_type=f32).astype(bf16)
        coords = spread(own, FS, nf).reshape(tokens, ranks)

        grad = lax.dot_general(
            coords, out_grad, (((0,), (0,)), ((), ())), preferred_element_type=f32
        )
        grad = pair_sum(grad.reshape(c, ranks // c, width), "c", f32)
        grad = pair_sum(grad.reshape(xl, ranks // c // xl, width), "xl", bf16)
        grad = exchange(grad.reshape(zl, zh * depth, width).astype(bf16), "zl")
        grad = jnp.sum(grad.astype(f32), axis=0)
        grad = exchange(grad.reshape(zh, depth, width), "zh")
        grad = jnp.sum(grad, axis=0)

        new_first = beta_one * first_moment + (1.0 - beta_one) * grad
        new_second = beta_two * second_moment + (1.0 - beta_two) * grad * grad
        correct_one = 1.0 - beta_one**adam_step
        correct_two = 1.0 - beta_two**adam_step
        update = (
            new_first / correct_one / (jnp.sqrt(new_second / correct_two) + eps_value)
        ).astype(bf16)

        full = spread(update, "zh", zh).reshape(zh * depth, width)
        full = spread(full, "zl", zl).reshape(zl * zh * depth, width)
        full = pair_gather(full, "xl").reshape(ranks // c, width)
        full = pair_gather(full, "c").reshape(ranks, width)

        basis_rows = lax.dynamic_slice_in_dim(proj_basis, lax.axis_index(DP) * height, height, 0)
        basis_rows = jnp.dot(basis_rows, order, preferred_element_type=f32).astype(bf16)
        delta = jnp.dot(basis_rows, full, preferred_element_type=f32)
        fresh = master_weight - step_size * delta
        new_weight = spread(fresh, FS, nf)
        new_weight = jnp.concatenate([new_weight[i] for i in range(nf)], axis=1)
        return (new_weight, new_first, new_second)

    return body


def split(mesh):
    names = ("xl", "zh", "zl", "c", "y", "xh")
    return Mesh(mesh.devices.reshape(2, 8, 4, 2, 4, 2), names)


def run_on(fine):
    sizes = dict(fine.shape)
    in_specs = (P(DP, FS), P(), P(DP, FS), P(DP, FS), P(DP, FS), P(DP, FS))
    out_specs = (P(DP, None), P(DP, FS), P(DP, FS))
    return jax.shard_map(
        build(sizes), mesh=fine, in_specs=in_specs, out_specs=out_specs, check_vma=False
    )


def solution(mesh):
    return run_on(split(mesh))
```

time: 1090 us -> 183 us (0.17)
  waiting for transfers between devices: 911 us -> 30 us
  blocking collectives: 152 us -> 105 us
  starting transfers between devices: 0.08 us -> 37.7 us
  between operations: 14.7 us -> 1.09 us
    unnamed x3 -> x0, waiting for transfers between devices: 809 us -> none
    all_gather x2 -> x0, blocking collectives: 152 us -> none  [the longest x1 119 us: body(): full_rank = lax.all_gather(update, 'dp', axis=0, tiled=True)]
    all_to_all x0 -> x5, blocking collectives: none -> 105 us  [exchange(): return lax.all_to_all(x, axis, 0, 0, tiled=False)]
    all_gather x1 -> x0, waiting for transfers between devices: 103 us -> none  [body(): lax.all_gather(activations, 'fsdp', axis=1, tiled=True)]
    ppermute x0 -> x4, starting transfers between devices: none -> 26.8 us  [swap(): return lax.ppermute(x, axis, [(0, 1), (1, 0)])]
    all_to_all x0 -> x2, waiting for transfers between devices: none -> 16.5 us  [exchange(): return lax.all_to_all(x, axis, 0, 0, tiled=False)]
    ppermute x0 -> x4, waiting for transfers between devices: none -> 13.5 us  [swap(): return lax.ppermute(x, axis, [(0, 1), (1, 0)])]
  transfers between devices with their start and end apart: 2 -> 6, of which waited for: 2 -> 6; matrix products, arithmetic and copies ran while one was open for 0% -> 0% of each run, Pallas kernels for 0% -> 0%
where the time goes in v1:
time: 183 us; the launch traced here: 182 us
  blocking collectives  105 us (57%)
  starting transfers between devices  37.7 us (21%)
  waiting for transfers between devices  30 us (16%)
  matrix products  4.29 us (2%)
  local copies, waits for them, and re-layouts  2.12 us (1%)
    all_to_all x5, blocking collectives, exchange(): return lax.all_to_all(x, axis, 0, 0, tiled=False)  105 us
    ppermute x4, starting transfers between devices, swap(): return lax.ppermute(x, axis, [(0, 1), (1, 0)])  26.8 us
    all_to_all x2, waiting for transfers between devices, exchange(): return lax.all_to_all(x, axis, 0, 0, tiled=False)  16.5 us
    ppermute x4, waiting for transfers between devices, swap(): return lax.ppermute(x, axis, [(0, 1), (1, 0)])  13.5 us
    all_to_all x2, starting transfers between devices, exchange(): return lax.all_to_all(x, axis, 0, 0, tiled=False)  10.9 us
  transfers between devices with their start and end apart: 6, of which 6 were waited for; matrix products, arithmetic and copies ran while one was open for 0% of the time, Pallas kernels for 0%

profile of v1, /device:TPU:1, one launch (start us, length us, event | category | flops | bytes accessed | tf_op | source)
XLA Modules:
  0.0 182.0 jit_solution(6403292797593210854)
XLA Ops:
  0.6 0.0 copy-start
  0.7 2.3 %fusion.19 = f32[512,256]{0,1:T(8,128)} fusion(bf16[256,512]{1,0:T(8,128)(2,1)} %param.6, bf16[4096,512]{1,0:T(8,128)(2,1)} %param.7, s32[]{:T(128)S(6)} %select_n.104), kind=kOutput, calls=%fused_computation.45 | convolution fusion | flops 134217728 | bytes 1310724 | tf_op jit(solution)/shard_map/dot_general | solution.py:74
  2.9 7.5 %all-to-all-start = ((f32[8,32,512]{2,1,0:T(8,128)}), f32[8,32,512]{2,1,0:T(8,128)S(1)}, u32[]{:S(2)}, u32[]{:S(2)}) async-start(f32[8,32,512]{2,1,0:T(8,128)} %bitcast.1), calls=%async_computation | async-start | bytes 1048576 | tf_op jit(solution)/shard_map/all_to_all | solution.py:23
  10.4 0.0 copy-start.10
  10.4 0.0 copy-start.12
  10.4 0.0 copy-start.3
  10.5 0.0 copy-start.5
  10.5 0.0 copy-start.7
  10.5 9.0 %all-to-all-done = f32[8,32,512]{2,1,0:T(8,128)S(1)} async-done(((f32[8,32,512]{2,1,0:T(8,128)}), f32[8,32,512]{2,1,0:T(8,128)S(1)}, u32[]{:S(2)}, u32[]{:S(2)}) %all-to-all-start) | async-done | bytes 524320 | tf_op jit(solution)/shard_map/all_to_all | solution.py:23
  19.5 0.3 convolution_convert_fusion
  19.8 0.0 copy-done.10
  19.8 0.0 copy-done.12
  19.8 0.0 copy-done.3
  19.9 0.0 copy-done.5
  19.9 0.0 copy-done.7
  19.9 0.7 broadcast_in_dim.10
  20.6 3.4 %all-to-all-start.1 = ((bf16[8,32,512]{2,1,0:T(8,128)(2,1)}), bf16[8,32,512]{2,1,0:T(8,128)(2,1)S(1)}, u32[]{:S(2)}, u32[]{:S(2)}) async-start(bf16[8,32,512]{2,1,0:T(8,128)(2,1)} %broadcast_in_dim.10), calls=%async_computation.1 | async-start | bytes 524288 | tf_op jit(solution)/shard_map/all_to_all | solution.py:23
  24.0 7.6 %all-to-all-done.1 = bf16[8,32,512]{2,1,0:T(8,128)(2,1)S(1)} async-done(((bf16[8,32,512]{2,1,0:T(8,128)(2,1)}), bf16[8,32,512]{2,1,0:T(8,128)(2,1)S(1)}, u32[]{:S(2)}, u32[]{:S(2)}) %all-to-all-start.1) | async-done | bytes 262176 | tf_op jit(solution)/shard_map/all_to_all | solution.py:23
  31.6 0.1 copy.12
  31.7 0.0 copy-done
  31.7 0.0 copy-start.2
  31.8 0.4 fusion.22
  32.1 0.1 dynamic-slice_bitcast_fusion
  32.2 14.5 %collective-permute-start = (f32[256,768]{1,0:T(8,128)S(1)}, f32[256,768]{1,0:T(8,128)S(1)}, u32[]{:S(2)}, u32[]{:S(2)}) collective-permute-start(f32[256,768]{1,0:T(8,128)S(1)} %dynamic-slice_bitcast_fusion), channel_id=1, source_target_pairs={{0,8},{8,0},{1,9},{9,1},{2,10},{10,2},{3,11},{11,3},{4,12},{12,4},... | collective-permute-start | bytes 2359304 | tf_op jit(solution)/shard_map/ppermute | solution.py:19
  46.7 1.9 %collective-permute-done = f32[256,768]{1,0:T(8,128)S(1)} collective-permute-done((f32[256,768]{1,0:T(8,128)S(1)}, f32[256,768]{1,0:T(8,128)S(1)}, u32[]{:S(2)}, u32[]{:S(2)}) %collective-permute-start) | collective-permute-done | bytes 786464 | tf_op jit(solution)/shard_map/ppermute | solution.py:19
  48.6 0.1 bitcast_add_fusion
  48.7 0.0 copy-start.4
  48.7 0.0 copy-start.6
  48.7 0.0 copy-start.8
  48.7 0.0 copy-start.9
  48.7 0.0 copy-start.11
  48.7 0.0 copy-start.13
  48.8 1.9 %collective-permute-start.1 = (bf16[128,768]{1,0:T(8,128)(2,1)S(1)}, bf16[128,768]{1,0:T(8,128)(2,1)S(1)}, u32[]{:S(2)}, u32[]{:S(2)}) collective-permute-start(bf16[128,768]{1,0:T(8,128)(2,1)S(1)} %fusion.24), channel_id=1, source_target_pairs={{0,512},{512,0},{1,513},{513,1},{2,514},{514,2},{3,515},{515,3},{4... | collective-permute-start | bytes 589832 | tf_op jit(solution)/shard_map/ppermute | solution.py:19
  50.7 6.1 %collective-permute-done.1 = bf16[128,768]{1,0:T(8,128)(2,1)S(1)} collective-permute-done((bf16[128,768]{1,0:T(8,128)(2,1)S(1)}, bf16[128,768]{1,0:T(8,128)(2,1)S(1)}, u32[]{:S(2)}, u32[]{:S(2)}) %collective-permute-start.1) | collective-permute-done | bytes 196640 | tf_op jit(solution)/shard_map/ppermute | solution.py:19
  56.8 8.1 %all_to_all.35 = bf16[4,32,768]{2,1,0:T(8,128)(2,1)S(1)} all-to-all(bf16[4,32,768]{2,1,0:T(8,128)(2,1)S(1)} %bitcast.80), channel_id=1, replica_groups=mesh['xl'=2,'zh'=8,'zl'=4,'c'=2,'y'=4,'xh'=2] {'zl'}, dimensions={0} | all-to-all | bytes 393216 | tf_op jit(solution)/shard_map/all_to_all | solution.py:23
  65.0 44.4 %all_to_all.36 = f32[8,4,768]{2,1,0:T(4,128)S(1)} all-to-all(f32[8,4,768]{2,1,0:T(4,128)S(1)} %reshape.39), channel_id=1, replica_groups=mesh['xl'=2,'zh'=8,'zl'=4,'c'=2,'y'=4,'xh'=2] {'zh'}, dimensions={0} | all-to-all | bytes 196608 | tf_op jit(solution)/shard_map/all_to_all | solution.py:23
  109.4 0.0 copy-done.2
  109.4 1.3 fusion.37
  110.7 26.7 %all_to_all.37 = bf16[8,4,768]{2,1,0:T(4,128)(2,1)S(1)} all-to-all(bf16[8,4,768]{2,1,0:T(4,128)(2,1)S(1)} %broadcast_in_dim.11), channel_id=1, replica_groups=mesh['xl'=2,'zh'=8,'zl'=4,'c'=2,'y'=4,'xh'=2] {'zh'}, dimensions={0} | all-to-all | bytes 98304 | tf_op jit(solution)/shard_map/all_to_all | solution.py:23
  137.4 9.4 %all_to_all.38 = bf16[4,32,768]{2,1,0:T(8,128)(2,1)S(1)} all-to-all(bf16[4,32,768]{2,1,0:T(8,128)(2,1)S(1)} %broadcast_in_dim.13), channel_id=1, replica_groups=mesh['xl'=2,'zh'=8,'zl'=4,'c'=2,'y'=4,'xh'=2] {'zl'}, dimensions={0} | all-to-all | bytes 393216 | tf_op jit(solution)/shard_map/all_to_all | solution.py:23
  146.8 2.2 %collective-permute-start.2 = (bf16[128,768]{1,0:T(8,128)(2,1)S(1)}, bf16[128,768]{1,0:T(8,128)(2,1)S(1)}, u32[]{:S(2)}, u32[]{:S(2)}) collective-permute-start(bf16[128,768]{1,0:T(8,128)(2,1)S(1)} %bitcast.79), channel_id=1, source_target_pairs={{0,512},{512,0},{1,513},{513,1},{2,514},{514,2},{3,515},{515,3},{4... | collective-permute-start | bytes 589832 | tf_op jit(solution)/shard_map/ppermute | solution.py:19
  149.0 4.2 %collective-permute-done.2 = bf16[128,768]{1,0:T(8,128)(2,1)S(1)} collective-permute-done((bf16[128,768]{1,0:T(8,128)(2,1)S(1)}, bf16[128,768]{1,0:T(8,128)(2,1)S(1)}, u32[]{:S(2)}, u32[]{:S(2)}) %collective-permute-start.2) | collective-permute-done | bytes 196640 | tf_op jit(solution)/shard_map/ppermute | solution.py:19
  153.3 8.2 %collective-permute-start.3 = (bf16[256,768]{1,0:T(8,128)(2,1)S(1)}, bf16[256,768]{1,0:T(8,128)(2,1)S(1)}, u32[]{:S(2)}, u32[]{:S(2)}) collective-permute-start(bf16[256,768]{1,0:T(8,128)(2,1)S(1)} %bitcast.75), channel_id=1, source_target_pairs={{0,8},{8,0},{1,9},{9,1},{2,10},{10,2},{3,11},{11,3},{4,12},{12,4},... | collective-permute-start | bytes 1179656 | tf_op jit(solution)/shard_map/ppermute | solution.py:19
  161.5 1.3 collective-permute-done.3
  162.9 0.1 select_bitcast_fusion.1
  162.9 0.1 pad_maximum_fusion
  163.0 0.0 copy-done.4
  163.0 0.0 copy-done.6
  163.0 0.0 copy-done.8
  163.1 0.0 copy-done.9
  163.1 0.0 copy-done.11
  163.1 0.0 copy-done.13
  163.1 1.3 convolution_subtract_fusion
  164.4 0.1 broadcast_in_dim.14
  164.5 16.5 %all_to_all.39 = f32[8,32,768]{2,1,0:T(8,128)S(1)} all-to-all(f32[8,32,768]{2,1,0:T(8,128)S(1)} %broadcast_in_dim.14), channel_id=1, replica_groups=mesh['xl'=2,'zh'=8,'zl'=4,'c'=2,'y'=4,'xh'=2] {'y','xh'}, dimensions={0} | all-to-all | bytes 1572864 | tf_op jit(solution)/shard_map/all_to_all | solution.py:23
  181.1 0.0 copy-start.1
  181.1 0.9 copy-done.1
  (22 shorter events, 0.4 us)
Async XLA Ops:
  0.6 31.1 %copy-start = (bf16[256,768]{1,0:T(8,128)(2,1)S(1)}, bf16[256,768]{1,0:T(8,128)(2,1)}, u32[]{:S(2)}) copy-start(bf16[256,768]{1,0:T(8,128)(2,1)} %param.8) | copy-start | bytes 1179652
  2.9 16.5 %all-to-all-start = ((f32[8,32,512]{2,1,0:T(8,128)}), f32[8,32,512]{2,1,0:T(8,128)S(1)}, u32[]{:S(2)}, u32[]{:S(2)}) async-start(f32[8,32,512]{2,1,0:T(8,128)} %bitcast.1), calls=%async_computation | async-start | bytes 1048576 | tf_op jit(solution)/shard_map/all_to_all | solution.py:23
  10.4 9.4 %copy-start.10 = (pred[512]{0:T(512)(128)(4,1)}, pred[512]{0:T(512)(128)(4,1)S(1)}, u32[]{:S(2)}) copy-start(pred[512]{0:T(512)(128)(4,1)S(1)} %get-tuple-element.10) | copy-start | bytes 1540
  10.4 9.4 %copy-start.12 = (pred[512]{0:T(512)(128)(4,1)}, pred[512]{0:T(512)(128)(4,1)S(1)}, u32[]{:S(2)}) copy-start(pred[512]{0:T(512)(128)(4,1)S(1)} %get-tuple-element.11) | copy-start | bytes 1540
  10.4 9.4 %copy-start.3 = (s32[512]{0:T(512)}, s32[512]{0:T(512)S(1)}, u32[]{:S(2)}) copy-start(s32[512]{0:T(512)S(1)} %get-tuple-element.13) | copy-start | bytes 6148
  10.5 9.4 %copy-start.5 = (s32[512]{0:T(512)}, s32[512]{0:T(512)S(1)}, u32[]{:S(2)}) copy-start(s32[512]{0:T(512)S(1)} %get-tuple-element.14) | copy-start | bytes 6148
  10.5 9.4 %copy-start.7 = (s32[512]{0:T(512)}, s32[512]{0:T(512)S(1)}, u32[]{:S(2)}) copy-start(s32[512]{0:T(512)S(1)} %get-tuple-element.15) | copy-start | bytes 6148
  20.6 11.0 %all-to-all-start.1 = ((bf16[8,32,512]{2,1,0:T(8,128)(2,1)}), bf16[8,32,512]{2,1,0:T(8,128)(2,1)S(1)}, u32[]{:S(2)}, u32[]{:S(2)}) async-start(bf16[8,32,512]{2,1,0:T(8,128)(2,1)} %broadcast_in_dim.10), calls=%async_computation.1 | async-start | bytes 524288 | tf_op jit(solution)/shard_map/all_to_all | solution.py:23
  31.7 77.6 %copy-start.2 = (f32[4,768]{1,0:T(4,128)S(1)}, f32[4,768]{1,0:T(4,128)}, u32[]{:S(2)}) copy-start(f32[4,768]{1,0:T(4,128)} %param.10) | copy-start | bytes 36868
  32.2 16.4 %collective-permute-start = (f32[256,768]{1,0:T(8,128)S(1)}, f32[256,768]{1,0:T(8,128)S(1)}, u32[]{:S(2)}, u32[]{:S(2)}) collective-permute-start(f32[256,768]{1,0:T(8,128)S(1)} %dynamic-slice_bitcast_fusion), channel_id=1, source_target_pairs={{0,8},{8,0},{1,9},{9,1},{2,10},{10,2},{3,11},{11,3},{4,12},{12,4},... | collective-permute-start | bytes 2359304 | tf_op jit(solution)/shard_map/ppermute | solution.py:19
  48.7 114.4 %copy-start.4 = (s32[512]{0:T(512)S(1)}, s32[512]{0:T(512)}, u32[]{:S(2)}) copy-start(s32[512]{0:T(512)} %copy-done.3) | copy-start | bytes 6148
  48.7 114.4 %copy-start.6 = (s32[512]{0:T(512)S(1)}, s32[512]{0:T(512)}, u32[]{:S(2)}) copy-start(s32[512]{0:T(512)} %copy-done.5) | copy-start | bytes 6148
  48.7 114.4 %copy-start.8 = (s32[512]{0:T(512)S(1)}, s32[512]{0:T(512)}, u32[]{:S(2)}) copy-start(s32[512]{0:T(512)} %copy-done.7) | copy-start | bytes 6148
  48.7 114.4 %copy-start.9 = (f32[32,768]{1,0:T(8,128)S(1)}, f32[32,768]{1,0:T(8,128)}, u32[]{:S(2)}) copy-start(f32[32,768]{1,0:T(8,128)} %param.9) | copy-start | bytes 294916
  48.7 114.4 %copy-start.11 = (pred[512]{0:T(512)(128)(4,1)S(1)}, pred[512]{0:T(512)(128)(4,1)}, u32[]{:S(2)}) copy-start(pred[512]{0:T(512)(128)(4,1)} %copy-done.10) | copy-start | bytes 1540
  48.7 114.4 %copy-start.13 = (pred[512]{0:T(512)(128)(4,1)S(1)}, pred[512]{0:T(512)(128)(4,1)}, u32[]{:S(2)}) copy-start(pred[512]{0:T(512)(128)(4,1)} %copy-done.12) | copy-start | bytes 1540
  48.8 8.0 %collective-permute-start.1 = (bf16[128,768]{1,0:T(8,128)(2,1)S(1)}, bf16[128,768]{1,0:T(8,128)(2,1)S(1)}, u32[]{:S(2)}, u32[]{:S(2)}) collective-permute-start(bf16[128,768]{1,0:T(8,128)(2,1)S(1)} %fusion.24), channel_id=1, source_target_pairs={{0,512},{512,0},{1,513},{513,1},{2,514},{514,2},{3,515},{515,3},{4... | collective-permute-start | bytes 589832 | tf_op jit(solution)/shard_map/ppermute | solution.py:19
  146.8 6.4 %collective-permute-start.2 = (bf16[128,768]{1,0:T(8,128)(2,1)S(1)}, bf16[128,768]{1,0:T(8,128)(2,1)S(1)}, u32[]{:S(2)}, u32[]{:S(2)}) collective-permute-start(bf16[128,768]{1,0:T(8,128)(2,1)S(1)} %bitcast.79), channel_id=1, source_target_pairs={{0,512},{512,0},{1,513},{513,1},{2,514},{514,2},{3,515},{515,3},{4... | collective-permute-start | bytes 589832 | tf_op jit(solution)/shard_map/ppermute | solution.py:19
  153.3 9.5 %collective-permute-start.3 = (bf16[256,768]{1,0:T(8,128)(2,1)S(1)}, bf16[256,768]{1,0:T(8,128)(2,1)S(1)}, u32[]{:S(2)}, u32[]{:S(2)}) collective-permute-start(bf16[256,768]{1,0:T(8,128)(2,1)S(1)} %bitcast.75), channel_id=1, source_target_pairs={{0,8},{8,0},{1,9},{9,1},{2,10},{10,2},{3,11},{11,3},{4,12},{12,4},... | collective-permute-start | bytes 1179656 | tf_op jit(solution)/shard_map/ppermute | solution.py:19
  181.1 0.9 copy-start.1

commit v2 on v1

--- a/solution.py
+++ b/solution.py
@@ -25,21 +25,6 @@
 
 def spread(x, axis, n):
     return exchange(jnp.broadcast_to(x[None], (n,) + x.shape), axis)
-
-
-def pair_sum(x, axis, kind):
-    me = lax.axis_index(axis)
-    mine = lax.dynamic_index_in_dim(x, me, 0, keepdims=False)
-    other = lax.dynamic_index_in_dim(x, 1 - me, 0, keepdims=False)
-    return mine + swap(other.astype(kind), axis).astype(f32)
-
-
-def pair_gather(x, axis):
-    me = lax.axis_index(axis)
-    other = swap(x, axis)
-    first = jnp.where(me == 0, x, other)
-    second = jnp.where(me == 0, other, x)
-    return jnp.stack([first, second])
 
 
 def rank_order(sizes, total):
@@ -70,22 +55,38 @@
         height = master_weight.shape[0]
         order = rank_order(sizes, ranks)
 
-        part_basis = lax.dynamic_slice_in_dim(proj_basis, lax.axis_index(FS) * feats, feats, 0)
-        part = jnp.dot(activations, part_basis, preferred_element_type=f32)
-        part = exchange(part.reshape(nf, tokens // nf, ranks), FS)
-        own = jnp.sum(part, axis=0).astype(bf16)
+        acts = exchange(activations.reshape(nf, tokens // nf, feats), FS)
+        own = lax.dot_general(
+            acts,
+            proj_basis.reshape(nf, feats, ranks),
+            (((0, 2), (0, 1)), ((), ())),
+            preferred_element_type=f32,
+        ).astype(bf16)
         own = jnp.dot(own, order, preferred_element_type=f32).astype(bf16)
-        coords = spread(own, FS, nf).reshape(tokens, ranks)
+        own = own.reshape(tokens // nf, c * xl, ranks // (c * xl)).swapaxes(0, 1)
+        own = jnp.broadcast_to(own[:, None], (c * xl, nf) + own.shape[1:])
+        own = own.reshape((c * xl * nf,) + own.shape[2:])
+        coords = exchange(own, ("c", "xl", "y", "xh"))
+        coords = coords.reshape(c * xl, tokens, ranks // (c * xl))
 
-        grad = lax.dot_general(
-            coords, out_grad, (((0,), (0,)), ((), ())), preferred_element_type=f32
+        me = lax.axis_index("c") * xl + lax.axis_index("xl")
+        og_x = swap(out_grad, "xl")
+        og_c = swap(out_grad, "c")
+        og_xc = swap(og_x, "c")
+        blocks = ((me, out_grad), (me ^ 2, og_c), (me ^ 1, og_x), (me ^ 3, og_xc))
+        grad = sum(
+            lax.dot_general(
+                lax.dynamic_index_in_dim(coords, i, 0, keepdims=False),
+                og,
+                (((0,), (0,)), ((), ())),
+                preferred_element_type=f32,
+            )
+            for i, og in blocks
         )
-        grad = pair_sum(grad.reshape(c, ranks // c, width), "c", f32)
-        grad = pair_sum(grad.reshape(xl, ranks // c // xl, width), "xl", bf16)
         grad = exchange(grad.reshape(zl, zh * depth, width).astype(bf16), "zl")
         grad = jnp.sum(grad.astype(f32), axis=0)
-        grad = exchange(grad.reshape(zh, depth, width), "zh")
-        grad = jnp.sum(grad, axis=0)
+        grad = exchange(grad.reshape(zh, depth, width).astype(bf16), "zh")
+        grad = jnp.sum(grad.astype(f32), axis=0)
 
         new_first = beta_one * first_moment + (1.0 - beta_one) * grad
         new_second = beta_two * second_moment + (1.0 - beta_two) * grad * grad
@@ -96,13 +97,23 @@
         ).astype(bf16)
 
         full = spread(update, "zh", zh).reshape(zh * depth, width)
-        full = spread(full, "zl", zl).reshape(zl * zh * depth, width)
-        full = pair_gather(full, "xl").reshape(ranks // c, width)
-        full = pair_gather(full, "c").reshape(ranks, width)
+        full = spread(full, ("xl", "zl"), xl * zl).reshape(ranks // c, width)
+        other = swap(full, "c")
 
         basis_rows = lax.dynamic_slice_in_dim(proj_basis, lax.axis_index(DP) * height, height, 0)
         basis_rows = jnp.dot(basis_rows, order, preferred_element_type=f32).astype(bf16)
-        delta = jnp.dot(basis_rows, full, preferred_element_type=f32)
+        basis_rows = basis_rows.reshape(height, c, ranks // c).swapaxes(0, 1)
+        core = lax.axis_index("c")
+        delta = jnp.dot(
+            lax.dynamic_index_in_dim(basis_rows, core, 0, keepdims=False),
+            full,
+            preferred_element_type=f32,
+        )
+        delta = delta + jnp.dot(
+            lax.dynamic_index_in_dim(basis_rows, 1 - core, 0, keepdims=False),
+            other,
+            preferred_element_type=f32,
+        )
         fresh = master_weight - step_size * delta
         new_weight = spread(fresh, FS, nf)
         new_weight = jnp.concatenate([new_weight[i] for i in range(nf)], axis=1)

time: 183 us -> 161 us (0.88)
  blocking collectives: 105 us -> 91.5 us
  waiting for transfers between devices: 30 us -> 18.4 us
  starting transfers between devices: 37.7 us -> 40 us
    all_to_all x2 -> x3, starting transfers between devices: 10.9 us -> 25.7 us  [exchange(): return lax.all_to_all(x, axis, 0, 0, tiled=False)]
    all_to_all x5 -> x4, blocking collectives: 105 us -> 91.5 us  [exchange(): return lax.all_to_all(x, axis, 0, 0, tiled=False)]
    ppermute x4, waiting for transfers between devices: 13.5 us -> 0.01 us  [swap(): return lax.ppermute(x, axis, [(0, 1), (1, 0)])]
    ppermute x4, starting transfers between devices: 26.8 us -> 14.2 us  [swap(): return lax.ppermute(x, axis, [(0, 1), (1, 0)])]
    dot_general x1, matrix products: 0.34 us -> 3.28 us  [body(): own = jnp.dot(own, order, preferred_element_type=f32).astype(bf16)]
    all_to_all x2 -> x3, waiting for transfers between devices: 16.5 us -> 18.4 us  [exchange(): return lax.all_to_all(x, axis, 0, 0, tiled=False)]
    dot_general x3 -> x7, matrix products: 3.95 us -> 2.44 us  [the longest x1 1.1 us: body(): jnp.dot(basis_rows, order, preferred_element_type=f32).astype(bf16)]
  transfers between devices with their start and end apart: 6 -> 7, of which waited for: 6 -> 3; matrix products, arithmetic and copies ran while one was open for 0% -> 4% of each run, Pallas kernels for 0% -> 0%
where the time goes in v2:
time: 161 us; the launch traced here: 160 us
  blocking collectives  91.5 us (57%)
  starting transfers between devices  40 us (25%)
  waiting for transfers between devices  18.4 us (11%)
  matrix products  5.73 us (4%)
  local copies, waits for them, and re-layouts  2.72 us (2%)
    all_to_all x4, blocking collectives, exchange(): return lax.all_to_all(x, axis, 0, 0, tiled=False)  91.5 us
    all_to_all x3, starting transfers between devices, exchange(): return lax.all_to_all(x, axis, 0, 0, tiled=False)  25.7 us
    all_to_all x3, waiting for transfers between devices, exchange(): return lax.all_to_all(x, axis, 0, 0, tiled=False)  18.4 us
    ppermute x4, starting transfers between devices, swap(): return lax.ppermute(x, axis, [(0, 1), (1, 0)])  14.2 us
    dot_general x1, matrix products, body(): own = jnp.dot(own, order, preferred_element_type=f32).astype(bf16)  3.28 us
  transfers between devices with their start and end apart: 7, of which 3 were waited for; matrix products, arithmetic and copies ran while one was open for 4% of the time, Pallas kernels for 0%

profile of v2, /device:TPU:1, one launch (start us, length us, event | category | flops | bytes accessed | tf_op | source)
XLA Modules:
  0.0 159.9 jit_solution(2710098407747957293)
XLA Ops:
  0.6 7.5 %all-to-all-start = ((bf16[8,32,512]{2,1,0:T(8,128)(2,1)}), bf16[8,32,512]{2,1,0:T(8,128)(2,1)S(1)}, u32[]{:S(2)}, u32[]{:S(2)}) async-start(bf16[8,32,512]{2,1,0:T(8,128)(2,1)} %bitcast.78), calls=%async_computation | async-start | bytes 524288 | tf_op jit(solution)/shard_map/all_to_all | solution.py:23
  8.1 2.2 %collective-permute-start.1 = (bf16[256,768]{1,0:T(8,128)(2,1)}, bf16[256,768]{1,0:T(8,128)(2,1)S(1)}, u32[]{:S(2)}, u32[]{:S(2)}) collective-permute-start(bf16[256,768]{1,0:T(8,128)(2,1)} %param.8), channel_id=1, source_target_pairs={{0,512},{512,0},{1,513},{513,1},{2,514},{514,2},{3,515},{515,3},{4... | collective-permute-start | bytes 1179656 | tf_op jit(solution)/shard_map/ppermute | solution.py:19
  10.4 5.4 %all-to-all-done = bf16[8,32,512]{2,1,0:T(8,128)(2,1)S(1)} async-done(((bf16[8,32,512]{2,1,0:T(8,128)(2,1)}), bf16[8,32,512]{2,1,0:T(8,128)(2,1)S(1)}, u32[]{:S(2)}, u32[]{:S(2)}) %all-to-all-start) | async-done | bytes 262176 | tf_op jit(solution)/shard_map/all_to_all | solution.py:23
  15.8 0.0 copy-start
  15.8 3.3 %convolution_convert_fusion = bf16[32,512]{1,0:T(8,128)(2,1)S(1)} fusion(bf16[8,32,512]{2,1,0:T(8,128)(2,1)S(1)} %all-to-all-done, bf16[8,512,512]{2,1,0:T(8,128)(2,1)} %bitcast.80, s32[512]{0:T(512)S(1)} %get-tuple-element.11, s32[512]{0:T(512)S(1)} %get-tuple-element.12, s32[512]{0:T(512)S(1)} %get-tuple-element.10, s32[512]{0:T(512)S(1)} %get-tuple-element.13, ...), kind=kOutput, calls=%fused_computation.25 | convolution fusion | flops 168853504 | bytes 4498432 | tf_op jit(solution)/shard_map/dot_general | solution.py:65
  19.0 0.0 copy-start.3
  19.1 0.0 copy-start.4
  19.1 0.7 broadcast_in_dim.10
  19.8 14.8 %all-to-all-start.1 = ((bf16[32,32,128]{2,1,0:T(8,128)(2,1)}), bf16[32,32,128]{2,1,0:T(8,128)(2,1)S(1)}, u32[]{:S(2)}, u32[]{:S(2)}) async-start(bf16[32,32,128]{2,1,0:T(8,128)(2,1)} %bitcast.5), calls=%async_computation.1 | async-start | bytes 524288 | tf_op jit(solution)/shard_map/all_to_all | solution.py:23
  34.7 0.0 copy-done
  34.7 2.2 %collective-permute-start = (bf16[256,768]{1,0:T(8,128)(2,1)S(1)}, bf16[256,768]{1,0:T(8,128)(2,1)S(1)}, u32[]{:S(2)}, u32[]{:S(2)}) collective-permute-start(bf16[256,768]{1,0:T(8,128)(2,1)S(1)} %copy-done), channel_id=1, source_target_pairs={{0,8},{8,0},{1,9},{9,1},{2,10},{10,2},{3,11},{11,3},{4,12},{12,4},... | collective-permute-start | bytes 1179656 | tf_op jit(solution)/shard_map/ppermute | solution.py:19
  36.9 0.0 collective-permute-done.1
  36.9 2.2 %collective-permute-start.2 = (bf16[256,768]{1,0:T(8,128)(2,1)S(1)}, bf16[256,768]{1,0:T(8,128)(2,1)S(1)}, u32[]{:S(2)}, u32[]{:S(2)}) collective-permute-start(bf16[256,768]{1,0:T(8,128)(2,1)S(1)} %collective-permute-done.1), channel_id=1, source_target_pairs={{0,8},{8,0},{1,9},{9,1},{2,10},{10,2},{3,11},{11,3},{4,12},{12,4},... | collective-permute-start | bytes 1179656 | tf_op jit(solution)/shard_map/ppermute | solution.py:19
  39.0 4.3 %all-to-all-done.1 = bf16[32,32,128]{2,1,0:T(8,128)(2,1)S(1)} async-done(((bf16[32,32,128]{2,1,0:T(8,128)(2,1)}), bf16[32,32,128]{2,1,0:T(8,128)(2,1)S(1)}, u32[]{:S(2)}, u32[]{:S(2)}) %all-to-all-start.1) | async-done | bytes 262176 | tf_op jit(solution)/shard_map/all_to_all | solution.py:23
  43.4 0.2 fusion.33
  43.6 0.0 collective-permute-done
  43.6 0.2 convolution_add_fusion.2
  43.9 0.2 convolution_add_fusion.1
  44.1 0.0 collective-permute-done.2
  44.1 0.2 fusion
  44.4 9.4 %all_to_all.35 = bf16[4,32,768]{2,1,0:T(8,128)(2,1)S(1)} all-to-all(bf16[4,32,768]{2,1,0:T(8,128)(2,1)S(1)} %bitcast.77), channel_id=1, replica_groups=mesh['xl'=2,'zh'=8,'zl'=4,'c'=2,'y'=4,'xh'=2] {'zl'}, dimensions={0} | all-to-all | bytes 393216 | tf_op jit(solution)/shard_map/all_to_all | solution.py:23
  53.8 40.2 %all_to_all.36 = bf16[8,4,768]{2,1,0:T(4,128)(2,1)S(1)} all-to-all(bf16[8,4,768]{2,1,0:T(4,128)(2,1)S(1)} %convert_element_type.32), channel_id=1, replica_groups=mesh['xl'=2,'zh'=8,'zl'=4,'c'=2,'y'=4,'xh'=2] {'zh'}, dimensions={0} | all-to-all | bytes 98304 | tf_op jit(solution)/shard_map/all_to_all | solution.py:23
  94.1 0.0 copy-done.3
  94.1 0.0 copy-done.4
  94.1 0.6 fusion.42
  94.8 24.4 %all_to_all.37 = bf16[8,4,768]{2,1,0:T(4,128)(2,1)S(1)} all-to-all(bf16[8,4,768]{2,1,0:T(4,128)(2,1)S(1)} %broadcast_in_dim.11), channel_id=1, replica_groups=mesh['xl'=2,'zh'=8,'zl'=4,'c'=2,'y'=4,'xh'=2] {'zh'}, dimensions={0} | all-to-all | bytes 98304 | tf_op jit(solution)/shard_map/all_to_all | solution.py:23
  119.2 0.8 broadcast_in_dim.13
  120.0 3.5 %all-to-all-start.5 = ((bf16[8,32,768]{2,1,0:T(8,128)(2,1)}), bf16[8,32,768]{2,1,0:T(8,128)(2,1)S(1)}, u32[]{:S(2)}, u32[]{:S(2)}) async-start(bf16[8,32,768]{2,1,0:T(8,128)(2,1)} %broadcast_in_dim.13), calls=%async_computation.5 | async-start | bytes 786432 | tf_op jit(solution)/shard_map/all_to_all | solution.py:23
  123.5 8.7 %all-to-all-done.5 = bf16[8,32,768]{2,1,0:T(8,128)(2,1)S(1)} async-done(((bf16[8,32,768]{2,1,0:T(8,128)(2,1)}), bf16[8,32,768]{2,1,0:T(8,128)(2,1)S(1)}, u32[]{:S(2)}, u32[]{:S(2)}) %all-to-all-start.5) | async-done | bytes 393248 | tf_op jit(solution)/shard_map/all_to_all | solution.py:23
  132.1 0.0 copy-start.1
  132.1 7.7 %collective-permute-start.3 = (bf16[256,768]{1,0:T(8,128)(2,1)S(1)}, bf16[256,768]{1,0:T(8,128)(2,1)S(1)}, u32[]{:S(2)}, u32[]{:S(2)}) collective-permute-start(bf16[256,768]{1,0:T(8,128)(2,1)S(1)} %bitcast.71), channel_id=1, source_target_pairs={{0,8},{8,0},{1,9},{9,1},{2,10},{10,2},{3,11},{11,3},{4,12},{12,4},... | collective-permute-start | bytes 1179656 | tf_op jit(solution)/shard_map/ppermute | solution.py:19
  139.8 1.1 convolution_convert_fusion.1
  141.0 0.1 constant_dynamic-slice_fusion
  141.0 0.2 fusion.40
  141.2 0.0 collective-permute-done.3
  141.2 0.0 copy-done.1
  141.2 0.2 fusion.1
  141.4 0.1 broadcast_in_dim.14
  141.5 17.4 %all_to_all.38 = f32[8,32,768]{2,1,0:T(8,128)S(1)} all-to-all(f32[8,32,768]{2,1,0:T(8,128)S(1)} %broadcast_in_dim.14), channel_id=1, replica_groups=mesh['xl'=2,'zh'=8,'zl'=4,'c'=2,'y'=4,'xh'=2] {'y','xh'}, dimensions={0} | all-to-all | bytes 1572864 | tf_op jit(solution)/shard_map/all_to_all | solution.py:23
  159.1 0.0 copy-start.2
  159.1 0.9 copy-done.2
  (19 shorter events, 0.3 us)
Async XLA Ops:
  0.6 15.1 %all-to-all-start = ((bf16[8,32,512]{2,1,0:T(8,128)(2,1)}), bf16[8,32,512]{2,1,0:T(8,128)(2,1)S(1)}, u32[]{:S(2)}, u32[]{:S(2)}) async-start(bf16[8,32,512]{2,1,0:T(8,128)(2,1)} %bitcast.78), calls=%async_computation | async-start | bytes 524288 | tf_op jit(solution)/shard_map/all_to_all | solution.py:23
  8.1 28.7 %collective-permute-start.1 = (bf16[256,768]{1,0:T(8,128)(2,1)}, bf16[256,768]{1,0:T(8,128)(2,1)S(1)}, u32[]{:S(2)}, u32[]{:S(2)}) collective-permute-start(bf16[256,768]{1,0:T(8,128)(2,1)} %param.8), channel_id=1, source_target_pairs={{0,512},{512,0},{1,513},{513,1},{2,514},{514,2},{3,515},{515,3},{4... | collective-permute-start | bytes 1179656 | tf_op jit(solution)/shard_map/ppermute | solution.py:19
  15.8 18.9 %copy-start = (bf16[256,768]{1,0:T(8,128)(2,1)S(1)}, bf16[256,768]{1,0:T(8,128)(2,1)}, u32[]{:S(2)}) copy-start(bf16[256,768]{1,0:T(8,128)(2,1)} %param.8) | copy-start | bytes 1179652
  19.0 75.1 %copy-start.3 = (f32[4,768]{1,0:T(4,128)S(1)}, f32[4,768]{1,0:T(4,128)}, u32[]{:S(2)}) copy-start(f32[4,768]{1,0:T(4,128)} %param.10) | copy-start | bytes 36868
  19.1 75.1 %copy-start.4 = (f32[4,768]{1,0:T(4,128)S(1)}, f32[4,768]{1,0:T(4,128)}, u32[]{:S(2)}) copy-start(f32[4,768]{1,0:T(4,128)} %param.11) | copy-start | bytes 36868
  19.8 23.5 %all-to-all-start.1 = ((bf16[32,32,128]{2,1,0:T(8,128)(2,1)}), bf16[32,32,128]{2,1,0:T(8,128)(2,1)S(1)}, u32[]{:S(2)}, u32[]{:S(2)}) async-start(bf16[32,32,128]{2,1,0:T(8,128)(2,1)} %bitcast.5), calls=%async_computation.1 | async-start | bytes 524288 | tf_op jit(solution)/shard_map/all_to_all | solution.py:23
  34.7 9.0 %collective-permute-start = (bf16[256,768]{1,0:T(8,128)(2,1)S(1)}, bf16[256,768]{1,0:T(8,128)(2,1)S(1)}, u32[]{:S(2)}, u32[]{:S(2)}) collective-permute-start(bf16[256,768]{1,0:T(8,128)(2,1)S(1)} %copy-done), channel_id=1, source_target_pairs={{0,8},{8,0},{1,9},{9,1},{2,10},{10,2},{3,11},{11,3},{4,12},{12,4},... | collective-permute-start | bytes 1179656 | tf_op jit(solution)/shard_map/ppermute | solution.py:19
  36.9 7.3 %collective-permute-start.2 = (bf16[256,768]{1,0:T(8,128)(2,1)S(1)}, bf16[256,768]{1,0:T(8,128)(2,1)S(1)}, u32[]{:S(2)}, u32[]{:S(2)}) collective-permute-start(bf16[256,768]{1,0:T(8,128)(2,1)S(1)} %collective-permute-done.1), channel_id=1, source_target_pairs={{0,8},{8,0},{1,9},{9,1},{2,10},{10,2},{3,11},{11,3},{4,12},{12,4},... | collective-permute-start | bytes 1179656 | tf_op jit(solution)/shard_map/ppermute | solution.py:19
  120.0 12.1 %all-to-all-start.5 = ((bf16[8,32,768]{2,1,0:T(8,128)(2,1)}), bf16[8,32,768]{2,1,0:T(8,128)(2,1)S(1)}, u32[]{:S(2)}, u32[]{:S(2)}) async-start(bf16[8,32,768]{2,1,0:T(8,128)(2,1)} %broadcast_in_dim.13), calls=%async_computation.5 | async-start | bytes 786432 | tf_op jit(solution)/shard_map/all_to_all | solution.py:23
  132.1 9.1 %copy-start.1 = (f32[32,768]{1,0:T(8,128)S(1)}, f32[32,768]{1,0:T(8,128)}, u32[]{:S(2)}) copy-start(f32[32,768]{1,0:T(8,128)} %param.9) | copy-start | bytes 294916
  132.1 9.1 %collective-permute-start.3 = (bf16[256,768]{1,0:T(8,128)(2,1)S(1)}, bf16[256,768]{1,0:T(8,128)(2,1)S(1)}, u32[]{:S(2)}, u32[]{:S(2)}) collective-permute-start(bf16[256,768]{1,0:T(8,128)(2,1)S(1)} %bitcast.71), channel_id=1, source_target_pairs={{0,8},{8,0},{1,9},{9,1},{2,10},{10,2},{3,11},{11,3},{4,12},{12,4},... | collective-permute-start | bytes 1179656 | tf_op jit(solution)/shard_map/ppermute | solution.py:19
  159.1 0.9 copy-start.2

commit v3 on v2

--- a/solution.py
+++ b/solution.py
@@ -25,6 +25,12 @@
 
 def spread(x, axis, n):
     return exchange(jnp.broadcast_to(x[None], (n,) + x.shape), axis)
+
+
+def double(x, axis, gap, pieces=1):
+    pairs = [(i, i ^ gap) for i in range(lax.axis_size(axis))]
+    got = [lax.ppermute(part, axis, pairs) for part in jnp.split(x, pieces)]
+    return jnp.concatenate([x] + got)
 
 
 def rank_order(sizes, total):
@@ -55,14 +61,15 @@
         height = master_weight.shape[0]
         order = rank_order(sizes, ranks)
 
+        basis = jnp.dot(proj_basis, order, preferred_element_type=f32).astype(bf16)
+
         acts = exchange(activations.reshape(nf, tokens // nf, feats), FS)
         own = lax.dot_general(
             acts,
-            proj_basis.reshape(nf, feats, ranks),
+            basis.reshape(nf, feats, ranks),
             (((0, 2), (0, 1)), ((), ())),
             preferred_element_type=f32,
         ).astype(bf16)
-        own = jnp.dot(own, order, preferred_element_type=f32).astype(bf16)
         own = own.reshape(tokens // nf, c * xl, ranks // (c * xl)).swapaxes(0, 1)
         own = jnp.broadcast_to(own[:, None], (c * xl, nf) + own.shape[1:])
         own = own.reshape((c * xl * nf,) + own.shape[2:])
@@ -83,9 +90,15 @@
             )
             for i, og in blocks
         )
-        grad = exchange(grad.reshape(zl, zh * depth, width).astype(bf16), "zl")
-        grad = jnp.sum(grad.astype(f32), axis=0)
-        grad = exchange(grad.reshape(zh, depth, width).astype(bf16), "zh")
+        grad, weights = lax.optimization_barrier((grad.astype(bf16), master_weight[None]))
+        grad = exchange(grad.reshape(zl, zh * depth, width), "zl")
+        weights = double(weights, "y", 1)
+        grad, weights = lax.optimization_barrier((grad, weights))
+        grad = jnp.sum(grad.astype(f32), axis=0).astype(bf16)
+        grad, weights = lax.optimization_barrier((grad, weights))
+        grad = exchange(grad.reshape(zh, depth, width), "zh")
+        weights = double(weights, "xh", 1)
+        grad, weights = lax.optimization_barrier((grad, weights))
         grad = jnp.sum(grad.astype(f32), axis=0)
 
         new_first = beta_one * first_moment + (1.0 - beta_one) * grad
@@ -96,12 +109,16 @@
             new_first / correct_one / (jnp.sqrt(new_second / correct_two) + eps_value)
         ).astype(bf16)
 
-        full = spread(update, "zh", zh).reshape(zh * depth, width)
-        full = spread(full, ("xl", "zl"), xl * zl).reshape(ranks // c, width)
+        full = jnp.broadcast_to(update[None], (zh,) + update.shape)
+        full, weights = lax.optimization_barrier((full, weights))
+        full = exchange(full, "zh")
+        weights = double(weights, "y", 2, 2)
+        full, weights = lax.optimization_barrier((full, weights))
+        full = spread(full.reshape(zh * depth, width), ("xl", "zl"), xl * zl)
+        full = full.reshape(ranks // c, width)
         other = swap(full, "c")
 
-        basis_rows = lax.dynamic_slice_in_dim(proj_basis, lax.axis_index(DP) * height, height, 0)
-        basis_rows = jnp.dot(basis_rows, order, preferred_element_type=f32).astype(bf16)
+        basis_rows = lax.dynamic_slice_in_dim(basis, lax.axis_index(DP) * height, height, 0)
         basis_rows = basis_rows.reshape(height, c, ranks // c).swapaxes(0, 1)
         core = lax.axis_index("c")
         delta = jnp.dot(
@@ -114,9 +131,21 @@
             other,
             preferred_element_type=f32,
         )
-        fresh = master_weight - step_size * delta
-        new_weight = spread(fresh, FS, nf)
-        new_weight = jnp.concatenate([new_weight[i] for i in range(nf)], axis=1)
+        deltas = spread(delta.astype(bf16), FS, nf)
+        place = lax.axis_index(FS)
+
+        def block(other):
+            m = place ^ other
+            return (m & 4) | ((m & 1) << 1) | ((m >> 1) & 1)
+
+        new_weight = jnp.concatenate(
+            [
+                lax.dynamic_index_in_dim(weights, block(i), 0, keepdims=False)
+                - step_size * deltas[i].astype(f32)
+                for i in range(nf)
+            ],
+            axis=1,
+        )
         return (new_weight, new_first, new_second)
 
     return body

time: 161 us -> 176 us (1.093)
  blocking collectives: 91.5 us -> 11.9 us
  starting transfers between devices: 40 us -> 83.7 us
  waiting for transfers between devices: 18.4 us -> 54.9 us
  local copies, waits for them, and re-layouts: 2.72 us -> 11.3 us
  matrix products: 5.73 us -> 11.4 us
    all_to_all x4 -> x1, blocking collectives: 91.5 us -> 11.9 us  [exchange(): return lax.all_to_all(x, axis, 0, 0, tiled=False)]
    all_to_all x3 -> x6, starting transfers between devices: 25.7 us -> 58.5 us  [exchange(): return lax.all_to_all(x, axis, 0, 0, tiled=False)]
    all_to_all x3 -> x6, waiting for transfers between devices: 18.4 us -> 39.9 us  [exchange(): return lax.all_to_all(x, axis, 0, 0, tiled=False)]
    ppermute x0 -> x4, waiting for transfers between devices: none -> 15 us  [double(): got = [lax.ppermute(part, axis, pairs) for part in jnp.split(x, pieces)]]
    ppermute x0 -> x4, starting transfers between devices: none -> 11.1 us  [double(): got = [lax.ppermute(part, axis, pairs) for part in jnp.split(x, pieces)]]
    reshape x1 -> x2, local copies, waits for them, and re-layouts: 0.02 us -> 7.14 us  [the longest x1 6.51 us: body(): basis.reshape(nf, feats, ranks)]
    dot_general x2, matrix products: 4.38 us -> 9.3 us  [the longest x1 6.25 us: body(): basis = jnp.dot(proj_basis, order, preferred_element_type=f32).astype(bf16)]
  transfers between devices with their start and end apart: 7 -> 14, of which waited for: 3 -> 10; matrix products, arithmetic and copies ran while one was open for 4% -> 11% of each run, Pallas kernels for 0% -> 0%
where the time goes in v3:
time: 176 us; the launch traced here: 175 us
  starting transfers between devices  83.7 us (48%)
  waiting for transfers between devices  54.9 us (31%)
  blocking collectives  11.9 us (7%)
  matrix products  11.4 us (6%)
  local copies, waits for them, and re-layouts  11.3 us (6%)
    all_to_all x6, starting transfers between devices, exchange(): return lax.all_to_all(x, axis, 0, 0, tiled=False)  58.5 us
    all_to_all x6, waiting for transfers between devices, exchange(): return lax.all_to_all(x, axis, 0, 0, tiled=False)  39.9 us
    ppermute x4, waiting for transfers between devices, double(): got = [lax.ppermute(part, axis, pairs) for part in jnp.split(x, pieces)]  15 us
    ppermute x4, starting transfers between devices, swap(): return lax.ppermute(x, axis, [(0, 1), (1, 0)])  14.1 us
    all_to_all x1, blocking collectives, exchange(): return lax.all_to_all(x, axis, 0, 0, tiled=False)  11.9 us
    ppermute x4, starting transfers between devices, double(): got = [lax.ppermute(part, axis, pairs) for part in jnp.split(x, pieces)]  11.1 us
    reshape x1, local copies, waits for them, and re-layouts, body(): basis.reshape(nf, feats, ranks)  6.51 us
    dot_general x1, matrix products, body(): basis = jnp.dot(proj_basis, order, preferred_element_type=f32).astype(bf16)  6.25 us
  transfers between devices with their start and end apart: 14, of which 10 were waited for; matrix products, arithmetic and copies ran while one was open for 11% of the time, Pallas kernels for 0%

profile of v3, /device:TPU:1, one launch (start us, length us, event | category | flops | bytes accessed | tf_op | source)
XLA Modules:
  0.0 175.1 jit_solution(12114498960843942580)
XLA Ops:
  0.6 7.5 %all-to-all-start = ((bf16[8,32,512]{2,1,0:T(8,128)(2,1)}), bf16[8,32,512]{2,1,0:T(8,128)(2,1)S(1)}, u32[]{:S(2)}, u32[]{:S(2)}) async-start(bf16[8,32,512]{2,1,0:T(8,128)(2,1)} %bitcast.73), calls=%async_computation | async-start | bytes 524288 | tf_op jit(solution)/shard_map/all_to_all | solution.py:23
  8.1 2.2 %collective-permute-start.1 = (bf16[256,768]{1,0:T(8,128)(2,1)}, bf16[256,768]{1,0:T(8,128)(2,1)S(1)}, u32[]{:S(2)}, u32[]{:S(2)}) collective-permute-start(bf16[256,768]{1,0:T(8,128)(2,1)} %param.8), channel_id=1, source_target_pairs={{0,512},{512,0},{1,513},{513,1},{2,514},{514,2},{3,515},{515,3},{4... | collective-permute-start | bytes 1179656 | tf_op jit(solution)/shard_map/ppermute | solution.py:19
  10.4 6.3 %convolution_convert_fusion = bf16[512,4096]{1,0:T(8,128)(2,1)} fusion(bf16[4096,512]{1,0:T(8,128)(2,1)} %param.7, s32[512]{0:T(512)S(1)} %get-tuple-element.35, s32[512]{0:T(512)S(1)} %get-tuple-element.36, s32[512]{0:T(512)S(1)} %get-tuple-element.34, s32[512]{0:T(512)S(1)} %get-tuple-element.37, pred[512]{0:T(512)(128)(4,1)S(1)} %get-tuple-element.33, ...), kind=kOutput, calls=%fused_computation | convolution fusion | flops 2167668736 | bytes 8397824 | tf_op jit(solution)/shard_map/dot_general | solution.py:64
  16.6 6.5 %copy.16 = bf16[4096,512]{1,0:T(8,128)(2,1)} copy(bf16[4096,512]{0,1:T(8,128)(2,1)} %bitcast.64) | data formatting | bytes 8388608 | tf_op jit(solution)/shard_map/reshape | solution.py:69
  23.1 0.0 copy-start
  23.1 0.0 all-to-all-done
  23.1 0.0 copy-start.1
  23.1 3.0 %fusion.3 = bf16[32,512]{1,0:T(8,128)(2,1)S(1)} fusion(bf16[8,32,512]{2,1,0:T(8,128)(2,1)S(1)} %all-to-all-done, bf16[8,512,512]{2,1,0:T(8,128)(2,1)} %bitcast.63), kind=kOutput, calls=%fused_computation.27 | convolution fusion | flops 134234112 | bytes 4489216 | tf_op jit(solution)/shard_map/dot_general | solution.py:67
  26.2 0.0 copy-start.3
  26.2 0.0 copy-start.4
  26.3 0.7 broadcast_in_dim.12
  27.0 17.6 %all-to-all-start.1 = ((bf16[32,32,128]{2,1,0:T(8,128)(2,1)}), bf16[32,32,128]{2,1,0:T(8,128)(2,1)S(1)}, u32[]{:S(2)}, u32[]{:S(2)}) async-start(bf16[32,32,128]{2,1,0:T(8,128)(2,1)} %bitcast.6), calls=%async_computation.1 | async-start | bytes 524288 | tf_op jit(solution)/shard_map/all_to_all | solution.py:23
  44.6 0.0 copy-done
  44.6 2.1 %collective-permute-start = (bf16[256,768]{1,0:T(8,128)(2,1)S(1)}, bf16[256,768]{1,0:T(8,128)(2,1)S(1)}, u32[]{:S(2)}, u32[]{:S(2)}) collective-permute-start(bf16[256,768]{1,0:T(8,128)(2,1)S(1)} %copy-done), channel_id=1, source_target_pairs={{0,8},{8,0},{1,9},{9,1},{2,10},{10,2},{3,11},{11,3},{4,12},{12,4},... | collective-permute-start | bytes 1179656 | tf_op jit(solution)/shard_map/ppermute | solution.py:19
  46.8 0.0 collective-permute-done.1
  46.8 2.2 %collective-permute-start.2 = (bf16[256,768]{1,0:T(8,128)(2,1)S(1)}, bf16[256,768]{1,0:T(8,128)(2,1)S(1)}, u32[]{:S(2)}, u32[]{:S(2)}) collective-permute-start(bf16[256,768]{1,0:T(8,128)(2,1)S(1)} %collective-permute-done.1), channel_id=1, source_target_pairs={{0,8},{8,0},{1,9},{9,1},{2,10},{10,2},{3,11},{11,3},{4,12},{12,4},... | collective-permute-start | bytes 1179656 | tf_op jit(solution)/shard_map/ppermute | solution.py:19
  49.0 4.3 %all-to-all-done.1 = bf16[32,32,128]{2,1,0:T(8,128)(2,1)S(1)} async-done(((bf16[32,32,128]{2,1,0:T(8,128)(2,1)}), bf16[32,32,128]{2,1,0:T(8,128)(2,1)S(1)}, u32[]{:S(2)}, u32[]{:S(2)}) %all-to-all-start.1) | async-done | bytes 262176 | tf_op jit(solution)/shard_map/all_to_all | solution.py:23
  53.4 0.2 fusion.45
  53.6 0.0 collective-permute-done
  53.6 0.2 convolution_add_fusion.2
  53.9 0.2 convolution_add_fusion.1
  54.1 0.0 collective-permute-done.2
  54.1 0.9 fusion
  55.0 3.4 %all-to-all-start.2 = ((bf16[4,32,768]{2,1,0:T(8,128)(2,1)}), bf16[4,32,768]{2,1,0:T(8,128)(2,1)S(1)}, u32[]{:S(2)}, u32[]{:S(2)}) async-start(bf16[4,32,768]{2,1,0:T(8,128)(2,1)} %bitcast.13), calls=%async_computation.2 | async-start | bytes 393216 | tf_op jit(solution)/shard_map/all_to_all | solution.py:23
  58.4 0.0 copy-done.1
  58.4 2.1 %collective-permute-start.3 = (f32[1,32,768]{2,1,0:T(8,128)S(1)}, f32[1,32,768]{2,1,0:T(8,128)S(1)}, u32[]{:S(2)}, u32[]{:S(2)}) collective-permute-start(f32[1,32,768]{2,1,0:T(8,128)S(1)} %bitcast.75), channel_id=1, source_target_pairs={{0,2},{2,0},{4,6},{6,4},{1,3},{3,1},{5,7},{7,5},{8,10},{10,8},{12,... | collective-permute-start | bytes 294920 | tf_op jit(solution)/shard_map/ppermute | solution.py:32
  60.5 4.0 %collective-permute-done.3 = f32[1,32,768]{2,1,0:T(8,128)S(1)} collective-permute-done((f32[1,32,768]{2,1,0:T(8,128)S(1)}, f32[1,32,768]{2,1,0:T(8,128)S(1)}, u32[]{:S(2)}, u32[]{:S(2)}) %collective-permute-start.3) | collective-permute-done | bytes 98336 | tf_op jit(solution)/shard_map/ppermute | solution.py:32
  64.6 0.2 all-to-all-done.2
  64.8 0.6 reshape.63
  65.4 19.6 %all-to-all-start.3 = ((bf16[8,4,768]{2,1,0:T(4,128)(2,1)}), bf16[8,4,768]{2,1,0:T(4,128)(2,1)S(1)}, u32[]{:S(2)}, u32[]{:S(2)}) async-start(bf16[8,4,768]{2,1,0:T(4,128)(2,1)} %reshape.63), calls=%async_computation.3 | async-start | bytes 98304 | tf_op jit(solution)/shard_map/all_to_all | solution.py:23
  85.0 2.2 %collective-permute-start.4 = (f32[2,32,768]{2,1,0:T(8,128)S(1)}, f32[2,32,768]{2,1,0:T(8,128)S(1)}, u32[]{:S(2)}, u32[]{:S(2)}) collective-permute-start(f32[2,32,768]{2,1,0:T(8,128)S(1)} %pad_maximum_fusion.2), channel_id=1, source_target_pairs={{0,1},{1,0},{2,3},{3,2},{4,5},{5,4},{6,7},{7,6},{8,9},{9,8},{10,11... | collective-permute-start | bytes 589832 | tf_op jit(solution)/shard_map/ppermute | solution.py:32
  87.2 5.7 %collective-permute-done.4 = f32[2,32,768]{2,1,0:T(8,128)S(1)} collective-permute-done((f32[2,32,768]{2,1,0:T(8,128)S(1)}, f32[2,32,768]{2,1,0:T(8,128)S(1)}, u32[]{:S(2)}, u32[]{:S(2)}) %collective-permute-start.4) | collective-permute-done | bytes 196640 | tf_op jit(solution)/shard_map/ppermute | solution.py:32
  93.0 15.3 %all-to-all-done.3 = bf16[8,4,768]{2,1,0:T(4,128)(2,1)S(1)} async-done(((bf16[8,4,768]{2,1,0:T(4,128)(2,1)}), bf16[8,4,768]{2,1,0:T(4,128)(2,1)S(1)}, u32[]{:S(2)}, u32[]{:S(2)}) %all-to-all-start.3) | async-done | bytes 49184 | tf_op jit(solution)/shard_map/all_to_all | solution.py:23
  108.3 0.0 copy-done.3
  108.3 0.0 copy-done.4
  108.3 0.6 fusion.54
  109.0 0.6 broadcast_in_dim.14
  109.6 5.8 %all-to-all-start.4 = ((bf16[8,4,768]{2,1,0:T(4,128)(2,1)}), bf16[8,4,768]{2,1,0:T(4,128)(2,1)S(1)}, u32[]{:S(2)}, u32[]{:S(2)}) async-start(bf16[8,4,768]{2,1,0:T(4,128)(2,1)} %broadcast_in_dim.14), calls=%async_computation.4 | async-start | bytes 98304 | tf_op jit(solution)/shard_map/all_to_all | solution.py:23
  115.4 3.2 %collective-permute-start.6 = (f32[2,32,768]{2,1,0:T(8,128)S(1)}, f32[2,32,768]{2,1,0:T(8,128)S(1)}, u32[]{:S(2)}, u32[]{:S(2)}) collective-permute-start(f32[2,32,768]{2,1,0:T(8,128)S(1)} %get-tuple-element.31), channel_id=1, source_target_pairs={{0,4},{2,6},{4,0},{6,2},{1,5},{3,7},{5,1},{7,3},{8,12},{10,14},{12... | collective-permute-start | bytes 589832 | tf_op jit(solution)/shard_map/ppermute | solution.py:32
  118.5 3.6 %collective-permute-start.5 = (f32[2,32,768]{2,1,0:T(8,128)S(1)}, f32[2,32,768]{2,1,0:T(8,128)S(1)}, u32[]{:S(2)}, u32[]{:S(2)}) collective-permute-start(f32[2,32,768]{2,1,0:T(8,128)S(1)} %get-tuple-element.30), channel_id=1, source_target_pairs={{0,4},{2,6},{4,0},{6,2},{1,5},{3,7},{5,1},{7,3},{8,12},{10,14},{12... | collective-permute-start | bytes 589832 | tf_op jit(solution)/shard_map/ppermute | solution.py:32
  122.2 1.1 collective-permute-done.6
  123.3 4.1 %collective-permute-done.5 = f32[2,32,768]{2,1,0:T(8,128)S(1)} collective-permute-done((f32[2,32,768]{2,1,0:T(8,128)S(1)}, f32[2,32,768]{2,1,0:T(8,128)S(1)}, u32[]{:S(2)}, u32[]{:S(2)}) %collective-permute-start.5) | collective-permute-done | bytes 196640 | tf_op jit(solution)/shard_map/ppermute | solution.py:32
  127.4 0.1 pad_maximum_fusion
  127.5 10.5 %all-to-all-done.4 = bf16[8,4,768]{2,1,0:T(4,128)(2,1)S(1)} async-done(((bf16[8,4,768]{2,1,0:T(4,128)(2,1)}), bf16[8,4,768]{2,1,0:T(4,128)(2,1)S(1)}, u32[]{:S(2)}, u32[]{:S(2)}) %all-to-all-start.4) | async-done | bytes 49184 | tf_op jit(solution)/shard_map/all_to_all | solution.py:23
  138.0 11.9 %all_to_all.35 = bf16[8,32,768]{2,1,0:T(8,128)(2,1)S(1)} all-to-all(bf16[8,32,768]{2,1,0:T(8,128)(2,1)S(1)} %broadcast_in_dim.32), channel_id=1, replica_groups=mesh['xl'=2,'zh'=8,'zl'=4,'c'=2,'y'=4,'xh'=2] {'xl','zl'}, dimensions={0} | all-to-all | bytes 786432 | tf_op jit(solution)/shard_map/all_to_all | solution.py:23
  149.9 7.6 %collective-permute-start.7 = (bf16[256,768]{1,0:T(8,128)(2,1)S(1)}, bf16[256,768]{1,0:T(8,128)(2,1)S(1)}, u32[]{:S(2)}, u32[]{:S(2)}) collective-permute-start(bf16[256,768]{1,0:T(8,128)(2,1)S(1)} %bitcast.65), channel_id=1, source_target_pairs={{0,8},{8,0},{1,9},{9,1},{2,10},{10,2},{3,11},{11,3},{4,12},{12,4},... | collective-permute-start | bytes 1179656 | tf_op jit(solution)/shard_map/ppermute | solution.py:19
  157.5 1.0 constant_dynamic-slice_fusion
  158.6 0.2 fusion.40
  158.8 0.1 collective-permute-done.7
  158.9 0.2 fusion.1
  159.1 0.8 broadcast_in_dim.33
  159.9 4.6 %all-to-all-start.6 = ((bf16[8,32,768]{2,1,0:T(8,128)(2,1)}), bf16[8,32,768]{2,1,0:T(8,128)(2,1)S(1)}, u32[]{:S(2)}, u32[]{:S(2)}) async-start(bf16[8,32,768]{2,1,0:T(8,128)(2,1)} %broadcast_in_dim.33), calls=%async_computation.6 | async-start | bytes 786432 | tf_op jit(solution)/shard_map/all_to_all | solution.py:23
  164.4 9.6 %all-to-all-done.6 = bf16[8,32,768]{2,1,0:T(8,128)(2,1)S(1)} async-done(((bf16[8,32,768]{2,1,0:T(8,128)(2,1)}), bf16[8,32,768]{2,1,0:T(8,128)(2,1)S(1)}, u32[]{:S(2)}, u32[]{:S(2)}) %all-to-all-start.6) | async-done | bytes 393248 | tf_op jit(solution)/shard_map/all_to_all | solution.py:23
  174.3 0.0 copy-start.2
  174.3 0.9 copy-done.2
  (20 shorter events, 0.4 us)
Async XLA Ops:
  0.6 22.5 %all-to-all-start = ((bf16[8,32,512]{2,1,0:T(8,128)(2,1)}), bf16[8,32,512]{2,1,0:T(8,128)(2,1)S(1)}, u32[]{:S(2)}, u32[]{:S(2)}) async-start(bf16[8,32,512]{2,1,0:T(8,128)(2,1)} %bitcast.73), calls=%async_computation | async-start | bytes 524288 | tf_op jit(solution)/shard_map/all_to_all | solution.py:23
  8.1 38.7 %collective-permute-start.1 = (bf16[256,768]{1,0:T(8,128)(2,1)}, bf16[256,768]{1,0:T(8,128)(2,1)S(1)}, u32[]{:S(2)}, u32[]{:S(2)}) collective-permute-start(bf16[256,768]{1,0:T(8,128)(2,1)} %param.8), channel_id=1, source_target_pairs={{0,512},{512,0},{1,513},{513,1},{2,514},{514,2},{3,515},{515,3},{4... | collective-permute-start | bytes 1179656 | tf_op jit(solution)/shard_map/ppermute | solution.py:19
  23.1 21.5 %copy-start = (bf16[256,768]{1,0:T(8,128)(2,1)S(1)}, bf16[256,768]{1,0:T(8,128)(2,1)}, u32[]{:S(2)}) copy-start(bf16[256,768]{1,0:T(8,128)(2,1)} %param.8) | copy-start | bytes 1179652
  23.1 35.3 %copy-start.1 = (f32[32,768]{1,0:T(8,128)S(1)}, f32[32,768]{1,0:T(8,128)}, u32[]{:S(2)}) copy-start(f32[32,768]{1,0:T(8,128)} %param.9) | copy-start | bytes 294916
  26.2 82.1 %copy-start.3 = (f32[4,768]{1,0:T(4,128)S(1)}, f32[4,768]{1,0:T(4,128)}, u32[]{:S(2)}) copy-start(f32[4,768]{1,0:T(4,128)} %param.10) | copy-start | bytes 36868
  26.2 82.1 %copy-start.4 = (f32[4,768]{1,0:T(4,128)S(1)}, f32[4,768]{1,0:T(4,128)}, u32[]{:S(2)}) copy-start(f32[4,768]{1,0:T(4,128)} %param.11) | copy-start | bytes 36868
  27.0 26.4 %all-to-all-start.1 = ((bf16[32,32,128]{2,1,0:T(8,128)(2,1)}), bf16[32,32,128]{2,1,0:T(8,128)(2,1)S(1)}, u32[]{:S(2)}, u32[]{:S(2)}) async-start(bf16[32,32,128]{2,1,0:T(8,128)(2,1)} %bitcast.6), calls=%async_computation.1 | async-start | bytes 524288 | tf_op jit(solution)/shard_map/all_to_all | solution.py:23
  44.6 8.9 %collective-permute-start = (bf16[256,768]{1,0:T(8,128)(2,1)S(1)}, bf16[256,768]{1,0:T(8,128)(2,1)S(1)}, u32[]{:S(2)}, u32[]{:S(2)}) collective-permute-start(bf16[256,768]{1,0:T(8,128)(2,1)S(1)} %copy-done), channel_id=1, source_target_pairs={{0,8},{8,0},{1,9},{9,1},{2,10},{10,2},{3,11},{11,3},{4,12},{12,4},... | collective-permute-start | bytes 1179656 | tf_op jit(solution)/shard_map/ppermute | solution.py:19
  46.8 7.3 %collective-permute-start.2 = (bf16[256,768]{1,0:T(8,128)(2,1)S(1)}, bf16[256,768]{1,0:T(8,128)(2,1)S(1)}, u32[]{:S(2)}, u32[]{:S(2)}) collective-permute-start(bf16[256,768]{1,0:T(8,128)(2,1)S(1)} %collective-permute-done.1), channel_id=1, source_target_pairs={{0,8},{8,0},{1,9},{9,1},{2,10},{10,2},{3,11},{11,3},{4,12},{12,4},... | collective-permute-start | bytes 1179656 | tf_op jit(solution)/shard_map/ppermute | solution.py:19
  55.0 9.7 %all-to-all-start.2 = ((bf16[4,32,768]{2,1,0:T(8,128)(2,1)}), bf16[4,32,768]{2,1,0:T(8,128)(2,1)S(1)}, u32[]{:S(2)}, u32[]{:S(2)}) async-start(bf16[4,32,768]{2,1,0:T(8,128)(2,1)} %bitcast.13), calls=%async_computation.2 | async-start | bytes 393216 | tf_op jit(solution)/shard_map/all_to_all | solution.py:23
  58.4 6.1 %collective-permute-start.3 = (f32[1,32,768]{2,1,0:T(8,128)S(1)}, f32[1,32,768]{2,1,0:T(8,128)S(1)}, u32[]{:S(2)}, u32[]{:S(2)}) collective-permute-start(f32[1,32,768]{2,1,0:T(8,128)S(1)} %bitcast.75), channel_id=1, source_target_pairs={{0,2},{2,0},{4,6},{6,4},{1,3},{3,1},{5,7},{7,5},{8,10},{10,8},{12,... | collective-permute-start | bytes 294920 | tf_op jit(solution)/shard_map/ppermute | solution.py:32
  65.4 42.9 %all-to-all-start.3 = ((bf16[8,4,768]{2,1,0:T(4,128)(2,1)}), bf16[8,4,768]{2,1,0:T(4,128)(2,1)S(1)}, u32[]{:S(2)}, u32[]{:S(2)}) async-start(bf16[8,4,768]{2,1,0:T(4,128)(2,1)} %reshape.63), calls=%async_computation.3 | async-start | bytes 98304 | tf_op jit(solution)/shard_map/all_to_all | solution.py:23
  85.0 7.9 %collective-permute-start.4 = (f32[2,32,768]{2,1,0:T(8,128)S(1)}, f32[2,32,768]{2,1,0:T(8,128)S(1)}, u32[]{:S(2)}, u32[]{:S(2)}) collective-permute-start(f32[2,32,768]{2,1,0:T(8,128)S(1)} %pad_maximum_fusion.2), channel_id=1, source_target_pairs={{0,1},{1,0},{2,3},{3,2},{4,5},{5,4},{6,7},{7,6},{8,9},{9,8},{10,11... | collective-permute-start | bytes 589832 | tf_op jit(solution)/shard_map/ppermute | solution.py:32
  109.6 28.4 %all-to-all-start.4 = ((bf16[8,4,768]{2,1,0:T(4,128)(2,1)}), bf16[8,4,768]{2,1,0:T(4,128)(2,1)S(1)}, u32[]{:S(2)}, u32[]{:S(2)}) async-start(bf16[8,4,768]{2,1,0:T(4,128)(2,1)} %broadcast_in_dim.14), calls=%async_computation.4 | async-start | bytes 98304 | tf_op jit(solution)/shard_map/all_to_all | solution.py:23
  115.4 7.9 %collective-permute-start.6 = (f32[2,32,768]{2,1,0:T(8,128)S(1)}, f32[2,32,768]{2,1,0:T(8,128)S(1)}, u32[]{:S(2)}, u32[]{:S(2)}) collective-permute-start(f32[2,32,768]{2,1,0:T(8,128)S(1)} %get-tuple-element.31), channel_id=1, source_target_pairs={{0,4},{2,6},{4,0},{6,2},{1,5},{3,7},{5,1},{7,3},{8,12},{10,14},{12... | collective-permute-start | bytes 589832 | tf_op jit(solution)/shard_map/ppermute | solution.py:32
  118.5 8.9 %collective-permute-start.5 = (f32[2,32,768]{2,1,0:T(8,128)S(1)}, f32[2,32,768]{2,1,0:T(8,128)S(1)}, u32[]{:S(2)}, u32[]{:S(2)}) collective-permute-start(f32[2,32,768]{2,1,0:T(8,128)S(1)} %get-tuple-element.30), channel_id=1, source_target_pairs={{0,4},{2,6},{4,0},{6,2},{1,5},{3,7},{5,1},{7,3},{8,12},{10,14},{12... | collective-permute-start | bytes 589832 | tf_op jit(solution)/shard_map/ppermute | solution.py:32
  149.9 8.9 %collective-permute-start.7 = (bf16[256,768]{1,0:T(8,128)(2,1)S(1)}, bf16[256,768]{1,0:T(8,128)(2,1)S(1)}, u32[]{:S(2)}, u32[]{:S(2)}) collective-permute-start(bf16[256,768]{1,0:T(8,128)(2,1)S(1)} %bitcast.65), channel_id=1, source_target_pairs={{0,8},{8,0},{1,9},{9,1},{2,10},{10,2},{3,11},{11,3},{4,12},{12,4},... | collective-permute-start | bytes 1179656 | tf_op jit(solution)/shard_map/ppermute | solution.py:19
  159.9 14.2 %all-to-all-start.6 = ((bf16[8,32,768]{2,1,0:T(8,128)(2,1)}), bf16[8,32,768]{2,1,0:T(8,128)(2,1)S(1)}, u32[]{:S(2)}, u32[]{:S(2)}) async-start(bf16[8,32,768]{2,1,0:T(8,128)(2,1)} %broadcast_in_dim.33), calls=%async_computation.6 | async-start | bytes 786432 | tf_op jit(solution)/shard_map/all_to_all | solution.py:23
  174.3 0.9 copy-start.2

commit v4 on v2

--- a/solution.py
+++ b/solution.py
@@ -1,6 +1,8 @@
 import jax
 import jax.numpy as jnp
 from jax import lax
+from jax.experimental import pallas as pl
+from jax.experimental.pallas import tpu as pltpu
 from jax.sharding import Mesh, PartitionSpec as P
 
 beta_one = 0.9
@@ -28,19 +30,65 @@
 
 
 def rank_order(sizes, total):
-    xl, zh, zl, c = (sizes[a] for a in DP)
-    depth = total // (xl * zh * zl * c)
-    new = lax.broadcasted_iota(jnp.int32, (total, total), 1)
+    zh, zl, c = (sizes[a] for a in ("zh", "zl", "c"))
+    depth = total // (zh * zl * c)
+    new = lax.broadcasted_iota(jnp.int32, (1, total), 1)
     j = new % depth
     rest = new // depth
     izh = rest % zh
     rest = rest // zh
-    izl = rest % zl
-    rest = rest // zl
-    ixl = rest % xl
-    ic = rest // xl
-    old = (((ixl * zh + izh) * zl + izl) * c + ic) * depth + j
+    old = ((izh * zl + rest % zl) * c + rest // zl) * depth + j
     return (lax.broadcasted_iota(jnp.int32, (total, total), 0) == old).astype(bf16)
+
+
+def coords_kernel(acts_ref, basis_ref, order_ref, out_ref, total):
+    step = pl.program_id(0)
+    part = jnp.dot(acts_ref[0], basis_ref[0], preferred_element_type=f32)
+
+    @pl.when(step == 0)
+    def _():
+        total[...] = part
+
+    @pl.when(step > 0)
+    def _():
+        total[...] += part
+
+    @pl.when(step == pl.num_programs(0) - 1)
+    def _():
+        own = total[...].astype(bf16)
+        block = order_ref.shape[0]
+        groups, copies, _, wide = out_ref.shape
+        per = block // wide
+        for x in range(groups // per):
+            half = own[:, x * block : (x + 1) * block]
+            half = jnp.dot(half, order_ref[...], preferred_element_type=f32).astype(bf16)
+            for k in range(per):
+                piece = half[:, k * wide : (k + 1) * wide]
+                for i in range(copies):
+                    out_ref[x * per + k, i] = piece
+
+
+def coords_copies(acts, basis, order, groups):
+    nf, tokens, feats = acts.shape
+    ranks = basis.shape[-1]
+    return pl.pallas_call(
+        coords_kernel,
+        grid=(nf,),
+        in_specs=[
+            pl.BlockSpec((1, tokens, feats), lambda i: (i, 0, 0)),
+            pl.BlockSpec((1, feats, ranks), lambda i: (i, 0, 0)),
+            pl.BlockSpec(order.shape, lambda i: (0, 0)),
+        ],
+        out_specs=pl.BlockSpec((groups, nf, tokens, ranks // groups), lambda i: (0, 0, 0, 0)),
+        out_shape=jax.ShapeDtypeStruct((groups, nf, tokens, ranks // groups), bf16),
+        scratch_shapes=[pltpu.VMEM((tokens, ranks), f32)],
+        cost_estimate=pl.CostEstimate(
+            flops=2 * nf * tokens * feats * ranks,
+            bytes_accessed=2 * nf * feats * (tokens + ranks),
+            transcendentals=0,
+        ),
+        compiler_params=pltpu.CompilerParams(vmem_limit_bytes=52 * 1024 * 1024),
+    )(acts, basis, order)
 
 
 def build(sizes):
@@ -53,27 +101,19 @@
         width = out_grad.shape[1]
         depth = first_moment.shape[0]
         height = master_weight.shape[0]
-        order = rank_order(sizes, ranks)
+        order = rank_order(sizes, ranks // xl)
 
         acts = exchange(activations.reshape(nf, tokens // nf, feats), FS)
-        own = lax.dot_general(
-            acts,
-            proj_basis.reshape(nf, feats, ranks),
-            (((0, 2), (0, 1)), ((), ())),
-            preferred_element_type=f32,
-        ).astype(bf16)
-        own = jnp.dot(own, order, preferred_element_type=f32).astype(bf16)
-        own = own.reshape(tokens // nf, c * xl, ranks // (c * xl)).swapaxes(0, 1)
-        own = jnp.broadcast_to(own[:, None], (c * xl, nf) + own.shape[1:])
-        own = own.reshape((c * xl * nf,) + own.shape[2:])
-        coords = exchange(own, ("c", "xl", "y", "xh"))
-        coords = coords.reshape(c * xl, tokens, ranks // (c * xl))
+        own = coords_copies(acts, proj_basis.reshape(nf, feats, ranks), order, xl * c)
+        own = own.reshape((xl * c * nf,) + own.shape[2:])
+        coords = exchange(own, ("xl", "c", "y", "xh"))
+        coords = coords.reshape(xl * c, tokens, ranks // (xl * c))
 
-        me = lax.axis_index("c") * xl + lax.axis_index("xl")
+        me = lax.axis_index("xl") * c + lax.axis_index("c")
         og_x = swap(out_grad, "xl")
         og_c = swap(out_grad, "c")
         og_xc = swap(og_x, "c")
-        blocks = ((me, out_grad), (me ^ 2, og_c), (me ^ 1, og_x), (me ^ 3, og_xc))
+        blocks = ((me, out_grad), (me ^ 1, og_c), (me ^ 2, og_x), (me ^ 3, og_xc))
         grad = sum(
             lax.dot_general(
                 lax.dynamic_index_in_dim(coords, i, 0, keepdims=False),
@@ -86,6 +126,23 @@
         grad = exchange(grad.reshape(zl, zh * depth, width).astype(bf16), "zl")
         grad = jnp.sum(grad.astype(f32), axis=0)
         grad = exchange(grad.reshape(zh, depth, width).astype(bf16), "zh")
+
+        rows = lax.dynamic_slice_in_dim(proj_basis, lax.axis_index(DP) * height, height, 0)
+        block = ranks // xl
+        rows = [
+            jnp.dot(
+                rows[:, i * block : (i + 1) * block], order, preferred_element_type=f32
+            ).astype(bf16)
+            for i in range(xl)
+        ]
+        piece = block // c
+        basis_rows = jnp.stack(
+            [
+                jnp.concatenate([r[:, k * piece : (k + 1) * piece] for r in rows], axis=1)
+                for k in range(c)
+            ]
+        )
+        grad, basis_rows = lax.optimization_barrier((grad, basis_rows))
         grad = jnp.sum(grad.astype(f32), axis=0)
 
         new_first = beta_one * first_moment + (1.0 - beta_one) * grad
@@ -100,9 +157,6 @@
         full = spread(full, ("xl", "zl"), xl * zl).reshape(ranks // c, width)
         other = swap(full, "c")
 
-        basis_rows = lax.dynamic_slice_in_dim(proj_basis, lax.axis_index(DP) * height, height, 0)
-        basis_rows = jnp.dot(basis_rows, order, preferred_element_type=f32).astype(bf16)
-        basis_rows = basis_rows.reshape(height, c, ranks // c).swapaxes(0, 1)
         core = lax.axis_index("c")
         delta = jnp.dot(
             lax.dynamic_index_in_dim(basis_rows, core, 0, keepdims=False),

time: 161 us -> 164 us (1.019)
  blocking collectives: 91.5 us -> 53.3 us
  waiting for transfers between devices: 18.4 us -> 37.8 us
  starting transfers between devices: 40 us -> 59 us
  Pallas kernels: 0 us -> 6.16 us
  matrix products: 5.73 us -> 3.78 us
    all_to_all x4 -> x3, blocking collectives: 91.5 us -> 53.3 us  [exchange(): return lax.all_to_all(x, axis, 0, 0, tiled=False)]
    all_to_all x3 -> x4, starting transfers between devices: 25.7 us -> 44.9 us  [exchange(): return lax.all_to_all(x, axis, 0, 0, tiled=False)]
    all_to_all x3 -> x4, waiting for transfers between devices: 18.4 us -> 36.6 us  [exchange(): return lax.all_to_all(x, axis, 0, 0, tiled=False)]
    pallas_call x0 -> x1, Pallas kernels: none -> 6.16 us  [coords_copies(): pl.pallas_call(coords_kernel, grid=(nf,), in_specs=[pl.BlockSpec((1, toke...]
    dot_general x2, matrix products: 4.38 us -> 1.77 us  [body(): jnp.dot(rows[:, i * block:(i + 1) * block], order, preferred_element_type...]
  transfers between devices with their start and end apart: 7 -> 8, of which waited for: 3 -> 5; matrix products, arithmetic and copies ran while one was open for 4% -> 2% of each run, Pallas kernels for 0% -> 4%
where the time goes in v4:
time: 164 us; the launch traced here: 163 us
  starting transfers between devices  59 us (36%)
  blocking collectives  53.3 us (32%)
  waiting for transfers between devices  37.8 us (23%)
  Pallas kernels  6.16 us (4%)
  matrix products  3.78 us (2%)
  local copies, waits for them, and re-layouts  1.74 us (1%)
    all_to_all x3, blocking collectives, exchange(): return lax.all_to_all(x, axis, 0, 0, tiled=False)  53.3 us
    all_to_all x4, starting transfers between devices, exchange(): return lax.all_to_all(x, axis, 0, 0, tiled=False)  44.9 us
    all_to_all x4, waiting for transfers between devices, exchange(): return lax.all_to_all(x, axis, 0, 0, tiled=False)  36.6 us
    ppermute x4, starting transfers between devices, swap(): return lax.ppermute(x, axis, [(0, 1), (1, 0)])  14.2 us
    pallas_call x1, Pallas kernels, coords_copies(): pl.pallas_call(coords_kernel, grid=(nf,), in_specs=[pl.BlockSpec((1, toke...  6.16 us
  transfers between devices with their start and end apart: 8, of which 5 were waited for; matrix products, arithmetic and copies ran while one was open for 2% of the time, Pallas kernels for 4%

profile of v4, /device:TPU:1, one launch (start us, length us, event | category | flops | bytes accessed | tf_op | source)
XLA Modules:
  0.0 163.4 jit_solution(13228842681439201655)
XLA Ops:
  0.6 0.0 copy-start
  0.6 7.6 %all-to-all-start = ((bf16[8,32,512]{2,1,0:T(8,128)(2,1)}), bf16[8,32,512]{2,1,0:T(8,128)(2,1)S(1)}, u32[]{:S(2)}, u32[]{:S(2)}) async-start(bf16[8,32,512]{2,1,0:T(8,128)(2,1)} %bitcast.73), calls=%async_computation | async-start | bytes 524288 | tf_op jit(solution)/shard_map/all_to_all | solution.py:25
  8.3 2.2 %collective-permute-start.1 = (bf16[256,768]{1,0:T(8,128)(2,1)}, bf16[256,768]{1,0:T(8,128)(2,1)S(1)}, u32[]{:S(2)}, u32[]{:S(2)}) collective-permute-start(bf16[256,768]{1,0:T(8,128)(2,1)} %param.8), channel_id=1, source_target_pairs={{0,512},{512,0},{1,513},{513,1},{2,514},{514,2},{3,515},{515,3},{4... | collective-permute-start | bytes 1179656 | tf_op jit(solution)/shard_map/ppermute | solution.py:21
  10.5 5.4 %all-to-all-done.acts_ref = bf16[8,32,512]{2,1,0:T(8,128)(2,1)S(1)} async-done(((bf16[8,32,512]{2,1,0:T(8,128)(2,1)}), bf16[8,32,512]{2,1,0:T(8,128)(2,1)S(1)}, u32[]{:S(2)}, u32[]{:S(2)}) %all-to-all-start) | async-done | bytes 262176 | tf_op jit(solution)/shard_map/all_to_all | solution.py:25
  15.9 6.2 %shard_map.85 = bf16[4,8,32,128]{3,2,1,0:T(8,128)(2,1)} custom-call(bf16[8,32,512]{2,1,0:T(8,128)(2,1)S(1)} %all-to-all-done.acts_ref, bf16[8,512,512]{2,1,0:T(8,128)(2,1)} %bitcast.66, bf16[256,256]{1,0:T(8,128)(2,1)S(1)} %fusion.2.order_ref), custom_call_target="tpu_custom_call" | custom-call | flops 134217728 | bytes 4456448 | tf_op jit(solution)/shard_map/pallas_call | solution.py:74
  22.1 0.0 copy-start.3
  22.1 0.0 copy-start.4
  22.1 0.0 copy-start.1
  22.1 14.9 %all-to-all-start.1 = ((bf16[32,32,128]{2,1,0:T(8,128)(2,1)}), bf16[32,32,128]{2,1,0:T(8,128)(2,1)S(1)}, u32[]{:S(2)}, u32[]{:S(2)}) async-start(bf16[32,32,128]{2,1,0:T(8,128)(2,1)} %bitcast.2), calls=%async_computation.1 | async-start | bytes 524288 | tf_op jit(solution)/shard_map/all_to_all | solution.py:25
  37.0 0.0 copy-done
  37.0 2.2 %collective-permute-start = (bf16[256,768]{1,0:T(8,128)(2,1)S(1)}, bf16[256,768]{1,0:T(8,128)(2,1)S(1)}, u32[]{:S(2)}, u32[]{:S(2)}) collective-permute-start(bf16[256,768]{1,0:T(8,128)(2,1)S(1)} %copy-done), channel_id=1, source_target_pairs={{0,8},{8,0},{1,9},{9,1},{2,10},{10,2},{3,11},{11,3},{4,12},{12,4},... | collective-permute-start | bytes 1179656 | tf_op jit(solution)/shard_map/ppermute | solution.py:21
  39.2 0.0 collective-permute-done.1
  39.2 2.1 %collective-permute-start.2 = (bf16[256,768]{1,0:T(8,128)(2,1)S(1)}, bf16[256,768]{1,0:T(8,128)(2,1)S(1)}, u32[]{:S(2)}, u32[]{:S(2)}) collective-permute-start(bf16[256,768]{1,0:T(8,128)(2,1)S(1)} %collective-permute-done.1), channel_id=1, source_target_pairs={{0,8},{8,0},{1,9},{9,1},{2,10},{10,2},{3,11},{11,3},{4,12},{12,4},... | collective-permute-start | bytes 1179656 | tf_op jit(solution)/shard_map/ppermute | solution.py:21
  41.3 4.7 %all-to-all-done.1 = bf16[32,32,128]{2,1,0:T(8,128)(2,1)S(1)} async-done(((bf16[32,32,128]{2,1,0:T(8,128)(2,1)}), bf16[32,32,128]{2,1,0:T(8,128)(2,1)S(1)}, u32[]{:S(2)}, u32[]{:S(2)}) %all-to-all-start.1) | async-done | bytes 262176 | tf_op jit(solution)/shard_map/all_to_all | solution.py:25
  46.0 0.2 fusion.16
  46.3 0.0 collective-permute-done
  46.3 0.2 convolution_add_fusion.2
  46.5 0.2 convolution_add_fusion.1
  46.8 0.0 collective-permute-done.2
  46.8 0.9 fusion
  47.7 3.4 %all-to-all-start.2 = ((bf16[4,32,768]{2,1,0:T(8,128)(2,1)}), bf16[4,32,768]{2,1,0:T(8,128)(2,1)S(1)}, u32[]{:S(2)}, u32[]{:S(2)}) async-start(bf16[4,32,768]{2,1,0:T(8,128)(2,1)} %bitcast.8), calls=%async_computation.2 | async-start | bytes 393216 | tf_op jit(solution)/shard_map/all_to_all | solution.py:25
  51.1 0.9 convolution_convert_fusion.1
  52.0 0.9 convolution_convert_fusion
  52.9 5.0 %all-to-all-done.2 = bf16[4,32,768]{2,1,0:T(8,128)(2,1)S(1)} async-done(((bf16[4,32,768]{2,1,0:T(8,128)(2,1)}), bf16[4,32,768]{2,1,0:T(8,128)(2,1)S(1)}, u32[]{:S(2)}, u32[]{:S(2)}) %all-to-all-start.2) | async-done | bytes 196640 | tf_op jit(solution)/shard_map/all_to_all | solution.py:25
  57.8 0.6 convert_element_type.29
  58.5 19.0 %all-to-all-start.3 = ((bf16[8,4,768]{2,1,0:T(4,128)(2,1)}), bf16[8,4,768]{2,1,0:T(4,128)(2,1)S(1)}, u32[]{:S(2)}, u32[]{:S(2)}) async-start(bf16[8,4,768]{2,1,0:T(4,128)(2,1)} %convert_element_type.29), calls=%async_computation.3 | async-start | bytes 98304 | tf_op jit(solution)/shard_map/all_to_all | solution.py:25
  77.5 21.7 %all-to-all-done.3 = bf16[8,4,768]{2,1,0:T(4,128)(2,1)S(1)} async-done(((bf16[8,4,768]{2,1,0:T(4,128)(2,1)}), bf16[8,4,768]{2,1,0:T(4,128)(2,1)S(1)}, u32[]{:S(2)}, u32[]{:S(2)}) %all-to-all-start.3) | async-done | bytes 49184 | tf_op jit(solution)/shard_map/all_to_all | solution.py:25
  99.2 0.0 copy-done.3
  99.2 0.0 copy-done.4
  99.2 0.6 fusion.30
  99.9 24.2 %all_to_all.35 = bf16[8,4,768]{2,1,0:T(4,128)(2,1)S(1)} all-to-all(bf16[8,4,768]{2,1,0:T(4,128)(2,1)S(1)} %broadcast_in_dim.8), channel_id=1, replica_groups=mesh['xl'=2,'zh'=8,'zl'=4,'c'=2,'y'=4,'xh'=2] {'zh'}, dimensions={0} | all-to-all | bytes 98304 | tf_op jit(solution)/shard_map/all_to_all | solution.py:25
  124.1 12.5 %all_to_all.36 = bf16[8,32,768]{2,1,0:T(8,128)(2,1)S(1)} all-to-all(bf16[8,32,768]{2,1,0:T(8,128)(2,1)S(1)} %broadcast_in_dim.10), channel_id=1, replica_groups=mesh['xl'=2,'zh'=8,'zl'=4,'c'=2,'y'=4,'xh'=2] {'xl','zl'}, dimensions={0} | all-to-all | bytes 786432 | tf_op jit(solution)/shard_map/all_to_all | solution.py:25
  136.6 7.6 %collective-permute-start.3 = (bf16[256,768]{1,0:T(8,128)(2,1)S(1)}, bf16[256,768]{1,0:T(8,128)(2,1)S(1)}, u32[]{:S(2)}, u32[]{:S(2)}) collective-permute-start(bf16[256,768]{1,0:T(8,128)(2,1)S(1)} %bitcast.67), channel_id=1, source_target_pairs={{0,8},{8,0},{1,9},{9,1},{2,10},{10,2},{3,11},{11,3},{4,12},{12,4},... | collective-permute-start | bytes 1179656 | tf_op jit(solution)/shard_map/ppermute | solution.py:21
  144.2 0.2 fusion.25
  144.4 1.1 collective-permute-done.3
  145.6 0.0 copy-done.1
  145.6 0.2 fusion.1
  145.8 0.1 broadcast_in_dim.22
  145.8 16.6 %all_to_all.37 = f32[8,32,768]{2,1,0:T(8,128)S(1)} all-to-all(f32[8,32,768]{2,1,0:T(8,128)S(1)} %broadcast_in_dim.22), channel_id=1, replica_groups=mesh['xl'=2,'zh'=8,'zl'=4,'c'=2,'y'=4,'xh'=2] {'y','xh'}, dimensions={0} | all-to-all | bytes 1572864 | tf_op jit(solution)/shard_map/all_to_all | solution.py:25
  162.5 0.0 copy-start.2
  162.6 0.9 copy-done.2
  (19 shorter events, 0.3 us)
Async XLA Ops:
  0.6 36.3 %copy-start = (bf16[256,768]{1,0:T(8,128)(2,1)S(1)}, bf16[256,768]{1,0:T(8,128)(2,1)}, u32[]{:S(2)}) copy-start(bf16[256,768]{1,0:T(8,128)(2,1)} %param.8) | copy-start | bytes 1179652
  0.6 15.3 %all-to-all-start = ((bf16[8,32,512]{2,1,0:T(8,128)(2,1)}), bf16[8,32,512]{2,1,0:T(8,128)(2,1)S(1)}, u32[]{:S(2)}, u32[]{:S(2)}) async-start(bf16[8,32,512]{2,1,0:T(8,128)(2,1)} %bitcast.73), calls=%async_computation | async-start | bytes 524288 | tf_op jit(solution)/shard_map/all_to_all | solution.py:25
  8.3 30.9 %collective-permute-start.1 = (bf16[256,768]{1,0:T(8,128)(2,1)}, bf16[256,768]{1,0:T(8,128)(2,1)S(1)}, u32[]{:S(2)}, u32[]{:S(2)}) collective-permute-start(bf16[256,768]{1,0:T(8,128)(2,1)} %param.8), channel_id=1, source_target_pairs={{0,512},{512,0},{1,513},{513,1},{2,514},{514,2},{3,515},{515,3},{4... | collective-permute-start | bytes 1179656 | tf_op jit(solution)/shard_map/ppermute | solution.py:21
  22.1 77.1 %copy-start.3 = (f32[4,768]{1,0:T(4,128)S(1)}, f32[4,768]{1,0:T(4,128)}, u32[]{:S(2)}) copy-start(f32[4,768]{1,0:T(4,128)} %param.10) | copy-start | bytes 36868
  22.1 77.2 %copy-start.4 = (f32[4,768]{1,0:T(4,128)S(1)}, f32[4,768]{1,0:T(4,128)}, u32[]{:S(2)}) copy-start(f32[4,768]{1,0:T(4,128)} %param.11) | copy-start | bytes 36868
  22.1 123.5 %copy-start.1 = (f32[32,768]{1,0:T(8,128)S(1)}, f32[32,768]{1,0:T(8,128)}, u32[]{:S(2)}) copy-start(f32[32,768]{1,0:T(8,128)} %param.9) | copy-start | bytes 294916
  22.1 23.9 %all-to-all-start.1 = ((bf16[32,32,128]{2,1,0:T(8,128)(2,1)}), bf16[32,32,128]{2,1,0:T(8,128)(2,1)S(1)}, u32[]{:S(2)}, u32[]{:S(2)}) async-start(bf16[32,32,128]{2,1,0:T(8,128)(2,1)} %bitcast.2), calls=%async_computation.1 | async-start | bytes 524288 | tf_op jit(solution)/shard_map/all_to_all | solution.py:25
  37.0 9.3 %collective-permute-start = (bf16[256,768]{1,0:T(8,128)(2,1)S(1)}, bf16[256,768]{1,0:T(8,128)(2,1)S(1)}, u32[]{:S(2)}, u32[]{:S(2)}) collective-permute-start(bf16[256,768]{1,0:T(8,128)(2,1)S(1)} %copy-done), channel_id=1, source_target_pairs={{0,8},{8,0},{1,9},{9,1},{2,10},{10,2},{3,11},{11,3},{4,12},{12,4},... | collective-permute-start | bytes 1179656 | tf_op jit(solution)/shard_map/ppermute | solution.py:21
  39.2 7.5 %collective-permute-start.2 = (bf16[256,768]{1,0:T(8,128)(2,1)S(1)}, bf16[256,768]{1,0:T(8,128)(2,1)S(1)}, u32[]{:S(2)}, u32[]{:S(2)}) collective-permute-start(bf16[256,768]{1,0:T(8,128)(2,1)S(1)} %collective-permute-done.1), channel_id=1, source_target_pairs={{0,8},{8,0},{1,9},{9,1},{2,10},{10,2},{3,11},{11,3},{4,12},{12,4},... | collective-permute-start | bytes 1179656 | tf_op jit(solution)/shard_map/ppermute | solution.py:21
  47.7 10.1 %all-to-all-start.2 = ((bf16[4,32,768]{2,1,0:T(8,128)(2,1)}), bf16[4,32,768]{2,1,0:T(8,128)(2,1)S(1)}, u32[]{:S(2)}, u32[]{:S(2)}) async-start(bf16[4,32,768]{2,1,0:T(8,128)(2,1)} %bitcast.8), calls=%async_computation.2 | async-start | bytes 393216 | tf_op jit(solution)/shard_map/all_to_all | solution.py:25
  58.5 40.7 %all-to-all-start.3 = ((bf16[8,4,768]{2,1,0:T(4,128)(2,1)}), bf16[8,4,768]{2,1,0:T(4,128)(2,1)S(1)}, u32[]{:S(2)}, u32[]{:S(2)}) async-start(bf16[8,4,768]{2,1,0:T(4,128)(2,1)} %convert_element_type.29), calls=%async_computation.3 | async-start | bytes 98304 | tf_op jit(solution)/shard_map/all_to_all | solution.py:25
  136.6 9.0 %collective-permute-start.3 = (bf16[256,768]{1,0:T(8,128)(2,1)S(1)}, bf16[256,768]{1,0:T(8,128)(2,1)S(1)}, u32[]{:S(2)}, u32[]{:S(2)}) collective-permute-start(bf16[256,768]{1,0:T(8,128)(2,1)S(1)} %bitcast.67), channel_id=1, source_target_pairs={{0,8},{8,0},{1,9},{9,1},{2,10},{10,2},{3,11},{11,3},{4,12},{12,4},... | collective-permute-start | bytes 1179656 | tf_op jit(solution)/shard_map/ppermute | solution.py:21
  162.5 0.9 copy-start.2

commit v5 on v2

v5 whole, which is shorter than its diff:
```python
import jax
import jax.numpy as jnp
from jax import lax
from jax.sharding import Mesh, PartitionSpec as P

beta_one = 0.9
beta_two = 0.999
adam_step = 2
eps_value = 1e-08
step_size = 1.0

f32 = jnp.float32
bf16 = jnp.bfloat16
DP = ("xl", "zh", "zl", "c")
FS = ("y", "xh")


def swap(x, axis):
    return lax.ppermute(x, axis, [(0, 1), (1, 0)])


def exchange(x, axis):
    return lax.all_to_all(x, axis, 0, 0, tiled=False)


def spread(x, axis, n):
    return exchange(jnp.broadcast_to(x[None], (n,) + x.shape), axis)


def rank_order(sizes, total):
    zh, zl = sizes["zh"], sizes["zl"]
    unit = total // (zh * zl)
    new = lax.broadcasted_iota(jnp.int32, (1, total), 1)
    rest = new // unit
    old = ((rest % zh) * zl + rest // zh) * unit + new % unit
    return (lax.broadcasted_iota(jnp.int32, (total, total), 0) == old).astype(bf16)


def pick(x, i):
    return lax.dynamic_index_in_dim(x, i, 0, keepdims=False)


def build(sizes):
    xl, zh, zl, c = (sizes[a] for a in DP)
    nf = sizes["y"] * sizes["xh"]

    def body(activations, proj_basis, out_grad, master_weight, first_moment, second_moment):
        tokens, feats = activations.shape
        ranks = proj_basis.shape[1]
        width = out_grad.shape[1]
        depth = first_moment.shape[0]
        height = master_weight.shape[0]
        unit = c * depth
        half = width // c
        block = ranks // xl
        core, side = lax.axis_index("c"), lax.axis_index("xl")

        acts = exchange(activations.reshape(nf, tokens // nf, feats), FS)

        order = rank_order(sizes, block)
        rows = lax.dynamic_slice_in_dim(
            proj_basis, (lax.axis_index(DP) - core) * height, c * height, 0
        )
        rows = jnp.concatenate(
            [
                jnp.dot(
                    rows[:, i * block : (i + 1) * block], order, preferred_element_type=f32
                ).astype(bf16)
                for i in range(xl)
            ],
            axis=1,
        )
        acts, rows = lax.optimization_barrier((acts, rows))

        own = lax.dot_general(
            acts,
            proj_basis.reshape(nf, feats, ranks),
            (((0, 2), (0, 1)), ((), ())),
            preferred_element_type=f32,
        ).astype(bf16)
        own = jnp.stack([own[:, i * block : (i + 1) * block] for i in range(xl)])
        own = jnp.broadcast_to(own[:, None], (xl, nf) + own.shape[1:])
        coords = exchange(own.reshape(xl * nf, tokens // nf, block), ("xl", "y", "xh"))
        coords = coords.reshape(xl, tokens, block)

        def halves(x):
            return jnp.stack([x[:, i * half : (i + 1) * half] for i in range(c)])

        state = halves(jnp.concatenate([master_weight, first_moment, second_moment]))
        mine = pick(state, core)
        theirs = swap(pick(state, 1 - core), "c")
        both = jnp.stack([jnp.where(core == 0, mine, theirs), jnp.where(core == 0, theirs, mine)])
        weight_rows = both[:, :height]
        first = both[:, height : height + depth].reshape(unit, half)
        second = both[:, height + depth :].reshape(unit, half)

        grad = sum(
            lax.dot_general(pick(coords, i), og, (((0,), (0,)), ((), ())), preferred_element_type=f32)
            for i, og in ((side, out_grad), (1 - side, swap(out_grad, "xl")))
        )
        grad = grad.astype(bf16).reshape(zh, zl, unit, c, half).transpose(3, 1, 0, 2, 4)
        grad = exchange(grad.reshape(c * zl, zh * unit, half), ("c", "zl"))
        grad = jnp.sum(grad.astype(f32), axis=0)
        grad = exchange(grad.reshape(zh, unit, half).astype(bf16), "zh")
        grad = jnp.sum(grad.astype(f32), axis=0)

        correct_one = 1.0 - beta_one**adam_step
        correct_two = 1.0 - beta_two**adam_step

        def moments(first, second, grad):
            new_first = beta_one * first + (1.0 - beta_one) * grad
            new_second = beta_two * second + (1.0 - beta_two) * grad * grad
            return new_first, new_second

        new_first, new_second = moments(first, second, grad)
        update = (
            new_first / correct_one / (jnp.sqrt(new_second / correct_two) + eps_value)
        ).astype(bf16)

        full = spread(update, "zh", zh).reshape(zh * unit, half)
        full = spread(full, ("xl", "zl"), xl * zl).reshape(ranks, half)

        parts = grad.reshape(c, depth, half)
        kept = pick(parts, core)
        got = swap(pick(parts, 1 - core), "c")
        grad = jnp.concatenate(
            [jnp.where(core == 0, kept, got), jnp.where(core == 0, got, kept)], axis=1
        )
        new_first, new_second = moments(first_moment, second_moment, grad)

        delta = jnp.dot(rows, full, preferred_element_type=f32)
        fresh = weight_rows - step_size * delta.reshape(c, height, half)
        fresh = jnp.broadcast_to(fresh[None], (nf,) + fresh.shape)
        new_weight = exchange(fresh.reshape(nf * c, height, half), ("y", "xh", "c"))
        new_weight = jnp.concatenate([new_weight[i] for i in range(nf * c)], axis=1)
        return (new_weight, new_first, new_second)

    return body


def split(mesh):
    names = ("xl", "zh", "zl", "c", "y", "xh")
    return Mesh(mesh.devices.reshape(2, 8, 4, 2, 4, 2), names)


def run_on(fine):
    sizes = dict(fine.shape)
    in_specs = (P(DP, FS), P(), P(DP, FS), P(DP, FS), P(DP, FS), P(DP, FS))
    out_specs = (P(DP, None), P(DP, FS), P(DP, FS))
    return jax.shard_map(
        build(sizes), mesh=fine, in_specs=in_specs, out_specs=out_specs, check_vma=False
    )


def solution(mesh):
    return run_on(split(mesh))
```

time: 161 us -> 170 us (1.056)
  blocking collectives: 91.5 us -> 35.6 us
  waiting for transfers between devices: 18.4 us -> 53.8 us
  starting transfers between devices: 40 us -> 67.7 us
    all_to_all x4 -> x2, blocking collectives: 91.5 us -> 35.6 us  [exchange(): return lax.all_to_all(x, axis, 0, 0, tiled=False)]
    all_to_all x3 -> x5, starting transfers between devices: 25.7 us -> 60.5 us  [exchange(): return lax.all_to_all(x, axis, 0, 0, tiled=False)]
    all_to_all x3 -> x5, waiting for transfers between devices: 18.4 us -> 51.9 us  [exchange(): return lax.all_to_all(x, axis, 0, 0, tiled=False)]
    ppermute x4 -> x3, starting transfers between devices: 14.2 us -> 7.22 us  [swap(): return lax.ppermute(x, axis, [(0, 1), (1, 0)])]
    ppermute x4 -> x3, waiting for transfers between devices: 0.01 us -> 1.88 us  [swap(): return lax.ppermute(x, axis, [(0, 1), (1, 0)])]
    dot_general x8 -> x6, matrix products: 5.73 us -> 5.69 us  [the longest x1 3.02 us: body(): lax.dot_general(acts, proj_basis.reshape(nf, feats, ranks), (((0, 2), (0,...]
  transfers between devices with their start and end apart: 7 -> 8, of which waited for: 3 -> 7; matrix products, arithmetic and copies ran while one was open for 4% -> 2% of each run, Pallas kernels for 0% -> 0%
where the time goes in v5:
time: 170 us; the launch traced here: 169 us
  starting transfers between devices  67.7 us (40%)
  waiting for transfers between devices  53.8 us (32%)
  blocking collectives  35.6 us (21%)
  matrix products  5.69 us (3%)
  local copies, waits for them, and re-layouts  3.57 us (2%)
    all_to_all x5, starting transfers between devices, exchange(): return lax.all_to_all(x, axis, 0, 0, tiled=False)  60.5 us
    all_to_all x5, waiting for transfers between devices, exchange(): return lax.all_to_all(x, axis, 0, 0, tiled=False)  51.9 us
    all_to_all x2, blocking collectives, exchange(): return lax.all_to_all(x, axis, 0, 0, tiled=False)  35.6 us
    ppermute x3, starting transfers between devices, swap(): return lax.ppermute(x, axis, [(0, 1), (1, 0)])  7.22 us
  transfers between devices with their start and end apart: 8, of which 7 were waited for; matrix products, arithmetic and copies ran while one was open for 2% of the time, Pallas kernels for 0%

profile of v5, /device:TPU:1, one launch (start us, length us, event | category | flops | bytes accessed | tf_op | source)
XLA Modules:
  0.0 168.7 jit_solution(2568507141540674727)
XLA Ops:
  0.6 0.0 copy-start
  0.6 7.6 %all-to-all-start = ((bf16[8,32,512]{2,1,0:T(8,128)(2,1)}), bf16[8,32,512]{2,1,0:T(8,128)(2,1)S(1)}, u32[]{:S(2)}, u32[]{:S(2)}) async-start(bf16[8,32,512]{2,1,0:T(8,128)(2,1)} %bitcast.125), calls=%async_computation | async-start | bytes 524288 | tf_op jit(solution)/shard_map/all_to_all | solution.py:23
  8.3 0.9 convolution_convert_fusion.1
  9.2 0.9 convolution_convert_fusion
  10.2 5.7 %all-to-all-done = bf16[8,32,512]{2,1,0:T(8,128)(2,1)S(1)} async-done(((bf16[8,32,512]{2,1,0:T(8,128)(2,1)}), bf16[8,32,512]{2,1,0:T(8,128)(2,1)S(1)}, u32[]{:S(2)}, u32[]{:S(2)}) %all-to-all-start) | async-done | bytes 262176 | tf_op jit(solution)/shard_map/all_to_all | solution.py:23
  15.9 0.0 copy-start.1
  15.9 0.0 copy-start.2
  15.9 0.0 copy-start.3
  15.9 3.0 %fusion.1 = bf16[32,512]{1,0:T(8,128)(2,1)S(1)} fusion(bf16[8,32,512]{2,1,0:T(8,128)(2,1)S(1)} %all-to-all-done, bf16[8,512,512]{2,1,0:T(8,128)(2,1)} %bitcast.120), kind=kOutput, calls=%fused_computation.5 | convolution fusion | flops 134234112 | bytes 4489216 | tf_op jit(solution)/shard_map/dot_general | solution.py:75
  19.0 0.7 broadcast_in_dim.10
  19.7 3.5 %all-to-all-start.1 = ((bf16[16,32,256]{2,1,0:T(8,128)(2,1)}), bf16[16,32,256]{2,1,0:T(8,128)(2,1)S(1)}, u32[]{:S(2)}, u32[]{:S(2)}) async-start(bf16[16,32,256]{2,1,0:T(8,128)(2,1)} %bitcast.12), calls=%async_computation.1 | async-start | bytes 524288 | tf_op jit(solution)/shard_map/all_to_all | solution.py:23
  23.2 0.0 copy-done
  23.3 3.2 %collective-permute-start.1 = (bf16[256,768]{1,0:T(8,128)(2,1)S(1)}, bf16[256,768]{1,0:T(8,128)(2,1)S(1)}, u32[]{:S(2)}, u32[]{:S(2)}) collective-permute-start(bf16[256,768]{1,0:T(8,128)(2,1)S(1)} %copy-done), channel_id=1, source_target_pairs={{0,512},{512,0},{1,513},{513,1},{2,514},{514,2},{3,515},{515,3},{4... | collective-permute-start | bytes 1179656 | tf_op jit(solution)/shard_map/ppermute | solution.py:19
  26.5 4.2 %all-to-all-done.1 = bf16[16,32,256]{2,1,0:T(8,128)(2,1)S(1)} async-done(((bf16[16,32,256]{2,1,0:T(8,128)(2,1)}), bf16[16,32,256]{2,1,0:T(8,128)(2,1)S(1)}, u32[]{:S(2)}, u32[]{:S(2)}) %all-to-all-start.1) | async-done | bytes 262176 | tf_op jit(solution)/shard_map/all_to_all | solution.py:23
  30.6 0.3 fusion.3
  30.9 0.8 collective-permute-done.1
  31.8 0.3 fusion
  32.1 0.8 copy.10
  32.9 15.7 %all-to-all-start.2 = ((bf16[8,64,384]{2,1,0:T(8,128)(2,1)}), bf16[8,64,384]{2,1,0:T(8,128)(2,1)S(1)}, u32[]{:S(2)}, u32[]{:S(2)}) async-start(bf16[8,64,384]{2,1,0:T(8,128)(2,1)} %bitcast.18), calls=%async_computation.2 | async-start | bytes 786432 | tf_op jit(solution)/shard_map/all_to_all | solution.py:23
  48.6 0.0 copy-done.1
  48.6 0.0 copy-done.2
  48.6 0.0 copy-done.3
  48.7 2.0 %collective-permute-start = (f32[40,384]{1,0:T(8,128)S(1)}, f32[40,384]{1,0:T(8,128)S(1)}, u32[]{:S(2)}, u32[]{:S(2)}) collective-permute-start(f32[40,384]{1,0:T(8,128)S(1)} %fusion.12), channel_id=1, source_target_pairs={{0,8},{8,0},{1,9},{9,1},{2,10},{10,2},{3,11},{11,3},{4,12},{12,4},... | collective-permute-start | bytes 184328 | tf_op jit(solution)/shard_map/ppermute | solution.py:19
  50.7 9.8 %all-to-all-done.2 = bf16[8,64,384]{2,1,0:T(8,128)(2,1)S(1)} async-done(((bf16[8,64,384]{2,1,0:T(8,128)(2,1)}), bf16[8,64,384]{2,1,0:T(8,128)(2,1)S(1)}, u32[]{:S(2)}, u32[]{:S(2)}) %all-to-all-start.2) | async-done | bytes 393248 | tf_op jit(solution)/shard_map/all_to_all | solution.py:23
  60.4 0.7 reduce_sum.21
  61.1 22.0 %all-to-all-start.3 = ((bf16[8,8,384]{2,1,0:T(8,128)(2,1)}), bf16[8,8,384]{2,1,0:T(8,128)(2,1)S(1)}, u32[]{:S(2)}, u32[]{:S(2)}) async-start(bf16[8,8,384]{2,1,0:T(8,128)(2,1)} %bitcast.19), calls=%async_computation.3 | async-start | bytes 98304 | tf_op jit(solution)/shard_map/all_to_all | solution.py:23
  83.2 0.0 collective-permute-done
  83.2 21.5 %all-to-all-done.3 = bf16[8,8,384]{2,1,0:T(8,128)(2,1)S(1)} async-done(((bf16[8,8,384]{2,1,0:T(8,128)(2,1)}), bf16[8,8,384]{2,1,0:T(8,128)(2,1)S(1)}, u32[]{:S(2)}, u32[]{:S(2)}) %all-to-all-start.3) | async-done | bytes 49184 | tf_op jit(solution)/shard_map/all_to_all | solution.py:23
  104.8 24.5 %all_to_all.35 = bf16[8,8,384]{2,1,0:T(8,128)(2,1)S(1)} all-to-all(bf16[8,8,384]{2,1,0:T(8,128)(2,1)S(1)} %broadcast_in_dim.11), channel_id=1, replica_groups=mesh['xl'=2,'zh'=8,'zl'=4,'c'=2,'y'=4,'xh'=2] {'zh'}, dimensions={0} | all-to-all | bytes 98304 | tf_op jit(solution)/shard_map/all_to_all | solution.py:23
  129.4 11.1 %all_to_all.36 = bf16[8,64,384]{2,1,0:T(8,128)(2,1)S(1)} all-to-all(bf16[8,64,384]{2,1,0:T(8,128)(2,1)S(1)} %broadcast_in_dim.13), channel_id=1, replica_groups=mesh['xl'=2,'zh'=8,'zl'=4,'c'=2,'y'=4,'xh'=2] {'xl','zl'}, dimensions={0} | all-to-all | bytes 786432 | tf_op jit(solution)/shard_map/all_to_all | solution.py:23
  140.4 0.2 fusion.10
  140.6 1.0 broadcast_in_dim.14
  141.6 11.6 %all-to-all-start.6 = ((f32[16,32,384]{2,1,0:T(8,128)}), f32[16,32,384]{2,1,0:T(8,128)S(1)}, u32[]{:S(2)}, u32[]{:S(2)}) async-start(f32[16,32,384]{2,1,0:T(8,128)} %bitcast.23), calls=%async_computation.6 | async-start | bytes 1572864 | tf_op jit(solution)/shard_map/all_to_all | solution.py:23
  153.2 2.0 %collective-permute-start.2 = (f32[4,384]{1,0:T(4,128)S(1)}, f32[4,384]{1,0:T(4,128)S(1)}, u32[]{:S(2)}, u32[]{:S(2)}) collective-permute-start(f32[4,384]{1,0:T(4,128)S(1)} %dynamic-slice_bitcast_fusion), channel_id=1, source_target_pairs={{0,8},{8,0},{1,9},{9,1},{2,10},{10,2},{3,11},{11,3},{4,12},{12,4},... | collective-permute-start | bytes 18440 | tf_op jit(solution)/shard_map/ppermute | solution.py:19
  155.3 1.0 collective-permute-done.2
  156.3 0.6 fusion.38
  156.9 10.7 %all-to-all-done.6 = f32[16,32,384]{2,1,0:T(8,128)S(1)} async-done(((f32[16,32,384]{2,1,0:T(8,128)}), f32[16,32,384]{2,1,0:T(8,128)S(1)}, u32[]{:S(2)}, u32[]{:S(2)}) %all-to-all-start.6) | async-done | bytes 786464 | tf_op jit(solution)/shard_map/all_to_all | solution.py:23
  167.8 0.0 copy-start.4
  167.8 0.9 copy-done.4
  (34 shorter events, 0.3 us)
Async XLA Ops:
  0.6 22.6 %copy-start = (bf16[256,768]{1,0:T(8,128)(2,1)S(1)}, bf16[256,768]{1,0:T(8,128)(2,1)}, u32[]{:S(2)}) copy-start(bf16[256,768]{1,0:T(8,128)(2,1)} %param.8) | copy-start | bytes 1179652
  0.6 15.3 %all-to-all-start = ((bf16[8,32,512]{2,1,0:T(8,128)(2,1)}), bf16[8,32,512]{2,1,0:T(8,128)(2,1)S(1)}, u32[]{:S(2)}, u32[]{:S(2)}) async-start(bf16[8,32,512]{2,1,0:T(8,128)(2,1)} %bitcast.125), calls=%async_computation | async-start | bytes 524288 | tf_op jit(solution)/shard_map/all_to_all | solution.py:23
  15.9 32.7 %copy-start.1 = (f32[32,768]{1,0:T(8,128)S(1)}, f32[32,768]{1,0:T(8,128)}, u32[]{:S(2)}) copy-start(f32[32,768]{1,0:T(8,128)} %param.9) | copy-start | bytes 294916
  15.9 32.7 %copy-start.2 = (f32[4,768]{1,0:T(4,128)S(1)}, f32[4,768]{1,0:T(4,128)}, u32[]{:S(2)}) copy-start(f32[4,768]{1,0:T(4,128)} %param.11) | copy-start | bytes 36868
  15.9 32.7 %copy-start.3 = (f32[4,768]{1,0:T(4,128)S(1)}, f32[4,768]{1,0:T(4,128)}, u32[]{:S(2)}) copy-start(f32[4,768]{1,0:T(4,128)} %param.10) | copy-start | bytes 36868
  19.7 10.9 %all-to-all-start.1 = ((bf16[16,32,256]{2,1,0:T(8,128)(2,1)}), bf16[16,32,256]{2,1,0:T(8,128)(2,1)S(1)}, u32[]{:S(2)}, u32[]{:S(2)}) async-start(bf16[16,32,256]{2,1,0:T(8,128)(2,1)} %bitcast.12), calls=%async_computation.1 | async-start | bytes 524288 | tf_op jit(solution)/shard_map/all_to_all | solution.py:23
  23.3 8.5 %collective-permute-start.1 = (bf16[256,768]{1,0:T(8,128)(2,1)S(1)}, bf16[256,768]{1,0:T(8,128)(2,1)S(1)}, u32[]{:S(2)}, u32[]{:S(2)}) collective-permute-start(bf16[256,768]{1,0:T(8,128)(2,1)S(1)} %copy-done), channel_id=1, source_target_pairs={{0,512},{512,0},{1,513},{513,1},{2,514},{514,2},{3,515},{515,3},{4... | collective-permute-start | bytes 1179656 | tf_op jit(solution)/shard_map/ppermute | solution.py:19
  32.9 27.6 %all-to-all-start.2 = ((bf16[8,64,384]{2,1,0:T(8,128)(2,1)}), bf16[8,64,384]{2,1,0:T(8,128)(2,1)S(1)}, u32[]{:S(2)}, u32[]{:S(2)}) async-start(bf16[8,64,384]{2,1,0:T(8,128)(2,1)} %bitcast.18), calls=%async_computation.2 | async-start | bytes 786432 | tf_op jit(solution)/shard_map/all_to_all | solution.py:23
  48.7 34.5 %collective-permute-start = (f32[40,384]{1,0:T(8,128)S(1)}, f32[40,384]{1,0:T(8,128)S(1)}, u32[]{:S(2)}, u32[]{:S(2)}) collective-permute-start(f32[40,384]{1,0:T(8,128)S(1)} %fusion.12), channel_id=1, source_target_pairs={{0,8},{8,0},{1,9},{9,1},{2,10},{10,2},{3,11},{11,3},{4,12},{12,4},... | collective-permute-start | bytes 184328 | tf_op jit(solution)/shard_map/ppermute | solution.py:19
  61.1 43.7 %all-to-all-start.3 = ((bf16[8,8,384]{2,1,0:T(8,128)(2,1)}), bf16[8,8,384]{2,1,0:T(8,128)(2,1)S(1)}, u32[]{:S(2)}, u32[]{:S(2)}) async-start(bf16[8,8,384]{2,1,0:T(8,128)(2,1)} %bitcast.19), calls=%async_computation.3 | async-start | bytes 98304 | tf_op jit(solution)/shard_map/all_to_all | solution.py:23
  141.6 26.0 %all-to-all-start.6 = ((f32[16,32,384]{2,1,0:T(8,128)}), f32[16,32,384]{2,1,0:T(8,128)S(1)}, u32[]{:S(2)}, u32[]{:S(2)}) async-start(f32[16,32,384]{2,1,0:T(8,128)} %bitcast.23), calls=%async_computation.6 | async-start | bytes 1572864 | tf_op jit(solution)/shard_map/all_to_all | solution.py:23
  153.2 3.1 %collective-permute-start.2 = (f32[4,384]{1,0:T(4,128)S(1)}, f32[4,384]{1,0:T(4,128)S(1)}, u32[]{:S(2)}, u32[]{:S(2)}) collective-permute-start(f32[4,384]{1,0:T(4,128)S(1)} %dynamic-slice_bitcast_fusion), channel_id=1, source_target_pairs={{0,8},{8,0},{1,9},{9,1},{2,10},{10,2},{3,11},{11,3},{4,12},{12,4},... | collective-permute-start | bytes 18440 | tf_op jit(solution)/shard_map/ppermute | solution.py:19
  167.8 0.9 copy-start.4

commit v6 on v2

--- a/solution.py
+++ b/solution.py
@@ -83,7 +83,10 @@
             )
             for i, og in blocks
         )
-        grad = exchange(grad.reshape(zl, zh * depth, width).astype(bf16), "zl")
+        grad, weight = lax.optimization_barrier((grad.astype(bf16), master_weight))
+        weight = jnp.concatenate([weight, weight[: height // 2]])
+        weights = lax.all_gather(weight, FS, axis=0, tiled=False)
+        grad = exchange(grad.reshape(zl, zh * depth, width), "zl")
         grad = jnp.sum(grad.astype(f32), axis=0)
         grad = exchange(grad.reshape(zh, depth, width).astype(bf16), "zh")
         grad = jnp.sum(grad.astype(f32), axis=0)
@@ -96,7 +99,9 @@
             new_first / correct_one / (jnp.sqrt(new_second / correct_two) + eps_value)
         ).astype(bf16)
 
-        full = spread(update, "zh", zh).reshape(zh * depth, width)
+        full = spread(update, "zh", zh)
+        full, weights = lax.optimization_barrier((full, weights))
+        full = full.reshape(zh * depth, width)
         full = spread(full, ("xl", "zl"), xl * zl).reshape(ranks // c, width)
         other = swap(full, "c")
 
@@ -114,9 +119,10 @@
             other,
             preferred_element_type=f32,
         )
-        fresh = master_weight - step_size * delta
-        new_weight = spread(fresh, FS, nf)
-        new_weight = jnp.concatenate([new_weight[i] for i in range(nf)], axis=1)
+        deltas = spread(delta.astype(bf16), FS, nf)
+        new_weight = jnp.concatenate(
+            [weights[i, :height] - step_size * deltas[i].astype(f32) for i in range(nf)], axis=1
+        )
         return (new_weight, new_first, new_second)
 
     return body

time: 161 us -> 182 us (1.13)
  waiting for transfers between devices: 18.4 us -> 34.7 us
  between operations: 0.95 us -> 14.4 us
  blocking collectives: 91.5 us -> 78.7 us
  starting transfers between devices: 40 us -> 43.3 us
    all_to_all x4 -> x3, blocking collectives: 91.5 us -> 78.7 us  [exchange(): return lax.all_to_all(x, axis, 0, 0, tiled=False)]
    all_gather x0 -> x1, waiting for transfers between devices: none -> 10.1 us  [body(): weights = lax.all_gather(weight, FS, axis=0, tiled=False)]
    all_to_all x3 -> x4, waiting for transfers between devices: 18.4 us -> 24.6 us  [exchange(): return lax.all_to_all(x, axis, 0, 0, tiled=False)]
    all_to_all x3 -> x4, starting transfers between devices: 25.7 us -> 30.2 us  [exchange(): return lax.all_to_all(x, axis, 0, 0, tiled=False)]
  transfers between devices with their start and end apart: 7 -> 9, of which waited for: 3 -> 5; matrix products, arithmetic and copies ran while one was open for 4% -> 4% of each run, Pallas kernels for 0% -> 0%
where the time goes in v6:
time: 182 us
  blocking collectives  78.7 us (43%)
  starting transfers between devices  43.3 us (24%)
  waiting for transfers between devices  34.7 us (19%)
  between operations  14.4 us (8%)
  matrix products  6.4 us (4%)
  local copies, waits for them, and re-layouts  2.63 us (1%)
    all_to_all x3, blocking collectives, exchange(): return lax.all_to_all(x, axis, 0, 0, tiled=False)  78.7 us
    all_to_all x4, starting transfers between devices, exchange(): return lax.all_to_all(x, axis, 0, 0, tiled=False)  30.2 us
    all_to_all x4, waiting for transfers between devices, exchange(): return lax.all_to_all(x, axis, 0, 0, tiled=False)  24.6 us
    ppermute x4, starting transfers between devices, swap(): return lax.ppermute(x, axis, [(0, 1), (1, 0)])  13.1 us
    all_gather x1, waiting for transfers between devices, body(): weights = lax.all_gather(weight, FS, axis=0, tiled=False)  10.1 us
  transfers between devices with their start and end apart: 9, of which 5 were waited for; matrix products, arithmetic and copies ran while one was open for 4% of the time, Pallas kernels for 0%

profile of v6, /device:TPU:1, one launch (start us, length us, event | category | flops | bytes accessed | tf_op | source)
XLA Modules:
  0.0 181.5 jit_solution(8634454073912566813)
XLA Ops:
  7.2 7.5 %all-to-all-start = ((bf16[8,32,512]{2,1,0:T(8,128)(2,1)}), bf16[8,32,512]{2,1,0:T(8,128)(2,1)S(1)}, u32[]{:S(2)}, u32[]{:S(2)}) async-start(bf16[8,32,512]{2,1,0:T(8,128)(2,1)} %bitcast.70), calls=%async_computation | async-start | bytes 524288 | tf_op jit(solution)/shard_map/all_to_all | solution.py:23
  14.7 2.2 %collective-permute-start.1 = (bf16[256,768]{1,0:T(8,128)(2,1)}, bf16[256,768]{1,0:T(8,128)(2,1)S(1)}, u32[]{:S(2)}, u32[]{:S(2)}) collective-permute-start(bf16[256,768]{1,0:T(8,128)(2,1)} %param.8), channel_id=1, source_target_pairs={{0,512},{512,0},{1,513},{513,1},{2,514},{514,2},{3,515},{515,3},{4... | collective-permute-start | bytes 1179656 | tf_op jit(solution)/shard_map/ppermute | solution.py:19
  16.9 5.4 %all-to-all-done = bf16[8,32,512]{2,1,0:T(8,128)(2,1)S(1)} async-done(((bf16[8,32,512]{2,1,0:T(8,128)(2,1)}), bf16[8,32,512]{2,1,0:T(8,128)(2,1)S(1)}, u32[]{:S(2)}, u32[]{:S(2)}) %all-to-all-start) | async-done | bytes 262176 | tf_op jit(solution)/shard_map/all_to_all | solution.py:23
  22.3 0.0 copy-start.1
  22.3 3.3 %convolution_convert_fusion.1 = bf16[32,512]{1,0:T(8,128)(2,1)S(1)} fusion(bf16[8,32,512]{2,1,0:T(8,128)(2,1)S(1)} %all-to-all-done, bf16[8,512,512]{2,1,0:T(8,128)(2,1)} %bitcast.72, s32[512]{0:T(512)S(1)} %get-tuple-element.19, s32[512]{0:T(512)S(1)} %get-tuple-element.20, s32[512]{0:T(512)S(1)} %get-tuple-element.18, s32[512]{0:T(512)S(1)} %get-tuple-element.21, ...), kind=kOutput, calls=%fused_computation.26 | convolution fusion | flops 168853504 | bytes 4498432 | tf_op jit(solution)/shard_map/dot_general | solution.py:65
  25.6 0.7 broadcast_in_dim.10
  26.4 14.8 %all-to-all-start.1 = ((bf16[32,32,128]{2,1,0:T(8,128)(2,1)}), bf16[32,32,128]{2,1,0:T(8,128)(2,1)S(1)}, u32[]{:S(2)}, u32[]{:S(2)}) async-start(bf16[32,32,128]{2,1,0:T(8,128)(2,1)} %bitcast.4), calls=%async_computation.1 | async-start | bytes 524288 | tf_op jit(solution)/shard_map/all_to_all | solution.py:23
  41.2 0.0 copy-done.1
  41.2 2.2 %collective-permute-start = (bf16[256,768]{1,0:T(8,128)(2,1)S(1)}, bf16[256,768]{1,0:T(8,128)(2,1)S(1)}, u32[]{:S(2)}, u32[]{:S(2)}) collective-permute-start(bf16[256,768]{1,0:T(8,128)(2,1)S(1)} %copy-done.1), channel_id=1, source_target_pairs={{0,8},{8,0},{1,9},{9,1},{2,10},{10,2},{3,11},{11,3},{4,12},{12,4},... | collective-permute-start | bytes 1179656 | tf_op jit(solution)/shard_map/ppermute | solution.py:19
  43.4 0.0 collective-permute-done.1
  43.4 2.2 %collective-permute-start.2 = (bf16[256,768]{1,0:T(8,128)(2,1)S(1)}, bf16[256,768]{1,0:T(8,128)(2,1)S(1)}, u32[]{:S(2)}, u32[]{:S(2)}) collective-permute-start(bf16[256,768]{1,0:T(8,128)(2,1)S(1)} %collective-permute-done.1), channel_id=1, source_target_pairs={{0,8},{8,0},{1,9},{9,1},{2,10},{10,2},{3,11},{11,3},{4,12},{12,4},... | collective-permute-start | bytes 1179656 | tf_op jit(solution)/shard_map/ppermute | solution.py:19
  45.6 4.3 %all-to-all-done.1 = bf16[32,32,128]{2,1,0:T(8,128)(2,1)S(1)} async-done(((bf16[32,32,128]{2,1,0:T(8,128)(2,1)}), bf16[32,32,128]{2,1,0:T(8,128)(2,1)S(1)}, u32[]{:S(2)}, u32[]{:S(2)}) %all-to-all-start.1) | async-done | bytes 262176 | tf_op jit(solution)/shard_map/all_to_all | solution.py:23
  49.9 0.2 fusion.25
  50.1 0.0 collective-permute-done
  50.2 0.2 convolution_add_fusion.2
  50.4 0.0 copy-start.2
  50.4 0.0 slice-start
  50.4 0.2 convolution_add_fusion.1
  50.7 0.0 copy-start.4
  50.7 0.0 copy-start.5
  50.7 0.0 collective-permute-done.2
  50.7 0.9 fusion
  51.6 3.4 %all-to-all-start.2 = ((bf16[4,32,768]{2,1,0:T(8,128)(2,1)}), bf16[4,32,768]{2,1,0:T(8,128)(2,1)S(1)}, u32[]{:S(2)}, u32[]{:S(2)}) async-start(bf16[4,32,768]{2,1,0:T(8,128)(2,1)} %bitcast.10), calls=%async_computation.2 | async-start | bytes 393216 | tf_op jit(solution)/shard_map/all_to_all | solution.py:23
  55.0 0.0 all-gather.3.cloned.1.call-start
  55.1 0.0 copy-done.2
  55.1 0.0 slice-done
  55.1 0.7 pad_maximum_fusion
  55.7 0.0 all-gather.3.cloned.1.call-update
  55.8 5.9 %all-to-all-done.2 = bf16[4,32,768]{2,1,0:T(8,128)(2,1)S(1)} async-done(((bf16[4,32,768]{2,1,0:T(8,128)(2,1)}), bf16[4,32,768]{2,1,0:T(8,128)(2,1)S(1)}, u32[]{:S(2)}, u32[]{:S(2)}) %all-to-all-start.2) | async-done | bytes 196640 | tf_op jit(solution)/shard_map/all_to_all | solution.py:23
  61.8 40.5 %all_to_all.35 = bf16[8,4,768]{2,1,0:T(4,128)(2,1)S(1)} all-to-all(bf16[8,4,768]{2,1,0:T(4,128)(2,1)S(1)} %convert_element_type.62), channel_id=1, replica_groups=mesh['xl'=2,'zh'=8,'zl'=4,'c'=2,'y'=4,'xh'=2] {'zh'}, dimensions={0} | all-to-all | bytes 98304 | tf_op jit(solution)/shard_map/all_to_all | solution.py:23
  102.3 0.0 copy-done.4
  102.3 0.0 copy-done.5
  102.3 0.6 fusion.34
  102.9 24.3 %all_to_all.36 = bf16[8,4,768]{2,1,0:T(4,128)(2,1)S(1)} all-to-all(bf16[8,4,768]{2,1,0:T(4,128)(2,1)S(1)} %broadcast_in_dim.11), channel_id=1, replica_groups=mesh['xl'=2,'zh'=8,'zl'=4,'c'=2,'y'=4,'xh'=2] {'zh'}, dimensions={0} | all-to-all | bytes 98304 | tf_op jit(solution)/shard_map/all_to_all | solution.py:23
  127.3 10.1 %all-gather.3.cloned.1.call-done = f32[384,768]{1,0:T(8,128)} async-done(((f32[48,768]{1,0:T(8,128)}), f32[384,768]{1,0:T(8,128)}) %all-gather.3.cloned.1.call-update) | async-done | bytes 1179664 | tf_op jit(solution)/shard_map/all_gather | solution.py:88
  137.4 0.8 broadcast_in_dim.13
  138.1 4.5 %all-to-all-start.5 = ((bf16[8,32,768]{2,1,0:T(8,128)(2,1)}), bf16[8,32,768]{2,1,0:T(8,128)(2,1)S(1)}, u32[]{:S(2)}, u32[]{:S(2)}) async-start(bf16[8,32,768]{2,1,0:T(8,128)(2,1)} %broadcast_in_dim.13), calls=%async_computation.5 | async-start | bytes 786432 | tf_op jit(solution)/shard_map/all_to_all | solution.py:23
  142.7 8.9 %all-to-all-done.5 = bf16[8,32,768]{2,1,0:T(8,128)(2,1)S(1)} async-done(((bf16[8,32,768]{2,1,0:T(8,128)(2,1)}), bf16[8,32,768]{2,1,0:T(8,128)(2,1)S(1)}, u32[]{:S(2)}, u32[]{:S(2)}) %all-to-all-start.5) | async-done | bytes 393248 | tf_op jit(solution)/shard_map/all_to_all | solution.py:23
  151.6 6.5 %collective-permute-start.3 = (bf16[256,768]{1,0:T(8,128)(2,1)S(1)}, bf16[256,768]{1,0:T(8,128)(2,1)S(1)}, u32[]{:S(2)}, u32[]{:S(2)}) collective-permute-start(bf16[256,768]{1,0:T(8,128)(2,1)S(1)} %bitcast.56), channel_id=1, source_target_pairs={{0,8},{8,0},{1,9},{9,1},{2,10},{10,2},{3,11},{11,3},{4,12},{12,4},... | collective-permute-start | bytes 1179656 | tf_op jit(solution)/shard_map/ppermute | solution.py:19
  158.1 1.1 convolution_convert_fusion
  159.2 0.1 constant_dynamic-slice_fusion
  159.3 0.0 copy-start
  159.3 0.2 fusion.32
  159.5 0.0 collective-permute-done.3
  159.5 0.2 fusion.1
  159.8 13.9 %all_to_all.37 = bf16[8,32,768]{2,1,0:T(8,128)(2,1)S(1)} all-to-all(bf16[8,32,768]{2,1,0:T(8,128)(2,1)S(1)} %broadcast_in_dim.14), channel_id=1, replica_groups=mesh['xl'=2,'zh'=8,'zl'=4,'c'=2,'y'=4,'xh'=2] {'y','xh'}, dimensions={0} | all-to-all | bytes 786432 | tf_op jit(solution)/shard_map/all_to_all | solution.py:23
  173.7 0.0 copy-done
  173.8 0.0 copy-start.3
  173.8 0.9 copy-done.3
  (20 shorter events, 0.3 us)
Async XLA Ops:
  7.2 15.1 %all-to-all-start = ((bf16[8,32,512]{2,1,0:T(8,128)(2,1)}), bf16[8,32,512]{2,1,0:T(8,128)(2,1)S(1)}, u32[]{:S(2)}, u32[]{:S(2)}) async-start(bf16[8,32,512]{2,1,0:T(8,128)(2,1)} %bitcast.70), calls=%async_computation | async-start | bytes 524288 | tf_op jit(solution)/shard_map/all_to_all | solution.py:23
  14.7 28.7 %collective-permute-start.1 = (bf16[256,768]{1,0:T(8,128)(2,1)}, bf16[256,768]{1,0:T(8,128)(2,1)S(1)}, u32[]{:S(2)}, u32[]{:S(2)}) collective-permute-start(bf16[256,768]{1,0:T(8,128)(2,1)} %param.8), channel_id=1, source_target_pairs={{0,512},{512,0},{1,513},{513,1},{2,514},{514,2},{3,515},{515,3},{4... | collective-permute-start | bytes 1179656 | tf_op jit(solution)/shard_map/ppermute | solution.py:19
  22.3 18.9 %copy-start.1 = (bf16[256,768]{1,0:T(8,128)(2,1)S(1)}, bf16[256,768]{1,0:T(8,128)(2,1)}, u32[]{:S(2)}) copy-start(bf16[256,768]{1,0:T(8,128)(2,1)} %param.8) | copy-start | bytes 1179652
  26.4 23.5 %all-to-all-start.1 = ((bf16[32,32,128]{2,1,0:T(8,128)(2,1)}), bf16[32,32,128]{2,1,0:T(8,128)(2,1)S(1)}, u32[]{:S(2)}, u32[]{:S(2)}) async-start(bf16[32,32,128]{2,1,0:T(8,128)(2,1)} %bitcast.4), calls=%async_computation.1 | async-start | bytes 524288 | tf_op jit(solution)/shard_map/all_to_all | solution.py:23
  41.2 9.0 %collective-permute-start = (bf16[256,768]{1,0:T(8,128)(2,1)S(1)}, bf16[256,768]{1,0:T(8,128)(2,1)S(1)}, u32[]{:S(2)}, u32[]{:S(2)}) collective-permute-start(bf16[256,768]{1,0:T(8,128)(2,1)S(1)} %copy-done.1), channel_id=1, source_target_pairs={{0,8},{8,0},{1,9},{9,1},{2,10},{10,2},{3,11},{11,3},{4,12},{12,4},... | collective-permute-start | bytes 1179656 | tf_op jit(solution)/shard_map/ppermute | solution.py:19
  43.4 7.3 %collective-permute-start.2 = (bf16[256,768]{1,0:T(8,128)(2,1)S(1)}, bf16[256,768]{1,0:T(8,128)(2,1)S(1)}, u32[]{:S(2)}, u32[]{:S(2)}) collective-permute-start(bf16[256,768]{1,0:T(8,128)(2,1)S(1)} %collective-permute-done.1), channel_id=1, source_target_pairs={{0,8},{8,0},{1,9},{9,1},{2,10},{10,2},{3,11},{11,3},{4,12},{12,4},... | collective-permute-start | bytes 1179656 | tf_op jit(solution)/shard_map/ppermute | solution.py:19
  50.4 4.7 %copy-start.2 = (f32[32,768]{1,0:T(8,128)S(1)}, f32[32,768]{1,0:T(8,128)}, u32[]{:S(2)}) copy-start(f32[32,768]{1,0:T(8,128)} %param.9) | copy-start | bytes 294916
  50.4 4.7 %slice-start = ((f32[32,768]{1,0:T(8,128)}), f32[16,768]{1,0:T(8,128)S(1)}, s32[]{:S(2)}) async-start(f32[32,768]{1,0:T(8,128)} %param.9), calls=%async_computation.8 | async-start | bytes 98304 | tf_op jit(solution)/shard_map/slice | solution.py:87
  50.7 51.6 %copy-start.4 = (f32[4,768]{1,0:T(4,128)S(1)}, f32[4,768]{1,0:T(4,128)}, u32[]{:S(2)}) copy-start(f32[4,768]{1,0:T(4,128)} %param.10) | copy-start | bytes 36868
  50.7 51.6 %copy-start.5 = (f32[4,768]{1,0:T(4,128)S(1)}, f32[4,768]{1,0:T(4,128)}, u32[]{:S(2)}) copy-start(f32[4,768]{1,0:T(4,128)} %param.11) | copy-start | bytes 36868
  51.6 10.1 %all-to-all-start.2 = ((bf16[4,32,768]{2,1,0:T(8,128)(2,1)}), bf16[4,32,768]{2,1,0:T(8,128)(2,1)S(1)}, u32[]{:S(2)}, u32[]{:S(2)}) async-start(bf16[4,32,768]{2,1,0:T(8,128)(2,1)} %bitcast.10), calls=%async_computation.2 | async-start | bytes 393216 | tf_op jit(solution)/shard_map/all_to_all | solution.py:23
  55.0 82.3 %all-gather.3.cloned.1.call-start = ((), (), s32[]{:S(2)}) async-start(), calls=%async_computation.7 | async-start | bytes 1327104 | tf_op jit(solution)/shard_map/all_gather | solution.py:88
  138.1 13.5 %all-to-all-start.5 = ((bf16[8,32,768]{2,1,0:T(8,128)(2,1)}), bf16[8,32,768]{2,1,0:T(8,128)(2,1)S(1)}, u32[]{:S(2)}, u32[]{:S(2)}) async-start(bf16[8,32,768]{2,1,0:T(8,128)(2,1)} %broadcast_in_dim.13), calls=%async_computation.5 | async-start | bytes 786432 | tf_op jit(solution)/shard_map/all_to_all | solution.py:23
  151.6 7.9 %collective-permute-start.3 = (bf16[256,768]{1,0:T(8,128)(2,1)S(1)}, bf16[256,768]{1,0:T(8,128)(2,1)S(1)}, u32[]{:S(2)}, u32[]{:S(2)}) collective-permute-start(bf16[256,768]{1,0:T(8,128)(2,1)S(1)} %bitcast.56), channel_id=1, source_target_pairs={{0,8},{8,0},{1,9},{9,1},{2,10},{10,2},{3,11},{11,3},{4,12},{12,4},... | collective-permute-start | bytes 1179656 | tf_op jit(solution)/shard_map/ppermute | solution.py:19
  159.3 14.3 %copy-start = (f32[384,768]{1,0:T(8,128)S(1)}, f32[384,768]{1,0:T(8,128)}, u32[]{:S(2)}) copy-start(f32[384,768]{1,0:T(8,128)} %all-gather.3.cloned.1.call-done) | copy-start | bytes 3538948
  173.8 0.9 copy-start.3
Sparse Core Ops, SparseCore 0:
  60.2 77.1 all-gather.2

commit v7 on v2

--- a/solution.py
+++ b/solution.py
@@ -97,23 +97,11 @@
         ).astype(bf16)
 
         full = spread(update, "zh", zh).reshape(zh * depth, width)
-        full = spread(full, ("xl", "zl"), xl * zl).reshape(ranks // c, width)
-        other = swap(full, "c")
+        full = spread(full, ("c", "xl", "zl"), c * xl * zl).reshape(ranks, width)
 
         basis_rows = lax.dynamic_slice_in_dim(proj_basis, lax.axis_index(DP) * height, height, 0)
         basis_rows = jnp.dot(basis_rows, order, preferred_element_type=f32).astype(bf16)
-        basis_rows = basis_rows.reshape(height, c, ranks // c).swapaxes(0, 1)
-        core = lax.axis_index("c")
-        delta = jnp.dot(
-            lax.dynamic_index_in_dim(basis_rows, core, 0, keepdims=False),
-            full,
-            preferred_element_type=f32,
-        )
-        delta = delta + jnp.dot(
-            lax.dynamic_index_in_dim(basis_rows, 1 - core, 0, keepdims=False),
-            other,
-            preferred_element_type=f32,
-        )
+        delta = jnp.dot(basis_rows, full, preferred_element_type=f32)
         fresh = master_weight - step_size * delta
         new_weight = spread(fresh, FS, nf)
         new_weight = jnp.concatenate([new_weight[i] for i in range(nf)], axis=1)

time: 161 us -> 170 us (1.056)
  waiting for transfers between devices: 18.4 us -> 31 us
  starting transfers between devices: 40 us -> 37 us
    all_to_all x3, waiting for transfers between devices: 18.4 us -> 31 us  [exchange(): return lax.all_to_all(x, axis, 0, 0, tiled=False)]
    ppermute x4 -> x3, starting transfers between devices: 14.2 us -> 6.54 us  [swap(): return lax.ppermute(x, axis, [(0, 1), (1, 0)])]
    all_to_all x3, starting transfers between devices: 25.7 us -> 30.5 us  [exchange(): return lax.all_to_all(x, axis, 0, 0, tiled=False)]
  transfers between devices with their start and end apart: 7 -> 6, of which waited for: 3 -> 3; matrix products, arithmetic and copies ran while one was open for 4% -> 3% of each run, Pallas kernels for 0% -> 0%
where the time goes in v7:
time: 170 us; the launch traced here: 169 us
  blocking collectives  91.5 us (54%)
  starting transfers between devices  37 us (22%)
  waiting for transfers between devices  31 us (18%)
  matrix products  5.54 us (3%)
  local copies, waits for them, and re-layouts  2.82 us (2%)
    all_to_all x4, blocking collectives, exchange(): return lax.all_to_all(x, axis, 0, 0, tiled=False)  91.5 us
    all_to_all x3, waiting for transfers between devices, exchange(): return lax.all_to_all(x, axis, 0, 0, tiled=False)  31 us
    all_to_all x3, starting transfers between devices, exchange(): return lax.all_to_all(x, axis, 0, 0, tiled=False)  30.5 us
    ppermute x3, starting transfers between devices, swap(): return lax.ppermute(x, axis, [(0, 1), (1, 0)])  6.54 us
  transfers between devices with their start and end apart: 6, of which 3 were waited for; matrix products, arithmetic and copies ran while one was open for 3% of the time, Pallas kernels for 0%

profile of v7, /device:TPU:1, one launch (start us, length us, event | category | flops | bytes accessed | tf_op | source)
XLA Modules:
  0.0 169.5 jit_solution(17116218883568188284)
XLA Ops:
  0.6 7.5 %all-to-all-start = ((bf16[8,32,512]{2,1,0:T(8,128)(2,1)}), bf16[8,32,512]{2,1,0:T(8,128)(2,1)S(1)}, u32[]{:S(2)}, u32[]{:S(2)}) async-start(bf16[8,32,512]{2,1,0:T(8,128)(2,1)} %bitcast.70), calls=%async_computation | async-start | bytes 524288 | tf_op jit(solution)/shard_map/all_to_all | solution.py:23
  8.1 2.2 %collective-permute-start.1 = (bf16[256,768]{1,0:T(8,128)(2,1)}, bf16[256,768]{1,0:T(8,128)(2,1)S(1)}, u32[]{:S(2)}, u32[]{:S(2)}) collective-permute-start(bf16[256,768]{1,0:T(8,128)(2,1)} %param.8), channel_id=1, source_target_pairs={{0,512},{512,0},{1,513},{513,1},{2,514},{514,2},{3,515},{515,3},{4... | collective-permute-start | bytes 1179656 | tf_op jit(solution)/shard_map/ppermute | solution.py:19
  10.4 5.4 %all-to-all-done = bf16[8,32,512]{2,1,0:T(8,128)(2,1)S(1)} async-done(((bf16[8,32,512]{2,1,0:T(8,128)(2,1)}), bf16[8,32,512]{2,1,0:T(8,128)(2,1)S(1)}, u32[]{:S(2)}, u32[]{:S(2)}) %all-to-all-start) | async-done | bytes 262176 | tf_op jit(solution)/shard_map/all_to_all | solution.py:23
  15.8 0.0 copy-start
  15.8 3.3 %convolution_convert_fusion = bf16[32,512]{1,0:T(8,128)(2,1)S(1)} fusion(bf16[8,32,512]{2,1,0:T(8,128)(2,1)S(1)} %all-to-all-done, bf16[8,512,512]{2,1,0:T(8,128)(2,1)} %bitcast.72, s32[512]{0:T(512)S(1)} %get-tuple-element.9, s32[512]{0:T(512)S(1)} %get-tuple-element.10, s32[512]{0:T(512)S(1)} %get-tuple-element.8, s32[512]{0:T(512)S(1)} %get-tuple-element.11, ...), kind=kOutput, calls=%fused_computation.24 | convolution fusion | flops 168853504 | bytes 4498432 | tf_op jit(solution)/shard_map/dot_general | solution.py:65
  19.0 0.0 copy-start.2
  19.1 0.0 copy-start.3
  19.1 0.7 broadcast_in_dim.10
  19.8 0.0 copy-start.4
  19.8 14.9 %all-to-all-start.1 = ((bf16[32,32,128]{2,1,0:T(8,128)(2,1)}), bf16[32,32,128]{2,1,0:T(8,128)(2,1)S(1)}, u32[]{:S(2)}, u32[]{:S(2)}) async-start(bf16[32,32,128]{2,1,0:T(8,128)(2,1)} %bitcast.4), calls=%async_computation.1 | async-start | bytes 524288 | tf_op jit(solution)/shard_map/all_to_all | solution.py:23
  34.8 0.0 copy-done
  34.8 2.2 %collective-permute-start = (bf16[256,768]{1,0:T(8,128)(2,1)S(1)}, bf16[256,768]{1,0:T(8,128)(2,1)S(1)}, u32[]{:S(2)}, u32[]{:S(2)}) collective-permute-start(bf16[256,768]{1,0:T(8,128)(2,1)S(1)} %copy-done), channel_id=1, source_target_pairs={{0,8},{8,0},{1,9},{9,1},{2,10},{10,2},{3,11},{11,3},{4,12},{12,4},... | collective-permute-start | bytes 1179656 | tf_op jit(solution)/shard_map/ppermute | solution.py:19
  37.0 0.0 collective-permute-done.1
  37.0 2.2 %collective-permute-start.2 = (bf16[256,768]{1,0:T(8,128)(2,1)S(1)}, bf16[256,768]{1,0:T(8,128)(2,1)S(1)}, u32[]{:S(2)}, u32[]{:S(2)}) collective-permute-start(bf16[256,768]{1,0:T(8,128)(2,1)S(1)} %collective-permute-done.1), channel_id=1, source_target_pairs={{0,8},{8,0},{1,9},{9,1},{2,10},{10,2},{3,11},{11,3},{4,12},{12,4},... | collective-permute-start | bytes 1179656 | tf_op jit(solution)/shard_map/ppermute | solution.py:19
  39.2 4.3 %all-to-all-done.1 = bf16[32,32,128]{2,1,0:T(8,128)(2,1)S(1)} async-done(((bf16[32,32,128]{2,1,0:T(8,128)(2,1)}), bf16[32,32,128]{2,1,0:T(8,128)(2,1)S(1)}, u32[]{:S(2)}, u32[]{:S(2)}) %all-to-all-start.1) | async-done | bytes 262176 | tf_op jit(solution)/shard_map/all_to_all | solution.py:23
  43.5 0.2 fusion.32
  43.8 0.0 collective-permute-done
  43.8 0.2 convolution_add_fusion.2
  44.0 0.2 convolution_add_fusion.1
  44.3 0.0 collective-permute-done.2
  44.3 0.2 fusion
  44.5 9.4 %all_to_all.35 = bf16[4,32,768]{2,1,0:T(8,128)(2,1)S(1)} all-to-all(bf16[4,32,768]{2,1,0:T(8,128)(2,1)S(1)} %bitcast.69), channel_id=1, replica_groups=mesh['xl'=2,'zh'=8,'zl'=4,'c'=2,'y'=4,'xh'=2] {'zl'}, dimensions={0} | all-to-all | bytes 393216 | tf_op jit(solution)/shard_map/all_to_all | solution.py:23
  54.0 40.2 %all_to_all.36 = bf16[8,4,768]{2,1,0:T(4,128)(2,1)S(1)} all-to-all(bf16[8,4,768]{2,1,0:T(4,128)(2,1)S(1)} %convert_element_type.32), channel_id=1, replica_groups=mesh['xl'=2,'zh'=8,'zl'=4,'c'=2,'y'=4,'xh'=2] {'zh'}, dimensions={0} | all-to-all | bytes 98304 | tf_op jit(solution)/shard_map/all_to_all | solution.py:23
  94.3 0.0 copy-done.2
  94.3 0.0 copy-done.3
  94.3 0.6 fusion.41
  94.9 24.4 %all_to_all.37 = bf16[8,4,768]{2,1,0:T(4,128)(2,1)S(1)} all-to-all(bf16[8,4,768]{2,1,0:T(4,128)(2,1)S(1)} %broadcast_in_dim.11), channel_id=1, replica_groups=mesh['xl'=2,'zh'=8,'zl'=4,'c'=2,'y'=4,'xh'=2] {'zh'}, dimensions={0} | all-to-all | bytes 98304 | tf_op jit(solution)/shard_map/all_to_all | solution.py:23
  119.4 1.0 broadcast_in_dim.13
  120.3 8.0 %all-to-all-start.5 = ((bf16[16,32,768]{2,1,0:T(8,128)(2,1)}), bf16[16,32,768]{2,1,0:T(8,128)(2,1)S(1)}, u32[]{:S(2)}, u32[]{:S(2)}) async-start(bf16[16,32,768]{2,1,0:T(8,128)(2,1)} %broadcast_in_dim.13), calls=%async_computation.5 | async-start | bytes 1572864 | tf_op jit(solution)/shard_map/all_to_all | solution.py:23
  128.4 21.2 %all-to-all-done.5 = bf16[16,32,768]{2,1,0:T(8,128)(2,1)S(1)} async-done(((bf16[16,32,768]{2,1,0:T(8,128)(2,1)}), bf16[16,32,768]{2,1,0:T(8,128)(2,1)S(1)}, u32[]{:S(2)}, u32[]{:S(2)}) %all-to-all-start.5) | async-done | bytes 786464 | tf_op jit(solution)/shard_map/all_to_all | solution.py:23
  149.6 0.0 copy-done.4
  149.6 1.3 convolution_subtract_fusion
  150.9 0.1 broadcast_in_dim.14
  151.0 17.4 %all_to_all.38 = f32[8,32,768]{2,1,0:T(8,128)S(1)} all-to-all(f32[8,32,768]{2,1,0:T(8,128)S(1)} %broadcast_in_dim.14), channel_id=1, replica_groups=mesh['xl'=2,'zh'=8,'zl'=4,'c'=2,'y'=4,'xh'=2] {'y','xh'}, dimensions={0} | all-to-all | bytes 1572864 | tf_op jit(solution)/shard_map/all_to_all | solution.py:23
  168.6 0.0 copy-start.1
  168.6 0.9 copy-done.1
  (18 shorter events, 0.2 us)
Async XLA Ops:
  0.6 15.1 %all-to-all-start = ((bf16[8,32,512]{2,1,0:T(8,128)(2,1)}), bf16[8,32,512]{2,1,0:T(8,128)(2,1)S(1)}, u32[]{:S(2)}, u32[]{:S(2)}) async-start(bf16[8,32,512]{2,1,0:T(8,128)(2,1)} %bitcast.70), calls=%async_computation | async-start | bytes 524288 | tf_op jit(solution)/shard_map/all_to_all | solution.py:23
  8.1 28.9 %collective-permute-start.1 = (bf16[256,768]{1,0:T(8,128)(2,1)}, bf16[256,768]{1,0:T(8,128)(2,1)S(1)}, u32[]{:S(2)}, u32[]{:S(2)}) collective-permute-start(bf16[256,768]{1,0:T(8,128)(2,1)} %param.8), channel_id=1, source_target_pairs={{0,512},{512,0},{1,513},{513,1},{2,514},{514,2},{3,515},{515,3},{4... | collective-permute-start | bytes 1179656 | tf_op jit(solution)/shard_map/ppermute | solution.py:19
  15.8 19.0 %copy-start = (bf16[256,768]{1,0:T(8,128)(2,1)S(1)}, bf16[256,768]{1,0:T(8,128)(2,1)}, u32[]{:S(2)}) copy-start(bf16[256,768]{1,0:T(8,128)(2,1)} %param.8) | copy-start | bytes 1179652
  19.0 75.2 %copy-start.2 = (f32[4,768]{1,0:T(4,128)S(1)}, f32[4,768]{1,0:T(4,128)}, u32[]{:S(2)}) copy-start(f32[4,768]{1,0:T(4,128)} %param.10) | copy-start | bytes 36868
  19.1 75.2 %copy-start.3 = (f32[4,768]{1,0:T(4,128)S(1)}, f32[4,768]{1,0:T(4,128)}, u32[]{:S(2)}) copy-start(f32[4,768]{1,0:T(4,128)} %param.11) | copy-start | bytes 36868
  19.8 129.8 %copy-start.4 = (f32[32,768]{1,0:T(8,128)S(1)}, f32[32,768]{1,0:T(8,128)}, u32[]{:S(2)}) copy-start(f32[32,768]{1,0:T(8,128)} %param.9) | copy-start | bytes 294916
  19.8 23.7 %all-to-all-start.1 = ((bf16[32,32,128]{2,1,0:T(8,128)(2,1)}), bf16[32,32,128]{2,1,0:T(8,128)(2,1)S(1)}, u32[]{:S(2)}, u32[]{:S(2)}) async-start(bf16[32,32,128]{2,1,0:T(8,128)(2,1)} %bitcast.4), calls=%async_computation.1 | async-start | bytes 524288 | tf_op jit(solution)/shard_map/all_to_all | solution.py:23
  34.8 9.0 %collective-permute-start = (bf16[256,768]{1,0:T(8,128)(2,1)S(1)}, bf16[256,768]{1,0:T(8,128)(2,1)S(1)}, u32[]{:S(2)}, u32[]{:S(2)}) collective-permute-start(bf16[256,768]{1,0:T(8,128)(2,1)S(1)} %copy-done), channel_id=1, source_target_pairs={{0,8},{8,0},{1,9},{9,1},{2,10},{10,2},{3,11},{11,3},{4,12},{12,4},... | collective-permute-start | bytes 1179656 | tf_op jit(solution)/shard_map/ppermute | solution.py:19
  37.0 7.3 %collective-permute-start.2 = (bf16[256,768]{1,0:T(8,128)(2,1)S(1)}, bf16[256,768]{1,0:T(8,128)(2,1)S(1)}, u32[]{:S(2)}, u32[]{:S(2)}) collective-permute-start(bf16[256,768]{1,0:T(8,128)(2,1)S(1)} %collective-permute-done.1), channel_id=1, source_target_pairs={{0,8},{8,0},{1,9},{9,1},{2,10},{10,2},{3,11},{11,3},{4,12},{12,4},... | collective-permute-start | bytes 1179656 | tf_op jit(solution)/shard_map/ppermute | solution.py:19
  120.3 29.3 %all-to-all-start.5 = ((bf16[16,32,768]{2,1,0:T(8,128)(2,1)}), bf16[16,32,768]{2,1,0:T(8,128)(2,1)S(1)}, u32[]{:S(2)}, u32[]{:S(2)}) async-start(bf16[16,32,768]{2,1,0:T(8,128)(2,1)} %broadcast_in_dim.13), calls=%async_computation.5 | async-start | bytes 1572864 | tf_op jit(solution)/shard_map/all_to_all | solution.py:23
  168.6 0.9 copy-start.1

commit v8 on v7

--- a/solution.py
+++ b/solution.py
@@ -43,6 +43,19 @@
     return (lax.broadcasted_iota(jnp.int32, (total, total), 0) == old).astype(bf16)
 
 
+def back_order(sizes, total):
+    zh, zl = sizes["zh"], sizes["zl"]
+    unit = total // (zh * zl)
+    new = lax.broadcasted_iota(jnp.int32, (total, total), 1)
+    rest = new // unit
+    old = ((rest % zh) * zl + rest // zh) * unit + new % unit
+    return (lax.broadcasted_iota(jnp.int32, (total, total), 0) == old).astype(bf16)
+
+
+def pick(x, i):
+    return lax.dynamic_index_in_dim(x, i, 0, keepdims=False)
+
+
 def build(sizes):
     xl, zh, zl, c = (sizes[a] for a in DP)
     nf = sizes["y"] * sizes["xh"]
@@ -56,6 +69,23 @@
         order = rank_order(sizes, ranks)
 
         acts = exchange(activations.reshape(nf, tokens // nf, feats), FS)
+
+        core = lax.axis_index("c")
+        half, block = width // c, ranks // xl
+        back = back_order(sizes, block)
+        rows = lax.dynamic_slice_in_dim(
+            proj_basis, (lax.axis_index(DP) - core) * height, c * height, 0
+        )
+        rows = jnp.concatenate(
+            [
+                jnp.dot(
+                    rows[:, i * block : (i + 1) * block], back, preferred_element_type=f32
+                ).astype(bf16)
+                for i in range(xl)
+            ],
+            axis=1,
+        )
+        acts, rows = lax.optimization_barrier((acts, rows))
         own = lax.dot_general(
             acts,
             proj_basis.reshape(nf, feats, ranks),
@@ -67,6 +97,9 @@
         own = jnp.broadcast_to(own[:, None], (c * xl, nf) + own.shape[1:])
         own = own.reshape((c * xl * nf,) + own.shape[2:])
         coords = exchange(own, ("c", "xl", "y", "xh"))
+        mine = lax.dynamic_slice_in_dim(master_weight, core * half, half, 1)
+        theirs = swap(lax.dynamic_slice_in_dim(master_weight, (1 - core) * half, half, 1), "c")
+        coords, theirs = lax.optimization_barrier((coords, theirs))
         coords = coords.reshape(c * xl, tokens, ranks // (c * xl))
 
         me = lax.axis_index("c") * xl + lax.axis_index("xl")
@@ -96,15 +129,17 @@
             new_first / correct_one / (jnp.sqrt(new_second / correct_two) + eps_value)
         ).astype(bf16)
 
-        full = spread(update, "zh", zh).reshape(zh * depth, width)
-        full = spread(full, ("c", "xl", "zl"), c * xl * zl).reshape(ranks, width)
+        full = jnp.stack([update[:, i * half : (i + 1) * half] for i in range(c)])
+        full = jnp.broadcast_to(full[None], (zh,) + full.shape)
+        full = exchange(full.reshape(zh * c, depth, half), ("zh", "c"))
+        full = spread(full.reshape(zh * c * depth, half), ("xl", "zl"), xl * zl)
+        delta = jnp.dot(rows, full.reshape(ranks, half), preferred_element_type=f32)
 
-        basis_rows = lax.dynamic_slice_in_dim(proj_basis, lax.axis_index(DP) * height, height, 0)
-        basis_rows = jnp.dot(basis_rows, order, preferred_element_type=f32).astype(bf16)
-        delta = jnp.dot(basis_rows, full, preferred_element_type=f32)
-        fresh = master_weight - step_size * delta
-        new_weight = spread(fresh, FS, nf)
-        new_weight = jnp.concatenate([new_weight[i] for i in range(nf)], axis=1)
+        weight = jnp.stack([jnp.where(core == 0, mine, theirs), jnp.where(core == 0, theirs, mine)])
+        fresh = weight - step_size * delta.reshape(c, height, half)
+        fresh = jnp.broadcast_to(fresh[None], (nf,) + fresh.shape)
+        new_weight = exchange(fresh.reshape(nf * c, height, half), ("y", "xh", "c"))
+        new_weight = jnp.concatenate([new_weight[i] for i in range(nf * c)], axis=1)
         return (new_weight, new_first, new_second)
 
     return body

time: 170 us -> 164 us (0.965)
  waiting for transfers between devices: 31 us -> 18.6 us
  blocking collectives: 91.5 us -> 99.4 us
  starting transfers between devices: 37 us -> 34.4 us
    all_to_all x3, waiting for transfers between devices: 31 us -> 18.6 us  [exchange(): return lax.all_to_all(x, axis, 0, 0, tiled=False)]
    all_to_all x4, blocking collectives: 91.5 us -> 99.4 us  [exchange(): return lax.all_to_all(x, axis, 0, 0, tiled=False)]
    all_to_all x3, starting transfers between devices: 30.5 us -> 25.7 us  [exchange(): return lax.all_to_all(x, axis, 0, 0, tiled=False)]
    ppermute x3 -> x4, starting transfers between devices: 6.54 us -> 8.69 us  [swap(): return lax.ppermute(x, axis, [(0, 1), (1, 0)])]
  transfers between devices with their start and end apart: 6 -> 7, of which waited for: 3 -> 3; matrix products, arithmetic and copies ran while one was open for 3% -> 4% of each run, Pallas kernels for 0% -> 0%
where the time goes in v8:
time: 164 us; the launch traced here: 163 us
  blocking collectives  99.4 us (61%)
  starting transfers between devices  34.4 us (21%)
  waiting for transfers between devices  18.6 us (11%)
  matrix products  6.31 us (4%)
  local copies, waits for them, and re-layouts  2.68 us (2%)
    all_to_all x4, blocking collectives, exchange(): return lax.all_to_all(x, axis, 0, 0, tiled=False)  99.4 us
    all_to_all x3, starting transfers between devices, exchange(): return lax.all_to_all(x, axis, 0, 0, tiled=False)  25.7 us
    all_to_all x3, waiting for transfers between devices, exchange(): return lax.all_to_all(x, axis, 0, 0, tiled=False)  18.6 us
    ppermute x4, starting transfers between devices, swap(): return lax.ppermute(x, axis, [(0, 1), (1, 0)])  8.69 us
    dot_general x1, matrix products, body(): own = jnp.dot(own, order, preferred_element_type=f32).astype(bf16)  3.29 us
  transfers between devices with their start and end apart: 7, of which 3 were waited for; matrix products, arithmetic and copies ran while one was open for 4% of the time, Pallas kernels for 0%

profile of v8, /device:TPU:1, one launch (start us, length us, event | category | flops | bytes accessed | tf_op | source)
XLA Modules:
  0.0 163.2 jit_solution(961962267450452578)
XLA Ops:
  0.6 7.5 %all-to-all-start = ((bf16[8,32,512]{2,1,0:T(8,128)(2,1)}), bf16[8,32,512]{2,1,0:T(8,128)(2,1)S(1)}, u32[]{:S(2)}, u32[]{:S(2)}) async-start(bf16[8,32,512]{2,1,0:T(8,128)(2,1)} %bitcast.118), calls=%async_computation | async-start | bytes 524288 | tf_op jit(solution)/shard_map/all_to_all | solution.py:23
  8.1 2.2 %collective-permute-start.2 = (bf16[256,768]{1,0:T(8,128)(2,1)}, bf16[256,768]{1,0:T(8,128)(2,1)S(1)}, u32[]{:S(2)}, u32[]{:S(2)}) collective-permute-start(bf16[256,768]{1,0:T(8,128)(2,1)} %param.8), channel_id=1, source_target_pairs={{0,512},{512,0},{1,513},{513,1},{2,514},{514,2},{3,515},{515,3},{4... | collective-permute-start | bytes 1179656 | tf_op jit(solution)/shard_map/ppermute | solution.py:19
  10.4 0.9 convolution_convert_fusion.2
  11.3 0.9 convolution_convert_fusion.1
  12.3 3.4 %all-to-all-done = bf16[8,32,512]{2,1,0:T(8,128)(2,1)S(1)} async-done(((bf16[8,32,512]{2,1,0:T(8,128)(2,1)}), bf16[8,32,512]{2,1,0:T(8,128)(2,1)S(1)}, u32[]{:S(2)}, u32[]{:S(2)}) %all-to-all-start) | async-done | bytes 262176 | tf_op jit(solution)/shard_map/all_to_all | solution.py:23
  15.8 0.0 copy-start
  15.8 0.0 copy-start.1
  15.8 3.3 %convolution_convert_fusion = bf16[32,512]{1,0:T(8,128)(2,1)S(1)} fusion(bf16[8,32,512]{2,1,0:T(8,128)(2,1)S(1)} %all-to-all-done, bf16[8,512,512]{2,1,0:T(8,128)(2,1)} %bitcast.121, s32[512]{0:T(512)S(1)} %get-tuple-element.27, s32[512]{0:T(512)S(1)} %get-tuple-element.28, s32[512]{0:T(512)S(1)} %get-tuple-element.26, s32[512]{0:T(512)S(1)} %get-tuple-element.29, ...), kind=kOutput, calls=%fused_computation.24 | convolution fusion | flops 168853504 | bytes 4498432 | tf_op jit(solution)/shard_map/dot_general | solution.py:95
  19.1 0.0 copy-start.2
  19.1 0.0 copy-start.3
  19.1 0.7 broadcast_in_dim.10
  19.9 14.8 %all-to-all-start.1 = ((bf16[32,32,128]{2,1,0:T(8,128)(2,1)}), bf16[32,32,128]{2,1,0:T(8,128)(2,1)S(1)}, u32[]{:S(2)}, u32[]{:S(2)}) async-start(bf16[32,32,128]{2,1,0:T(8,128)(2,1)} %bitcast.4), calls=%async_computation.1 | async-start | bytes 524288 | tf_op jit(solution)/shard_map/all_to_all | solution.py:23
  34.7 0.0 copy-done
  34.7 2.2 %collective-permute-start.1 = (bf16[256,768]{1,0:T(8,128)(2,1)S(1)}, bf16[256,768]{1,0:T(8,128)(2,1)S(1)}, u32[]{:S(2)}, u32[]{:S(2)}) collective-permute-start(bf16[256,768]{1,0:T(8,128)(2,1)S(1)} %copy-done), channel_id=1, source_target_pairs={{0,8},{8,0},{1,9},{9,1},{2,10},{10,2},{3,11},{11,3},{4,12},{12,4},... | collective-permute-start | bytes 1179656 | tf_op jit(solution)/shard_map/ppermute | solution.py:19
  36.8 0.0 copy-done.1
  36.9 2.2 %collective-permute-start = (f32[32,384]{1,0:T(8,128)S(1)}, f32[32,384]{1,0:T(8,128)S(1)}, u32[]{:S(2)}, u32[]{:S(2)}) collective-permute-start(f32[32,384]{1,0:T(8,128)S(1)} %constant_dynamic-slice_fusion), channel_id=1, source_target_pairs={{0,8},{8,0},{1,9},{9,1},{2,10},{10,2},{3,11},{11,3},{4,12},{12,4},... | collective-permute-start | bytes 147464 | tf_op jit(solution)/shard_map/ppermute | solution.py:19
  39.1 0.0 collective-permute-done.2
  39.1 2.2 %collective-permute-start.3 = (bf16[256,768]{1,0:T(8,128)(2,1)S(1)}, bf16[256,768]{1,0:T(8,128)(2,1)S(1)}, u32[]{:S(2)}, u32[]{:S(2)}) collective-permute-start(bf16[256,768]{1,0:T(8,128)(2,1)S(1)} %collective-permute-done.2), channel_id=1, source_target_pairs={{0,8},{8,0},{1,9},{9,1},{2,10},{10,2},{3,11},{11,3},{4,12},{12,4},... | collective-permute-start | bytes 1179656 | tf_op jit(solution)/shard_map/ppermute | solution.py:19
  41.2 0.0 collective-permute-done
  41.3 2.1 %all-to-all-done.1 = bf16[32,32,128]{2,1,0:T(8,128)(2,1)S(1)} async-done(((bf16[32,32,128]{2,1,0:T(8,128)(2,1)}), bf16[32,32,128]{2,1,0:T(8,128)(2,1)S(1)}, u32[]{:S(2)}, u32[]{:S(2)}) %all-to-all-start.1) | async-done | bytes 262176 | tf_op jit(solution)/shard_map/all_to_all | solution.py:23
  43.4 0.2 fusion.51
  43.6 0.0 collective-permute-done.1
  43.6 0.2 convolution_add_fusion.2
  43.9 0.2 convolution_add_fusion.1
  44.1 0.0 collective-permute-done.3
  44.2 0.2 fusion
  44.4 9.4 %all_to_all.35 = bf16[4,32,768]{2,1,0:T(8,128)(2,1)S(1)} all-to-all(bf16[4,32,768]{2,1,0:T(8,128)(2,1)S(1)} %bitcast.116), channel_id=1, replica_groups=mesh['xl'=2,'zh'=8,'zl'=4,'c'=2,'y'=4,'xh'=2] {'zl'}, dimensions={0} | all-to-all | bytes 393216 | tf_op jit(solution)/shard_map/all_to_all | solution.py:23
  53.8 41.7 %all_to_all.36 = bf16[8,4,768]{2,1,0:T(4,128)(2,1)S(1)} all-to-all(bf16[8,4,768]{2,1,0:T(4,128)(2,1)S(1)} %convert_element_type.37), channel_id=1, replica_groups=mesh['xl'=2,'zh'=8,'zl'=4,'c'=2,'y'=4,'xh'=2] {'zh'}, dimensions={0} | all-to-all | bytes 98304 | tf_op jit(solution)/shard_map/all_to_all | solution.py:23
  95.6 0.0 copy-done.2
  95.6 0.0 copy-done.3
  95.6 0.6 fusion.76
  96.3 28.2 %all_to_all.37 = bf16[16,4,384]{2,1,0:T(4,128)(2,1)S(1)} all-to-all(bf16[16,4,384]{2,1,0:T(4,128)(2,1)S(1)} %bitcast.119), channel_id=1, replica_groups=mesh['xl'=2,'zh'=8,'zl'=4,'c'=2,'y'=4,'xh'=2] {'zh','c'}, dimensions={0} | all-to-all | bytes 98304 | tf_op jit(solution)/shard_map/all_to_all | solution.py:23
  124.5 0.8 broadcast_in_dim.13
  125.3 3.5 %all-to-all-start.5 = ((bf16[8,64,384]{2,1,0:T(8,128)(2,1)}), bf16[8,64,384]{2,1,0:T(8,128)(2,1)S(1)}, u32[]{:S(2)}, u32[]{:S(2)}) async-start(bf16[8,64,384]{2,1,0:T(8,128)(2,1)} %broadcast_in_dim.13), calls=%async_computation.5 | async-start | bytes 786432 | tf_op jit(solution)/shard_map/all_to_all | solution.py:23
  128.7 13.0 %all-to-all-done.5 = bf16[8,64,384]{2,1,0:T(8,128)(2,1)S(1)} async-done(((bf16[8,64,384]{2,1,0:T(8,128)(2,1)}), bf16[8,64,384]{2,1,0:T(8,128)(2,1)S(1)}, u32[]{:S(2)}, u32[]{:S(2)}) %all-to-all-start.5) | async-done | bytes 393248 | tf_op jit(solution)/shard_map/all_to_all | solution.py:23
  141.7 0.2 convolution_subtract_fusion
  141.9 0.1 broadcast_in_dim.14
  142.0 20.1 %all_to_all.38 = f32[16,32,384]{2,1,0:T(8,128)S(1)} all-to-all(f32[16,32,384]{2,1,0:T(8,128)S(1)} %bitcast.110), channel_id=1, replica_groups=mesh['xl'=2,'zh'=8,'zl'=4,'c'=2,'y'=4,'xh'=2] {'y','xh','c'}, dimensions={0} | all-to-all | bytes 1572864 | tf_op jit(solution)/shard_map/all_to_all | solution.py:23
  162.3 0.0 copy-start.4
  162.3 0.9 copy-done.4
  (34 shorter events, 0.3 us)
Async XLA Ops:
  0.6 15.1 %all-to-all-start = ((bf16[8,32,512]{2,1,0:T(8,128)(2,1)}), bf16[8,32,512]{2,1,0:T(8,128)(2,1)S(1)}, u32[]{:S(2)}, u32[]{:S(2)}) async-start(bf16[8,32,512]{2,1,0:T(8,128)(2,1)} %bitcast.118), calls=%async_computation | async-start | bytes 524288 | tf_op jit(solution)/shard_map/all_to_all | solution.py:23
  8.1 31.0 %collective-permute-start.2 = (bf16[256,768]{1,0:T(8,128)(2,1)}, bf16[256,768]{1,0:T(8,128)(2,1)S(1)}, u32[]{:S(2)}, u32[]{:S(2)}) collective-permute-start(bf16[256,768]{1,0:T(8,128)(2,1)} %param.8), channel_id=1, source_target_pairs={{0,512},{512,0},{1,513},{513,1},{2,514},{514,2},{3,515},{515,3},{4... | collective-permute-start | bytes 1179656 | tf_op jit(solution)/shard_map/ppermute | solution.py:19
  15.8 18.9 %copy-start = (bf16[256,768]{1,0:T(8,128)(2,1)S(1)}, bf16[256,768]{1,0:T(8,128)(2,1)}, u32[]{:S(2)}) copy-start(bf16[256,768]{1,0:T(8,128)(2,1)} %param.8) | copy-start | bytes 1179652
  15.8 21.1 %copy-start.1 = (f32[32,768]{1,0:T(8,128)S(1)}, f32[32,768]{1,0:T(8,128)}, u32[]{:S(2)}) copy-start(f32[32,768]{1,0:T(8,128)} %param.9) | copy-start | bytes 294916
  19.1 76.5 %copy-start.2 = (f32[4,768]{1,0:T(4,128)S(1)}, f32[4,768]{1,0:T(4,128)}, u32[]{:S(2)}) copy-start(f32[4,768]{1,0:T(4,128)} %param.10) | copy-start | bytes 36868
  19.1 76.5 %copy-start.3 = (f32[4,768]{1,0:T(4,128)S(1)}, f32[4,768]{1,0:T(4,128)}, u32[]{:S(2)}) copy-start(f32[4,768]{1,0:T(4,128)} %param.11) | copy-start | bytes 36868
  19.9 23.5 %all-to-all-start.1 = ((bf16[32,32,128]{2,1,0:T(8,128)(2,1)}), bf16[32,32,128]{2,1,0:T(8,128)(2,1)S(1)}, u32[]{:S(2)}, u32[]{:S(2)}) async-start(bf16[32,32,128]{2,1,0:T(8,128)(2,1)} %bitcast.4), calls=%async_computation.1 | async-start | bytes 524288 | tf_op jit(solution)/shard_map/all_to_all | solution.py:23
  34.7 9.0 %collective-permute-start.1 = (bf16[256,768]{1,0:T(8,128)(2,1)S(1)}, bf16[256,768]{1,0:T(8,128)(2,1)S(1)}, u32[]{:S(2)}, u32[]{:S(2)}) collective-permute-start(bf16[256,768]{1,0:T(8,128)(2,1)S(1)} %copy-done), channel_id=1, source_target_pairs={{0,8},{8,0},{1,9},{9,1},{2,10},{10,2},{3,11},{11,3},{4,12},{12,4},... | collective-permute-start | bytes 1179656 | tf_op jit(solution)/shard_map/ppermute | solution.py:19
  36.9 4.4 %collective-permute-start = (f32[32,384]{1,0:T(8,128)S(1)}, f32[32,384]{1,0:T(8,128)S(1)}, u32[]{:S(2)}, u32[]{:S(2)}) collective-permute-start(f32[32,384]{1,0:T(8,128)S(1)} %constant_dynamic-slice_fusion), channel_id=1, source_target_pairs={{0,8},{8,0},{1,9},{9,1},{2,10},{10,2},{3,11},{11,3},{4,12},{12,4},... | collective-permute-start | bytes 147464 | tf_op jit(solution)/shard_map/ppermute | solution.py:19
  39.1 5.1 %collective-permute-start.3 = (bf16[256,768]{1,0:T(8,128)(2,1)S(1)}, bf16[256,768]{1,0:T(8,128)(2,1)S(1)}, u32[]{:S(2)}, u32[]{:S(2)}) collective-permute-start(bf16[256,768]{1,0:T(8,128)(2,1)S(1)} %collective-permute-done.2), channel_id=1, source_target_pairs={{0,8},{8,0},{1,9},{9,1},{2,10},{10,2},{3,11},{11,3},{4,12},{12,4},... | collective-permute-start | bytes 1179656 | tf_op jit(solution)/shard_map/ppermute | solution.py:19
  125.3 16.5 %all-to-all-start.5 = ((bf16[8,64,384]{2,1,0:T(8,128)(2,1)}), bf16[8,64,384]{2,1,0:T(8,128)(2,1)S(1)}, u32[]{:S(2)}, u32[]{:S(2)}) async-start(bf16[8,64,384]{2,1,0:T(8,128)(2,1)} %broadcast_in_dim.13), calls=%async_computation.5 | async-start | bytes 786432 | tf_op jit(solution)/shard_map/all_to_all | solution.py:23
  162.3 0.9 copy-start.4

commit v9 on v2

--- a/solution.py
+++ b/solution.py
@@ -8,6 +8,7 @@
 adam_step = 2
 eps_value = 1e-08
 step_size = 1.0
+lift = 16.0
 
 f32 = jnp.float32
 bf16 = jnp.bfloat16
@@ -115,8 +116,10 @@
             preferred_element_type=f32,
         )
         fresh = master_weight - step_size * delta
-        new_weight = spread(fresh, FS, nf)
-        new_weight = jnp.concatenate([new_weight[i] for i in range(nf)], axis=1)
+        new_weight = spread((lift * fresh).astype(jnp.float16), FS, nf)
+        new_weight = jnp.concatenate(
+            [new_weight[i].astype(f32) * (1.0 / lift) for i in range(nf)], axis=1
+        )
         return (new_weight, new_first, new_second)
 
     return body

time: 161 us -> 157 us (0.975)
  blocking collectives: 91.5 us -> 87.6 us
    all_to_all x4, blocking collectives: 91.5 us -> 87.6 us  [exchange(): return lax.all_to_all(x, axis, 0, 0, tiled=False)]
where the time goes in v9:
time: 157 us; the launch traced here: 156 us
  blocking collectives  87.6 us (56%)
  starting transfers between devices  40 us (25%)
  waiting for transfers between devices  18.4 us (12%)
  matrix products  5.73 us (4%)
  local copies, waits for them, and re-layouts  2.62 us (2%)
    all_to_all x4, blocking collectives, exchange(): return lax.all_to_all(x, axis, 0, 0, tiled=False)  87.6 us
    all_to_all x3, starting transfers between devices, exchange(): return lax.all_to_all(x, axis, 0, 0, tiled=False)  25.7 us
    all_to_all x3, waiting for transfers between devices, exchange(): return lax.all_to_all(x, axis, 0, 0, tiled=False)  18.4 us
    ppermute x4, starting transfers between devices, swap(): return lax.ppermute(x, axis, [(0, 1), (1, 0)])  14.2 us
    dot_general x1, matrix products, body(): own = jnp.dot(own, order, preferred_element_type=f32).astype(bf16)  3.28 us
  transfers between devices with their start and end apart: 7, of which 3 were waited for; matrix products, arithmetic and copies ran while one was open for 4% of the time, Pallas kernels for 0%

profile of v9, /device:TPU:1, one launch (start us, length us, event | category | flops | bytes accessed | tf_op | source)
XLA Modules:
  0.0 156.0 jit_solution(17715845949292478232)
XLA Ops:
  0.6 7.5 %all-to-all-start = ((bf16[8,32,512]{2,1,0:T(8,128)(2,1)}), bf16[8,32,512]{2,1,0:T(8,128)(2,1)S(1)}, u32[]{:S(2)}, u32[]{:S(2)}) async-start(bf16[8,32,512]{2,1,0:T(8,128)(2,1)} %bitcast.62), calls=%async_computation | async-start | bytes 524288 | tf_op jit(solution)/shard_map/all_to_all | solution.py:24
  8.1 2.2 %collective-permute-start.1 = (bf16[256,768]{1,0:T(8,128)(2,1)}, bf16[256,768]{1,0:T(8,128)(2,1)S(1)}, u32[]{:S(2)}, u32[]{:S(2)}) collective-permute-start(bf16[256,768]{1,0:T(8,128)(2,1)} %param.8), channel_id=1, source_target_pairs={{0,512},{512,0},{1,513},{513,1},{2,514},{514,2},{3,515},{515,3},{4... | collective-permute-start | bytes 1179656 | tf_op jit(solution)/shard_map/ppermute | solution.py:20
  10.4 5.4 %all-to-all-done = bf16[8,32,512]{2,1,0:T(8,128)(2,1)S(1)} async-done(((bf16[8,32,512]{2,1,0:T(8,128)(2,1)}), bf16[8,32,512]{2,1,0:T(8,128)(2,1)S(1)}, u32[]{:S(2)}, u32[]{:S(2)}) %all-to-all-start) | async-done | bytes 262176 | tf_op jit(solution)/shard_map/all_to_all | solution.py:24
  15.8 0.0 copy-start
  15.8 3.3 %convolution_convert_fusion = bf16[32,512]{1,0:T(8,128)(2,1)S(1)} fusion(bf16[8,32,512]{2,1,0:T(8,128)(2,1)S(1)} %all-to-all-done, bf16[8,512,512]{2,1,0:T(8,128)(2,1)} %bitcast.64, s32[512]{0:T(512)S(1)} %get-tuple-element.11, s32[512]{0:T(512)S(1)} %get-tuple-element.12, s32[512]{0:T(512)S(1)} %get-tuple-element.10, s32[512]{0:T(512)S(1)} %get-tuple-element.13, ...), kind=kOutput, calls=%fused_computation.27 | convolution fusion | flops 168853504 | bytes 4498432 | tf_op jit(solution)/shard_map/dot_general | solution.py:66
  19.0 0.0 copy-start.3
  19.1 0.0 copy-start.4
  19.1 0.7 broadcast_in_dim.10
  19.8 14.8 %all-to-all-start.1 = ((bf16[32,32,128]{2,1,0:T(8,128)(2,1)}), bf16[32,32,128]{2,1,0:T(8,128)(2,1)S(1)}, u32[]{:S(2)}, u32[]{:S(2)}) async-start(bf16[32,32,128]{2,1,0:T(8,128)(2,1)} %bitcast.5), calls=%async_computation.1 | async-start | bytes 524288 | tf_op jit(solution)/shard_map/all_to_all | solution.py:24
  34.7 0.0 copy-done
  34.7 2.2 %collective-permute-start = (bf16[256,768]{1,0:T(8,128)(2,1)S(1)}, bf16[256,768]{1,0:T(8,128)(2,1)S(1)}, u32[]{:S(2)}, u32[]{:S(2)}) collective-permute-start(bf16[256,768]{1,0:T(8,128)(2,1)S(1)} %copy-done), channel_id=1, source_target_pairs={{0,8},{8,0},{1,9},{9,1},{2,10},{10,2},{3,11},{11,3},{4,12},{12,4},... | collective-permute-start | bytes 1179656 | tf_op jit(solution)/shard_map/ppermute | solution.py:20
  36.9 0.0 collective-permute-done.1
  36.9 2.2 %collective-permute-start.2 = (bf16[256,768]{1,0:T(8,128)(2,1)S(1)}, bf16[256,768]{1,0:T(8,128)(2,1)S(1)}, u32[]{:S(2)}, u32[]{:S(2)}) collective-permute-start(bf16[256,768]{1,0:T(8,128)(2,1)S(1)} %collective-permute-done.1), channel_id=1, source_target_pairs={{0,8},{8,0},{1,9},{9,1},{2,10},{10,2},{3,11},{11,3},{4,12},{12,4},... | collective-permute-start | bytes 1179656 | tf_op jit(solution)/shard_map/ppermute | solution.py:20
  39.0 4.3 %all-to-all-done.1 = bf16[32,32,128]{2,1,0:T(8,128)(2,1)S(1)} async-done(((bf16[32,32,128]{2,1,0:T(8,128)(2,1)}), bf16[32,32,128]{2,1,0:T(8,128)(2,1)S(1)}, u32[]{:S(2)}, u32[]{:S(2)}) %all-to-all-start.1) | async-done | bytes 262176 | tf_op jit(solution)/shard_map/all_to_all | solution.py:24
  43.4 0.2 fusion.27
  43.6 0.0 collective-permute-done
  43.6 0.2 convolution_add_fusion.2
  43.9 0.2 convolution_add_fusion.1
  44.1 0.0 collective-permute-done.2
  44.1 0.2 fusion
  44.4 9.4 %all_to_all.35 = bf16[4,32,768]{2,1,0:T(8,128)(2,1)S(1)} all-to-all(bf16[4,32,768]{2,1,0:T(8,128)(2,1)S(1)} %bitcast.61), channel_id=1, replica_groups=mesh['xl'=2,'zh'=8,'zl'=4,'c'=2,'y'=4,'xh'=2] {'zl'}, dimensions={0} | all-to-all | bytes 393216 | tf_op jit(solution)/shard_map/all_to_all | solution.py:24
  53.8 40.2 %all_to_all.36 = bf16[8,4,768]{2,1,0:T(4,128)(2,1)S(1)} all-to-all(bf16[8,4,768]{2,1,0:T(4,128)(2,1)S(1)} %convert_element_type.67), channel_id=1, replica_groups=mesh['xl'=2,'zh'=8,'zl'=4,'c'=2,'y'=4,'xh'=2] {'zh'}, dimensions={0} | all-to-all | bytes 98304 | tf_op jit(solution)/shard_map/all_to_all | solution.py:24
  94.1 0.0 copy-done.3
  94.1 0.0 copy-done.4
  94.1 0.6 fusion.36
  94.8 24.4 %all_to_all.37 = bf16[8,4,768]{2,1,0:T(4,128)(2,1)S(1)} all-to-all(bf16[8,4,768]{2,1,0:T(4,128)(2,1)S(1)} %broadcast_in_dim.11), channel_id=1, replica_groups=mesh['xl'=2,'zh'=8,'zl'=4,'c'=2,'y'=4,'xh'=2] {'zh'}, dimensions={0} | all-to-all | bytes 98304 | tf_op jit(solution)/shard_map/all_to_all | solution.py:24
  119.2 0.8 broadcast_in_dim.13
  120.0 3.5 %all-to-all-start.5 = ((bf16[8,32,768]{2,1,0:T(8,128)(2,1)}), bf16[8,32,768]{2,1,0:T(8,128)(2,1)S(1)}, u32[]{:S(2)}, u32[]{:S(2)}) async-start(bf16[8,32,768]{2,1,0:T(8,128)(2,1)} %broadcast_in_dim.13), calls=%async_computation.5 | async-start | bytes 786432 | tf_op jit(solution)/shard_map/all_to_all | solution.py:24
  123.5 8.7 %all-to-all-done.5 = bf16[8,32,768]{2,1,0:T(8,128)(2,1)S(1)} async-done(((bf16[8,32,768]{2,1,0:T(8,128)(2,1)}), bf16[8,32,768]{2,1,0:T(8,128)(2,1)S(1)}, u32[]{:S(2)}, u32[]{:S(2)}) %all-to-all-start.5) | async-done | bytes 393248 | tf_op jit(solution)/shard_map/all_to_all | solution.py:24
  132.1 0.0 copy-start.1
  132.1 7.7 %collective-permute-start.3 = (bf16[256,768]{1,0:T(8,128)(2,1)S(1)}, bf16[256,768]{1,0:T(8,128)(2,1)S(1)}, u32[]{:S(2)}, u32[]{:S(2)}) collective-permute-start(bf16[256,768]{1,0:T(8,128)(2,1)S(1)} %bitcast.55), channel_id=1, source_target_pairs={{0,8},{8,0},{1,9},{9,1},{2,10},{10,2},{3,11},{11,3},{4,12},{12,4},... | collective-permute-start | bytes 1179656 | tf_op jit(solution)/shard_map/ppermute | solution.py:20
  139.8 1.1 convolution_convert_fusion.1
  141.0 0.1 constant_dynamic-slice_fusion
  141.0 0.2 fusion.34
  141.2 0.0 collective-permute-done.3
  141.2 0.0 copy-done.1
  141.2 0.2 fusion.3
  141.5 13.5 %all_to_all.38 = f16[8,32,768]{2,1,0:T(8,128)(2,1)S(1)} all-to-all(f16[8,32,768]{2,1,0:T(8,128)(2,1)S(1)} %broadcast_in_dim.14), channel_id=1, replica_groups=mesh['xl'=2,'zh'=8,'zl'=4,'c'=2,'y'=4,'xh'=2] {'y','xh'}, dimensions={0} | all-to-all | bytes 786432 | tf_op jit(solution)/shard_map/all_to_all | solution.py:24
  155.1 0.0 copy-start.2
  155.1 0.9 copy-done.2
  (20 shorter events, 0.3 us)
Async XLA Ops:
  0.6 15.1 %all-to-all-start = ((bf16[8,32,512]{2,1,0:T(8,128)(2,1)}), bf16[8,32,512]{2,1,0:T(8,128)(2,1)S(1)}, u32[]{:S(2)}, u32[]{:S(2)}) async-start(bf16[8,32,512]{2,1,0:T(8,128)(2,1)} %bitcast.62), calls=%async_computation | async-start | bytes 524288 | tf_op jit(solution)/shard_map/all_to_all | solution.py:24
  8.1 28.7 %collective-permute-start.1 = (bf16[256,768]{1,0:T(8,128)(2,1)}, bf16[256,768]{1,0:T(8,128)(2,1)S(1)}, u32[]{:S(2)}, u32[]{:S(2)}) collective-permute-start(bf16[256,768]{1,0:T(8,128)(2,1)} %param.8), channel_id=1, source_target_pairs={{0,512},{512,0},{1,513},{513,1},{2,514},{514,2},{3,515},{515,3},{4... | collective-permute-start | bytes 1179656 | tf_op jit(solution)/shard_map/ppermute | solution.py:20
  15.8 18.9 %copy-start = (bf16[256,768]{1,0:T(8,128)(2,1)S(1)}, bf16[256,768]{1,0:T(8,128)(2,1)}, u32[]{:S(2)}) copy-start(bf16[256,768]{1,0:T(8,128)(2,1)} %param.8) | copy-start | bytes 1179652
  19.0 75.1 %copy-start.3 = (f32[4,768]{1,0:T(4,128)S(1)}, f32[4,768]{1,0:T(4,128)}, u32[]{:S(2)}) copy-start(f32[4,768]{1,0:T(4,128)} %param.10) | copy-start | bytes 36868
  19.1 75.1 %copy-start.4 = (f32[4,768]{1,0:T(4,128)S(1)}, f32[4,768]{1,0:T(4,128)}, u32[]{:S(2)}) copy-start(f32[4,768]{1,0:T(4,128)} %param.11) | copy-start | bytes 36868
  19.8 23.5 %all-to-all-start.1 = ((bf16[32,32,128]{2,1,0:T(8,128)(2,1)}), bf16[32,32,128]{2,1,0:T(8,128)(2,1)S(1)}, u32[]{:S(2)}, u32[]{:S(2)}) async-start(bf16[32,32,128]{2,1,0:T(8,128)(2,1)} %bitcast.5), calls=%async_computation.1 | async-start | bytes 524288 | tf_op jit(solution)/shard_map/all_to_all | solution.py:24
  34.7 9.0 %collective-permute-start = (bf16[256,768]{1,0:T(8,128)(2,1)S(1)}, bf16[256,768]{1,0:T(8,128)(2,1)S(1)}, u32[]{:S(2)}, u32[]{:S(2)}) collective-permute-start(bf16[256,768]{1,0:T(8,128)(2,1)S(1)} %copy-done), channel_id=1, source_target_pairs={{0,8},{8,0},{1,9},{9,1},{2,10},{10,2},{3,11},{11,3},{4,12},{12,4},... | collective-permute-start | bytes 1179656 | tf_op jit(solution)/shard_map/ppermute | solution.py:20
  36.9 7.3 %collective-permute-start.2 = (bf16[256,768]{1,0:T(8,128)(2,1)S(1)}, bf16[256,768]{1,0:T(8,128)(2,1)S(1)}, u32[]{:S(2)}, u32[]{:S(2)}) collective-permute-start(bf16[256,768]{1,0:T(8,128)(2,1)S(1)} %collective-permute-done.1), channel_id=1, source_target_pairs={{0,8},{8,0},{1,9},{9,1},{2,10},{10,2},{3,11},{11,3},{4,12},{12,4},... | collective-permute-start | bytes 1179656 | tf_op jit(solution)/shard_map/ppermute | solution.py:20
  120.0 12.1 %all-to-all-start.5 = ((bf16[8,32,768]{2,1,0:T(8,128)(2,1)}), bf16[8,32,768]{2,1,0:T(8,128)(2,1)S(1)}, u32[]{:S(2)}, u32[]{:S(2)}) async-start(bf16[8,32,768]{2,1,0:T(8,128)(2,1)} %broadcast_in_dim.13), calls=%async_computation.5 | async-start | bytes 786432 | tf_op jit(solution)/shard_map/all_to_all | solution.py:24
  132.1 9.1 %copy-start.1 = (f32[32,768]{1,0:T(8,128)S(1)}, f32[32,768]{1,0:T(8,128)}, u32[]{:S(2)}) copy-start(f32[32,768]{1,0:T(8,128)} %param.9) | copy-start | bytes 294916
  132.1 9.1 %collective-permute-start.3 = (bf16[256,768]{1,0:T(8,128)(2,1)S(1)}, bf16[256,768]{1,0:T(8,128)(2,1)S(1)}, u32[]{:S(2)}, u32[]{:S(2)}) collective-permute-start(bf16[256,768]{1,0:T(8,128)(2,1)S(1)} %bitcast.55), channel_id=1, source_target_pairs={{0,8},{8,0},{1,9},{9,1},{2,10},{10,2},{3,11},{11,3},{4,12},{12,4},... | collective-permute-start | bytes 1179656 | tf_op jit(solution)/shard_map/ppermute | solution.py:20
  155.1 0.9 copy-start.2

commit v10 on v7

--- a/solution.py
+++ b/solution.py
@@ -8,6 +8,7 @@
 adam_step = 2
 eps_value = 1e-08
 step_size = 1.0
+lift = 16.0
 
 f32 = jnp.float32
 bf16 = jnp.bfloat16
@@ -43,6 +44,17 @@
     return (lax.broadcasted_iota(jnp.int32, (total, total), 0) == old).astype(bf16)
 
 
+def back_order(sizes, total):
+    zh, zl, c = (sizes[a] for a in ("zh", "zl", "c"))
+    depth = total // (zh * zl * c)
+    new = lax.broadcasted_iota(jnp.int32, (total, total), 1)
+    rest = new // depth
+    izh = rest % zh
+    rest = rest // zh
+    old = ((izh * zl + rest % zl) * c + rest // zl) * depth + new % depth
+    return (lax.broadcasted_iota(jnp.int32, (total, total), 0) == old).astype(bf16)
+
+
 def build(sizes):
     xl, zh, zl, c = (sizes[a] for a in DP)
     nf = sizes["y"] * sizes["xh"]
@@ -56,6 +68,20 @@
         order = rank_order(sizes, ranks)
 
         acts = exchange(activations.reshape(nf, tokens // nf, feats), FS)
+
+        block = ranks // xl
+        back = back_order(sizes, block)
+        rows = lax.dynamic_slice_in_dim(proj_basis, lax.axis_index(DP) * height, height, 0)
+        rows = jnp.concatenate(
+            [
+                jnp.dot(
+                    rows[:, i * block : (i + 1) * block], back, preferred_element_type=f32
+                ).astype(bf16)
+                for i in range(xl)
+            ],
+            axis=1,
+        )
+        acts, rows = lax.optimization_barrier((acts, rows))
         own = lax.dot_general(
             acts,
             proj_basis.reshape(nf, feats, ranks),
@@ -97,14 +123,14 @@
         ).astype(bf16)
 
         full = spread(update, "zh", zh).reshape(zh * depth, width)
-        full = spread(full, ("c", "xl", "zl"), c * xl * zl).reshape(ranks, width)
-
-        basis_rows = lax.dynamic_slice_in_dim(proj_basis, lax.axis_index(DP) * height, height, 0)
-        basis_rows = jnp.dot(basis_rows, order, preferred_element_type=f32).astype(bf16)
-        delta = jnp.dot(basis_rows, full, preferred_element_type=f32)
+        full = spread(full, "zl", zl).reshape(zl * zh * depth, width)
+        full = lax.all_gather(full, ("xl", "c"), axis=0, tiled=True)
+        delta = jnp.dot(rows, full, preferred_element_type=f32)
         fresh = master_weight - step_size * delta
-        new_weight = spread(fresh, FS, nf)
-        new_weight = jnp.concatenate([new_weight[i] for i in range(nf)], axis=1)
+        new_weight = spread((lift * fresh).astype(jnp.float16), FS, nf)
+        new_weight = jnp.concatenate(
+            [new_weight[i].astype(f32) * (1.0 / lift) for i in range(nf)], axis=1
+        )
         return (new_weight, new_first, new_second)
 
     return body

time: 170 us -> 157 us (0.924)
  waiting for transfers between devices: 31 us -> 7.87 us
  blocking collectives: 91.5 us -> 110 us
  starting transfers between devices: 37 us -> 28.8 us
    all_to_all x3 -> x2, waiting for transfers between devices: 31 us -> 7.86 us  [exchange(): return lax.all_to_all(x, axis, 0, 0, tiled=False)]
    all_gather x0 -> x1, blocking collectives: none -> 13 us  [body(): full = lax.all_gather(full, ('xl', 'c'), axis=0, tiled=True)]
    all_to_all x3 -> x2, starting transfers between devices: 30.5 us -> 22.3 us  [exchange(): return lax.all_to_all(x, axis, 0, 0, tiled=False)]
    all_to_all x4 -> x5, blocking collectives: 91.5 us -> 96.8 us  [exchange(): return lax.all_to_all(x, axis, 0, 0, tiled=False)]
  transfers between devices with their start and end apart: 6 -> 5, of which waited for: 3 -> 2; matrix products, arithmetic and copies ran while one was open for 3% -> 4% of each run, Pallas kernels for 0% -> 0%
where the time goes in v10:
time: 157 us; the launch traced here: 156 us
  blocking collectives  110 us (70%)
  starting transfers between devices  28.8 us (18%)
  waiting for transfers between devices  7.87 us (5%)
  matrix products  6.29 us (4%)
  local copies, waits for them, and re-layouts  1.76 us (1%)
    all_to_all x5, blocking collectives, exchange(): return lax.all_to_all(x, axis, 0, 0, tiled=False)  96.8 us
    all_to_all x2, starting transfers between devices, exchange(): return lax.all_to_all(x, axis, 0, 0, tiled=False)  22.3 us
    all_gather x1, blocking collectives, body(): full = lax.all_gather(full, ('xl', 'c'), axis=0, tiled=True)  13 us
    all_to_all x2, waiting for transfers between devices, exchange(): return lax.all_to_all(x, axis, 0, 0, tiled=False)  7.86 us
    ppermute x3, starting transfers between devices, swap(): return lax.ppermute(x, axis, [(0, 1), (1, 0)])  6.54 us
    dot_general x1, matrix products, body(): own = jnp.dot(own, order, preferred_element_type=f32).astype(bf16)  3.28 us
  transfers between devices with their start and end apart: 5, of which 2 were waited for; matrix products, arithmetic and copies ran while one was open for 4% of the time, Pallas kernels for 0%

profile of v10, /device:TPU:1, one launch (start us, length us, event | category | flops | bytes accessed | tf_op | source)
XLA Modules:
  0.0 156.3 jit_solution(6840945773812959360)
XLA Ops:
  0.6 7.5 %all-to-all-start = ((bf16[8,32,512]{2,1,0:T(8,128)(2,1)}), bf16[8,32,512]{2,1,0:T(8,128)(2,1)S(1)}, u32[]{:S(2)}, u32[]{:S(2)}) async-start(bf16[8,32,512]{2,1,0:T(8,128)(2,1)} %bitcast.55), calls=%async_computation | async-start | bytes 524288 | tf_op jit(solution)/shard_map/all_to_all | solution.py:24
  8.1 2.2 %collective-permute-start.1 = (bf16[256,768]{1,0:T(8,128)(2,1)}, bf16[256,768]{1,0:T(8,128)(2,1)S(1)}, u32[]{:S(2)}, u32[]{:S(2)}) collective-permute-start(bf16[256,768]{1,0:T(8,128)(2,1)} %param.8), channel_id=1, source_target_pairs={{0,512},{512,0},{1,513},{513,1},{2,514},{514,2},{3,515},{515,3},{4... | collective-permute-start | bytes 1179656 | tf_op jit(solution)/shard_map/ppermute | solution.py:20
  10.4 0.9 convolution_convert_fusion.2
  11.3 0.9 convolution_convert_fusion.1
  12.2 3.5 %all-to-all-done = bf16[8,32,512]{2,1,0:T(8,128)(2,1)S(1)} async-done(((bf16[8,32,512]{2,1,0:T(8,128)(2,1)}), bf16[8,32,512]{2,1,0:T(8,128)(2,1)S(1)}, u32[]{:S(2)}, u32[]{:S(2)}) %all-to-all-start) | async-done | bytes 262176 | tf_op jit(solution)/shard_map/all_to_all | solution.py:24
  15.8 0.0 copy-start
  15.8 3.3 %convolution_convert_fusion = bf16[32,512]{1,0:T(8,128)(2,1)S(1)} fusion(bf16[8,32,512]{2,1,0:T(8,128)(2,1)S(1)} %all-to-all-done, bf16[8,512,512]{2,1,0:T(8,128)(2,1)} %bitcast.57, s32[512]{0:T(512)S(1)} %get-tuple-element.19, s32[512]{0:T(512)S(1)} %get-tuple-element.20, s32[512]{0:T(512)S(1)} %get-tuple-element.18, s32[512]{0:T(512)S(1)} %get-tuple-element.21, ...), kind=kOutput, calls=%fused_computation.26 | convolution fusion | flops 168853504 | bytes 4498432 | tf_op jit(solution)/shard_map/dot_general | solution.py:91
  19.0 0.0 copy-start.3
  19.1 0.0 copy-start.4
  19.1 0.0 copy-start.1
  19.1 0.7 broadcast_in_dim.10
  19.9 14.8 %all-to-all-start.1 = ((bf16[32,32,128]{2,1,0:T(8,128)(2,1)}), bf16[32,32,128]{2,1,0:T(8,128)(2,1)S(1)}, u32[]{:S(2)}, u32[]{:S(2)}) async-start(bf16[32,32,128]{2,1,0:T(8,128)(2,1)} %bitcast.4), calls=%async_computation.1 | async-start | bytes 524288 | tf_op jit(solution)/shard_map/all_to_all | solution.py:24
  34.7 0.0 copy-done
  34.7 2.2 %collective-permute-start = (bf16[256,768]{1,0:T(8,128)(2,1)S(1)}, bf16[256,768]{1,0:T(8,128)(2,1)S(1)}, u32[]{:S(2)}, u32[]{:S(2)}) collective-permute-start(bf16[256,768]{1,0:T(8,128)(2,1)S(1)} %copy-done), channel_id=1, source_target_pairs={{0,8},{8,0},{1,9},{9,1},{2,10},{10,2},{3,11},{11,3},{4,12},{12,4},... | collective-permute-start | bytes 1179656 | tf_op jit(solution)/shard_map/ppermute | solution.py:20
  36.9 0.0 collective-permute-done.1
  36.9 2.2 %collective-permute-start.2 = (bf16[256,768]{1,0:T(8,128)(2,1)S(1)}, bf16[256,768]{1,0:T(8,128)(2,1)S(1)}, u32[]{:S(2)}, u32[]{:S(2)}) collective-permute-start(bf16[256,768]{1,0:T(8,128)(2,1)S(1)} %collective-permute-done.1), channel_id=1, source_target_pairs={{0,8},{8,0},{1,9},{9,1},{2,10},{10,2},{3,11},{11,3},{4,12},{12,4},... | collective-permute-start | bytes 1179656 | tf_op jit(solution)/shard_map/ppermute | solution.py:20
  39.1 4.3 %all-to-all-done.1 = bf16[32,32,128]{2,1,0:T(8,128)(2,1)S(1)} async-done(((bf16[32,32,128]{2,1,0:T(8,128)(2,1)}), bf16[32,32,128]{2,1,0:T(8,128)(2,1)S(1)}, u32[]{:S(2)}, u32[]{:S(2)}) %all-to-all-start.1) | async-done | bytes 262176 | tf_op jit(solution)/shard_map/all_to_all | solution.py:24
  43.4 0.2 fusion.59
  43.6 0.0 collective-permute-done
  43.6 0.2 convolution_add_fusion.2
  43.9 0.2 convolution_add_fusion.1
  44.1 0.0 collective-permute-done.2
  44.2 0.2 fusion
  44.4 9.4 %all_to_all.35 = bf16[4,32,768]{2,1,0:T(8,128)(2,1)S(1)} all-to-all(bf16[4,32,768]{2,1,0:T(8,128)(2,1)S(1)} %bitcast.53), channel_id=1, replica_groups=mesh['xl'=2,'zh'=8,'zl'=4,'c'=2,'y'=4,'xh'=2] {'zl'}, dimensions={0} | all-to-all | bytes 393216 | tf_op jit(solution)/shard_map/all_to_all | solution.py:24
  53.8 40.2 %all_to_all.36 = bf16[8,4,768]{2,1,0:T(4,128)(2,1)S(1)} all-to-all(bf16[8,4,768]{2,1,0:T(4,128)(2,1)S(1)} %convert_element_type.72), channel_id=1, replica_groups=mesh['xl'=2,'zh'=8,'zl'=4,'c'=2,'y'=4,'xh'=2] {'zh'}, dimensions={0} | all-to-all | bytes 98304 | tf_op jit(solution)/shard_map/all_to_all | solution.py:24
  94.1 0.0 copy-done.3
  94.1 0.0 copy-done.4
  94.1 0.6 fusion.68
  94.8 24.5 %all_to_all.37 = bf16[8,4,768]{2,1,0:T(4,128)(2,1)S(1)} all-to-all(bf16[8,4,768]{2,1,0:T(4,128)(2,1)S(1)} %broadcast_in_dim.11), channel_id=1, replica_groups=mesh['xl'=2,'zh'=8,'zl'=4,'c'=2,'y'=4,'xh'=2] {'zh'}, dimensions={0} | all-to-all | bytes 98304 | tf_op jit(solution)/shard_map/all_to_all | solution.py:24
  119.3 8.4 %all_to_all.38 = bf16[4,32,768]{2,1,0:T(8,128)(2,1)S(1)} all-to-all(bf16[4,32,768]{2,1,0:T(8,128)(2,1)S(1)} %broadcast_in_dim.13), channel_id=1, replica_groups=mesh['xl'=2,'zh'=8,'zl'=4,'c'=2,'y'=4,'xh'=2] {'zl'}, dimensions={0} | all-to-all | bytes 393216 | tf_op jit(solution)/shard_map/all_to_all | solution.py:24
  127.7 13.0 %all_gather.3 = bf16[512,768]{1,0:T(8,128)(2,1)S(1)} all-gather(bf16[128,768]{1,0:T(8,128)(2,1)S(1)} %bitcast.54), channel_id=1, replica_groups=mesh['xl'=2,'zh'=8,'zl'=4,'c'=2,'y'=4,'xh'=2] {'xl','c'}, dimensions={0}, use_global_device_ids=true | all-gather | bytes 983040 | tf_op jit(solution)/shard_map/all_gather | solution.py:127
  140.7 0.0 copy-done.1
  140.7 0.2 fusion.2
  141.0 14.3 %all_to_all.39 = f16[8,32,768]{2,1,0:T(8,128)(2,1)S(1)} all-to-all(f16[8,32,768]{2,1,0:T(8,128)(2,1)S(1)} %broadcast_in_dim.14), channel_id=1, replica_groups=mesh['xl'=2,'zh'=8,'zl'=4,'c'=2,'y'=4,'xh'=2] {'y','xh'}, dimensions={0} | all-to-all | bytes 786432 | tf_op jit(solution)/shard_map/all_to_all | solution.py:24
  155.4 0.0 copy-start.2
  155.4 0.9 copy-done.2
  (24 shorter events, 0.3 us)
Async XLA Ops:
  0.6 15.1 %all-to-all-start = ((bf16[8,32,512]{2,1,0:T(8,128)(2,1)}), bf16[8,32,512]{2,1,0:T(8,128)(2,1)S(1)}, u32[]{:S(2)}, u32[]{:S(2)}) async-start(bf16[8,32,512]{2,1,0:T(8,128)(2,1)} %bitcast.55), calls=%async_computation | async-start | bytes 524288 | tf_op jit(solution)/shard_map/all_to_all | solution.py:24
  8.1 28.7 %collective-permute-start.1 = (bf16[256,768]{1,0:T(8,128)(2,1)}, bf16[256,768]{1,0:T(8,128)(2,1)S(1)}, u32[]{:S(2)}, u32[]{:S(2)}) collective-permute-start(bf16[256,768]{1,0:T(8,128)(2,1)} %param.8), channel_id=1, source_target_pairs={{0,512},{512,0},{1,513},{513,1},{2,514},{514,2},{3,515},{515,3},{4... | collective-permute-start | bytes 1179656 | tf_op jit(solution)/shard_map/ppermute | solution.py:20
  15.8 18.9 %copy-start = (bf16[256,768]{1,0:T(8,128)(2,1)S(1)}, bf16[256,768]{1,0:T(8,128)(2,1)}, u32[]{:S(2)}) copy-start(bf16[256,768]{1,0:T(8,128)(2,1)} %param.8) | copy-start | bytes 1179652
  19.0 75.1 %copy-start.3 = (f32[4,768]{1,0:T(4,128)S(1)}, f32[4,768]{1,0:T(4,128)}, u32[]{:S(2)}) copy-start(f32[4,768]{1,0:T(4,128)} %param.10) | copy-start | bytes 36868
  19.1 75.1 %copy-start.4 = (f32[4,768]{1,0:T(4,128)S(1)}, f32[4,768]{1,0:T(4,128)}, u32[]{:S(2)}) copy-start(f32[4,768]{1,0:T(4,128)} %param.11) | copy-start | bytes 36868
  19.1 121.6 %copy-start.1 = (f32[32,768]{1,0:T(8,128)S(1)}, f32[32,768]{1,0:T(8,128)}, u32[]{:S(2)}) copy-start(f32[32,768]{1,0:T(8,128)} %param.9) | copy-start | bytes 294916
  19.9 23.5 %all-to-all-start.1 = ((bf16[32,32,128]{2,1,0:T(8,128)(2,1)}), bf16[32,32,128]{2,1,0:T(8,128)(2,1)S(1)}, u32[]{:S(2)}, u32[]{:S(2)}) async-start(bf16[32,32,128]{2,1,0:T(8,128)(2,1)} %bitcast.4), calls=%async_computation.1 | async-start | bytes 524288 | tf_op jit(solution)/shard_map/all_to_all | solution.py:24
  34.7 9.0 %collective-permute-start = (bf16[256,768]{1,0:T(8,128)(2,1)S(1)}, bf16[256,768]{1,0:T(8,128)(2,1)S(1)}, u32[]{:S(2)}, u32[]{:S(2)}) collective-permute-start(bf16[256,768]{1,0:T(8,128)(2,1)S(1)} %copy-done), channel_id=1, source_target_pairs={{0,8},{8,0},{1,9},{9,1},{2,10},{10,2},{3,11},{11,3},{4,12},{12,4},... | collective-permute-start | bytes 1179656 | tf_op jit(solution)/shard_map/ppermute | solution.py:20
  36.9 7.3 %collective-permute-start.2 = (bf16[256,768]{1,0:T(8,128)(2,1)S(1)}, bf16[256,768]{1,0:T(8,128)(2,1)S(1)}, u32[]{:S(2)}, u32[]{:S(2)}) collective-permute-start(bf16[256,768]{1,0:T(8,128)(2,1)S(1)} %collective-permute-done.1), channel_id=1, source_target_pairs={{0,8},{8,0},{1,9},{9,1},{2,10},{10,2},{3,11},{11,3},{4,12},{12,4},... | collective-permute-start | bytes 1179656 | tf_op jit(solution)/shard_map/ppermute | solution.py:20
  155.4 0.9 copy-start.2

commit v11 on v10

--- a/solution.py
+++ b/solution.py
@@ -81,7 +81,7 @@
             ],
             axis=1,
         )
-        acts, rows = lax.optimization_barrier((acts, rows))
+        acts, rows, order = lax.optimization_barrier((acts, rows, order))
         own = lax.dot_general(
             acts,
             proj_basis.reshape(nf, feats, ranks),

time: 157 us -> 157 us (level)
  no operation moved by 1% of the time
where the time goes in v11:
time: 157 us; the launch traced here: 156 us
  blocking collectives  110 us (70%)
  starting transfers between devices  28.8 us (18%)
  waiting for transfers between devices  7.63 us (5%)
  matrix products  6.21 us (4%)
  local copies, waits for them, and re-layouts  1.77 us (1%)
    all_to_all x5, blocking collectives, exchange(): return lax.all_to_all(x, axis, 0, 0, tiled=False)  97.3 us
    all_to_all x2, starting transfers between devices, exchange(): return lax.all_to_all(x, axis, 0, 0, tiled=False)  22.3 us
    all_gather x1, blocking collectives, body(): full = lax.all_gather(full, ('xl', 'c'), axis=0, tiled=True)  12.7 us
    all_to_all x2, waiting for transfers between devices, exchange(): return lax.all_to_all(x, axis, 0, 0, tiled=False)  7.62 us
    ppermute x3, starting transfers between devices, swap(): return lax.ppermute(x, axis, [(0, 1), (1, 0)])  6.54 us
    dot_general x1, matrix products, body(): own = jnp.dot(own, order, preferred_element_type=f32).astype(bf16)  3.15 us
  transfers between devices with their start and end apart: 5, of which 2 were waited for; matrix products, arithmetic and copies ran while one was open for 4% of the time, Pallas kernels for 0%

profile of v11, /device:TPU:1, one launch (start us, length us, event | category | flops | bytes accessed | tf_op | source)
XLA Modules:
  0.0 156.4 jit_solution(16610360560441480867)
XLA Ops:
  0.6 7.5 %all-to-all-start = ((bf16[8,32,512]{2,1,0:T(8,128)(2,1)}), bf16[8,32,512]{2,1,0:T(8,128)(2,1)S(1)}, u32[]{:S(2)}, u32[]{:S(2)}) async-start(bf16[8,32,512]{2,1,0:T(8,128)(2,1)} %bitcast.57), calls=%async_computation | async-start | bytes 524288 | tf_op jit(solution)/shard_map/all_to_all | solution.py:24
  8.1 2.2 %collective-permute-start.1 = (bf16[256,768]{1,0:T(8,128)(2,1)}, bf16[256,768]{1,0:T(8,128)(2,1)S(1)}, u32[]{:S(2)}, u32[]{:S(2)}) collective-permute-start(bf16[256,768]{1,0:T(8,128)(2,1)} %param.8), channel_id=1, source_target_pairs={{0,512},{512,0},{1,513},{513,1},{2,514},{514,2},{3,515},{515,3},{4... | collective-permute-start | bytes 1179656 | tf_op jit(solution)/shard_map/ppermute | solution.py:20
  10.4 0.2 fusion.23
  10.6 0.9 convolution_convert_fusion.2
  11.5 0.0 copy-start
  11.5 1.0 convolution_convert_fusion.1
  12.5 3.3 %all-to-all-done = bf16[8,32,512]{2,1,0:T(8,128)(2,1)S(1)} async-done(((bf16[8,32,512]{2,1,0:T(8,128)(2,1)}), bf16[8,32,512]{2,1,0:T(8,128)(2,1)S(1)}, u32[]{:S(2)}, u32[]{:S(2)}) %all-to-all-start) | async-done | bytes 262176 | tf_op jit(solution)/shard_map/all_to_all | solution.py:24
  15.8 3.2 %convolution_convert_fusion = bf16[32,512]{1,0:T(8,128)(2,1)S(1)} fusion(bf16[512,512]{1,0:T(8,128)(2,1)S(1)} %fusion.23, bf16[8,32,512]{2,1,0:T(8,128)(2,1)S(1)} %all-to-all-done, bf16[8,512,512]{2,1,0:T(8,128)(2,1)} %bitcast.50), kind=kOutput, calls=%fused_computation.27 | convolution fusion | flops 151027712 | bytes 5013504 | tf_op jit(solution)/shard_map/dot_general | solution.py:91
  18.9 0.0 copy-start.3
  18.9 0.0 copy-start.4
  18.9 0.0 copy-start.1
  19.0 0.7 broadcast_in_dim.10
  19.7 14.8 %all-to-all-start.1 = ((bf16[32,32,128]{2,1,0:T(8,128)(2,1)}), bf16[32,32,128]{2,1,0:T(8,128)(2,1)S(1)}, u32[]{:S(2)}, u32[]{:S(2)}) async-start(bf16[32,32,128]{2,1,0:T(8,128)(2,1)} %bitcast.4), calls=%async_computation.1 | async-start | bytes 524288 | tf_op jit(solution)/shard_map/all_to_all | solution.py:24
  34.5 0.0 copy-done
  34.5 2.2 %collective-permute-start = (bf16[256,768]{1,0:T(8,128)(2,1)S(1)}, bf16[256,768]{1,0:T(8,128)(2,1)S(1)}, u32[]{:S(2)}, u32[]{:S(2)}) collective-permute-start(bf16[256,768]{1,0:T(8,128)(2,1)S(1)} %copy-done), channel_id=1, source_target_pairs={{0,8},{8,0},{1,9},{9,1},{2,10},{10,2},{3,11},{11,3},{4,12},{12,4},... | collective-permute-start | bytes 1179656 | tf_op jit(solution)/shard_map/ppermute | solution.py:20
  36.7 0.0 collective-permute-done.1
  36.7 2.2 %collective-permute-start.2 = (bf16[256,768]{1,0:T(8,128)(2,1)S(1)}, bf16[256,768]{1,0:T(8,128)(2,1)S(1)}, u32[]{:S(2)}, u32[]{:S(2)}) collective-permute-start(bf16[256,768]{1,0:T(8,128)(2,1)S(1)} %collective-permute-done.1), channel_id=1, source_target_pairs={{0,8},{8,0},{1,9},{9,1},{2,10},{10,2},{3,11},{11,3},{4,12},{12,4},... | collective-permute-start | bytes 1179656 | tf_op jit(solution)/shard_map/ppermute | solution.py:20
  38.9 4.3 %all-to-all-done.1 = bf16[32,32,128]{2,1,0:T(8,128)(2,1)S(1)} async-done(((bf16[32,32,128]{2,1,0:T(8,128)(2,1)}), bf16[32,32,128]{2,1,0:T(8,128)(2,1)S(1)}, u32[]{:S(2)}, u32[]{:S(2)}) %all-to-all-start.1) | async-done | bytes 262176 | tf_op jit(solution)/shard_map/all_to_all | solution.py:24
  43.3 0.2 fusion.42
  43.5 0.0 collective-permute-done
  43.5 0.2 convolution_add_fusion.2
  43.8 0.2 convolution_add_fusion.1
  44.0 0.0 collective-permute-done.2
  44.0 0.2 fusion
  44.3 9.4 %all_to_all.35 = bf16[4,32,768]{2,1,0:T(8,128)(2,1)S(1)} all-to-all(bf16[4,32,768]{2,1,0:T(8,128)(2,1)S(1)} %bitcast.55), channel_id=1, replica_groups=mesh['xl'=2,'zh'=8,'zl'=4,'c'=2,'y'=4,'xh'=2] {'zl'}, dimensions={0} | all-to-all | bytes 393216 | tf_op jit(solution)/shard_map/all_to_all | solution.py:24
  53.7 41.8 %all_to_all.36 = bf16[8,4,768]{2,1,0:T(4,128)(2,1)S(1)} all-to-all(bf16[8,4,768]{2,1,0:T(4,128)(2,1)S(1)} %convert_element_type.75), channel_id=1, replica_groups=mesh['xl'=2,'zh'=8,'zl'=4,'c'=2,'y'=4,'xh'=2] {'zh'}, dimensions={0} | all-to-all | bytes 98304 | tf_op jit(solution)/shard_map/all_to_all | solution.py:24
  95.6 0.0 copy-done.3
  95.6 0.0 copy-done.4
  95.6 0.6 fusion.51
  96.2 24.0 %all_to_all.37 = bf16[8,4,768]{2,1,0:T(4,128)(2,1)S(1)} all-to-all(bf16[8,4,768]{2,1,0:T(4,128)(2,1)S(1)} %broadcast_in_dim.11), channel_id=1, replica_groups=mesh['xl'=2,'zh'=8,'zl'=4,'c'=2,'y'=4,'xh'=2] {'zh'}, dimensions={0} | all-to-all | bytes 98304 | tf_op jit(solution)/shard_map/all_to_all | solution.py:24
  120.3 8.0 %all_to_all.38 = bf16[4,32,768]{2,1,0:T(8,128)(2,1)S(1)} all-to-all(bf16[4,32,768]{2,1,0:T(8,128)(2,1)S(1)} %broadcast_in_dim.13), channel_id=1, replica_groups=mesh['xl'=2,'zh'=8,'zl'=4,'c'=2,'y'=4,'xh'=2] {'zl'}, dimensions={0} | all-to-all | bytes 393216 | tf_op jit(solution)/shard_map/all_to_all | solution.py:24
  128.3 12.7 %all_gather.3 = bf16[512,768]{1,0:T(8,128)(2,1)S(1)} all-gather(bf16[128,768]{1,0:T(8,128)(2,1)S(1)} %bitcast.56), channel_id=1, replica_groups=mesh['xl'=2,'zh'=8,'zl'=4,'c'=2,'y'=4,'xh'=2] {'xl','c'}, dimensions={0}, use_global_device_ids=true | all-gather | bytes 983040 | tf_op jit(solution)/shard_map/all_gather | solution.py:127
  140.9 0.0 copy-done.1
  140.9 0.2 fusion.2
  141.2 14.1 %all_to_all.39 = f16[8,32,768]{2,1,0:T(8,128)(2,1)S(1)} all-to-all(f16[8,32,768]{2,1,0:T(8,128)(2,1)S(1)} %broadcast_in_dim.14), channel_id=1, replica_groups=mesh['xl'=2,'zh'=8,'zl'=4,'c'=2,'y'=4,'xh'=2] {'y','xh'}, dimensions={0} | all-to-all | bytes 786432 | tf_op jit(solution)/shard_map/all_to_all | solution.py:24
  155.5 0.0 copy-start.2
  155.5 0.9 copy-done.2
  (24 shorter events, 0.3 us)
Async XLA Ops:
  0.6 15.1 %all-to-all-start = ((bf16[8,32,512]{2,1,0:T(8,128)(2,1)}), bf16[8,32,512]{2,1,0:T(8,128)(2,1)S(1)}, u32[]{:S(2)}, u32[]{:S(2)}) async-start(bf16[8,32,512]{2,1,0:T(8,128)(2,1)} %bitcast.57), calls=%async_computation | async-start | bytes 524288 | tf_op jit(solution)/shard_map/all_to_all | solution.py:24
  8.1 28.6 %collective-permute-start.1 = (bf16[256,768]{1,0:T(8,128)(2,1)}, bf16[256,768]{1,0:T(8,128)(2,1)S(1)}, u32[]{:S(2)}, u32[]{:S(2)}) collective-permute-start(bf16[256,768]{1,0:T(8,128)(2,1)} %param.8), channel_id=1, source_target_pairs={{0,512},{512,0},{1,513},{513,1},{2,514},{514,2},{3,515},{515,3},{4... | collective-permute-start | bytes 1179656 | tf_op jit(solution)/shard_map/ppermute | solution.py:20
  11.5 23.0 %copy-start = (bf16[256,768]{1,0:T(8,128)(2,1)S(1)}, bf16[256,768]{1,0:T(8,128)(2,1)}, u32[]{:S(2)}) copy-start(bf16[256,768]{1,0:T(8,128)(2,1)} %param.8) | copy-start | bytes 1179652
  18.9 76.7 %copy-start.3 = (f32[4,768]{1,0:T(4,128)S(1)}, f32[4,768]{1,0:T(4,128)}, u32[]{:S(2)}) copy-start(f32[4,768]{1,0:T(4,128)} %param.10) | copy-start | bytes 36868
  18.9 76.7 %copy-start.4 = (f32[4,768]{1,0:T(4,128)S(1)}, f32[4,768]{1,0:T(4,128)}, u32[]{:S(2)}) copy-start(f32[4,768]{1,0:T(4,128)} %param.11) | copy-start | bytes 36868
  18.9 122.0 %copy-start.1 = (f32[32,768]{1,0:T(8,128)S(1)}, f32[32,768]{1,0:T(8,128)}, u32[]{:S(2)}) copy-start(f32[32,768]{1,0:T(8,128)} %param.9) | copy-start | bytes 294916
  19.7 23.5 %all-to-all-start.1 = ((bf16[32,32,128]{2,1,0:T(8,128)(2,1)}), bf16[32,32,128]{2,1,0:T(8,128)(2,1)S(1)}, u32[]{:S(2)}, u32[]{:S(2)}) async-start(bf16[32,32,128]{2,1,0:T(8,128)(2,1)} %bitcast.4), calls=%async_computation.1 | async-start | bytes 524288 | tf_op jit(solution)/shard_map/all_to_all | solution.py:24
  34.5 9.0 %collective-permute-start = (bf16[256,768]{1,0:T(8,128)(2,1)S(1)}, bf16[256,768]{1,0:T(8,128)(2,1)S(1)}, u32[]{:S(2)}, u32[]{:S(2)}) collective-permute-start(bf16[256,768]{1,0:T(8,128)(2,1)S(1)} %copy-done), channel_id=1, source_target_pairs={{0,8},{8,0},{1,9},{9,1},{2,10},{10,2},{3,11},{11,3},{4,12},{12,4},... | collective-permute-start | bytes 1179656 | tf_op jit(solution)/shard_map/ppermute | solution.py:20
  36.7 7.3 %collective-permute-start.2 = (bf16[256,768]{1,0:T(8,128)(2,1)S(1)}, bf16[256,768]{1,0:T(8,128)(2,1)S(1)}, u32[]{:S(2)}, u32[]{:S(2)}) collective-permute-start(bf16[256,768]{1,0:T(8,128)(2,1)S(1)} %collective-permute-done.1), channel_id=1, source_target_pairs={{0,8},{8,0},{1,9},{9,1},{2,10},{10,2},{3,11},{11,3},{4,12},{12,4},... | collective-permute-start | bytes 1179656 | tf_op jit(solution)/shard_map/ppermute | solution.py:20
  155.5 0.9 copy-start.2

commit v12 on v10

--- a/solution.py
+++ b/solution.py
@@ -98,7 +98,7 @@
         me = lax.axis_index("c") * xl + lax.axis_index("xl")
         og_x = swap(out_grad, "xl")
         og_c = swap(out_grad, "c")
-        og_xc = swap(og_x, "c")
+        og_xc = swap(og_c, "xl")
         blocks = ((me, out_grad), (me ^ 2, og_c), (me ^ 1, og_x), (me ^ 3, og_xc))
         grad = sum(
             lax.dot_general(

time: 157 us -> 171 us (1.089)
  waiting for transfers between devices: 7.87 us -> 15.9 us
  starting transfers between devices: 28.8 us -> 33.3 us
  blocking collectives: 110 us -> 112 us
    ppermute x3, waiting for transfers between devices: 0.01 us -> 12.6 us  [swap(): return lax.ppermute(x, axis, [(0, 1), (1, 0)])]
    ppermute x3, starting transfers between devices: 6.54 us -> 17.3 us  [swap(): return lax.ppermute(x, axis, [(0, 1), (1, 0)])]
    all_to_all x2, starting transfers between devices: 22.3 us -> 16 us  [exchange(): return lax.all_to_all(x, axis, 0, 0, tiled=False)]
    all_to_all x2, waiting for transfers between devices: 7.86 us -> 3.39 us  [exchange(): return lax.all_to_all(x, axis, 0, 0, tiled=False)]
    all_to_all x5, blocking collectives: 96.8 us -> 98.8 us  [exchange(): return lax.all_to_all(x, axis, 0, 0, tiled=False)]
  transfers between devices with their start and end apart: 5 -> 5, of which waited for: 2 -> 3; matrix products, arithmetic and copies ran while one was open for 4% -> 4% of each run, Pallas kernels for 0% -> 0%
where the time goes in v12:
time: 171 us
  blocking collectives  112 us (65%)
  starting transfers between devices  33.3 us (19%)
  waiting for transfers between devices  15.9 us (9%)
  matrix products  6.28 us (4%)
  local copies, waits for them, and re-layouts  1.76 us (1%)
    all_to_all x5, blocking collectives, exchange(): return lax.all_to_all(x, axis, 0, 0, tiled=False)  98.8 us
    ppermute x3, starting transfers between devices, swap(): return lax.ppermute(x, axis, [(0, 1), (1, 0)])  17.3 us
    all_to_all x2, starting transfers between devices, exchange(): return lax.all_to_all(x, axis, 0, 0, tiled=False)  16 us
    all_gather x1, blocking collectives, body(): full = lax.all_gather(full, ('xl', 'c'), axis=0, tiled=True)  13 us
    ppermute x3, waiting for transfers between devices, swap(): return lax.ppermute(x, axis, [(0, 1), (1, 0)])  12.6 us
  transfers between devices with their start and end apart: 5, of which 3 were waited for; matrix products, arithmetic and copies ran while one was open for 4% of the time, Pallas kernels for 0%

profile of v12, /device:TPU:1, one launch (start us, length us, event | category | flops | bytes accessed | tf_op | source)
XLA Modules:
  0.0 170.8 jit_solution(11874005801403067705)
XLA Ops:
  0.6 7.5 %all-to-all-start = ((bf16[8,32,512]{2,1,0:T(8,128)(2,1)}), bf16[8,32,512]{2,1,0:T(8,128)(2,1)S(1)}, u32[]{:S(2)}, u32[]{:S(2)}) async-start(bf16[8,32,512]{2,1,0:T(8,128)(2,1)} %bitcast.55), calls=%async_computation | async-start | bytes 524288 | tf_op jit(solution)/shard_map/all_to_all | solution.py:24
  8.1 12.0 %collective-permute-start = (bf16[256,768]{1,0:T(8,128)(2,1)}, bf16[256,768]{1,0:T(8,128)(2,1)S(1)}, u32[]{:S(2)}, u32[]{:S(2)}) collective-permute-start(bf16[256,768]{1,0:T(8,128)(2,1)} %param.8), channel_id=1, source_target_pairs={{0,8},{8,0},{1,9},{9,1},{2,10},{10,2},{3,11},{11,3},{4,12},{12,4},... | collective-permute-start | bytes 1179656 | tf_op jit(solution)/shard_map/ppermute | solution.py:20
  20.2 0.9 convolution_convert_fusion.2
  21.1 0.9 convolution_convert_fusion.1
  22.0 0.0 all-to-all-done
  22.0 0.0 copy-start
  22.1 3.3 %convolution_convert_fusion = bf16[32,512]{1,0:T(8,128)(2,1)S(1)} fusion(bf16[8,32,512]{2,1,0:T(8,128)(2,1)S(1)} %all-to-all-done, bf16[8,512,512]{2,1,0:T(8,128)(2,1)} %bitcast.57, s32[512]{0:T(512)S(1)} %get-tuple-element.19, s32[512]{0:T(512)S(1)} %get-tuple-element.20, s32[512]{0:T(512)S(1)} %get-tuple-element.18, s32[512]{0:T(512)S(1)} %get-tuple-element.21, ...), kind=kOutput, calls=%fused_computation.26 | convolution fusion | flops 168853504 | bytes 4498432 | tf_op jit(solution)/shard_map/dot_general | solution.py:91
  25.3 0.0 copy-start.3
  25.4 0.0 copy-start.4
  25.4 0.0 copy-start.1
  25.4 0.7 broadcast_in_dim.10
  26.2 8.5 %all-to-all-start.1 = ((bf16[32,32,128]{2,1,0:T(8,128)(2,1)}), bf16[32,32,128]{2,1,0:T(8,128)(2,1)S(1)}, u32[]{:S(2)}, u32[]{:S(2)}) async-start(bf16[32,32,128]{2,1,0:T(8,128)(2,1)} %bitcast.4), calls=%async_computation.1 | async-start | bytes 524288 | tf_op jit(solution)/shard_map/all_to_all | solution.py:24
  34.7 0.0 copy-done
  34.7 3.3 %collective-permute-start.1 = (bf16[256,768]{1,0:T(8,128)(2,1)S(1)}, bf16[256,768]{1,0:T(8,128)(2,1)S(1)}, u32[]{:S(2)}, u32[]{:S(2)}) collective-permute-start(bf16[256,768]{1,0:T(8,128)(2,1)S(1)} %copy-done), channel_id=1, source_target_pairs={{0,512},{512,0},{1,513},{513,1},{2,514},{514,2},{3,515},{515,3},{4... | collective-permute-start | bytes 1179656 | tf_op jit(solution)/shard_map/ppermute | solution.py:20
  38.0 0.0 collective-permute-done
  38.0 2.0 %collective-permute-start.2 = (bf16[256,768]{1,0:T(8,128)(2,1)S(1)}, bf16[256,768]{1,0:T(8,128)(2,1)S(1)}, u32[]{:S(2)}, u32[]{:S(2)}) collective-permute-start(bf16[256,768]{1,0:T(8,128)(2,1)S(1)} %collective-permute-done), channel_id=1, source_target_pairs={{0,512},{512,0},{1,513},{513,1},{2,514},{514,2},{3,515},{515,3},{4... | collective-permute-start | bytes 1179656 | tf_op jit(solution)/shard_map/ppermute | solution.py:20
  40.0 3.4 %all-to-all-done.1 = bf16[32,32,128]{2,1,0:T(8,128)(2,1)S(1)} async-done(((bf16[32,32,128]{2,1,0:T(8,128)(2,1)}), bf16[32,32,128]{2,1,0:T(8,128)(2,1)S(1)}, u32[]{:S(2)}, u32[]{:S(2)}) %all-to-all-start.1) | async-done | bytes 262176 | tf_op jit(solution)/shard_map/all_to_all | solution.py:24
  43.4 0.2 fusion.59
  43.6 0.2 convolution_add_fusion.2
  43.9 4.4 %collective-permute-done.1 = bf16[256,768]{1,0:T(8,128)(2,1)S(1)} collective-permute-done((bf16[256,768]{1,0:T(8,128)(2,1)S(1)}, bf16[256,768]{1,0:T(8,128)(2,1)S(1)}, u32[]{:S(2)}, u32[]{:S(2)}) %collective-permute-start.1) | collective-permute-done | bytes 393248 | tf_op jit(solution)/shard_map/ppermute | solution.py:20
  48.3 0.2 convolution_add_fusion.1
  48.5 8.2 %collective-permute-done.2 = bf16[256,768]{1,0:T(8,128)(2,1)S(1)} collective-permute-done((bf16[256,768]{1,0:T(8,128)(2,1)S(1)}, bf16[256,768]{1,0:T(8,128)(2,1)S(1)}, u32[]{:S(2)}, u32[]{:S(2)}) %collective-permute-start.2) | collective-permute-done | bytes 393248 | tf_op jit(solution)/shard_map/ppermute | solution.py:20
  56.7 0.2 fusion
  56.9 8.1 %all_to_all.35 = bf16[4,32,768]{2,1,0:T(8,128)(2,1)S(1)} all-to-all(bf16[4,32,768]{2,1,0:T(8,128)(2,1)S(1)} %bitcast.53), channel_id=1, replica_groups=mesh['xl'=2,'zh'=8,'zl'=4,'c'=2,'y'=4,'xh'=2] {'zl'}, dimensions={0} | all-to-all | bytes 393216 | tf_op jit(solution)/shard_map/all_to_all | solution.py:24
  65.1 42.6 %all_to_all.36 = bf16[8,4,768]{2,1,0:T(4,128)(2,1)S(1)} all-to-all(bf16[8,4,768]{2,1,0:T(4,128)(2,1)S(1)} %convert_element_type.72), channel_id=1, replica_groups=mesh['xl'=2,'zh'=8,'zl'=4,'c'=2,'y'=4,'xh'=2] {'zh'}, dimensions={0} | all-to-all | bytes 98304 | tf_op jit(solution)/shard_map/all_to_all | solution.py:24
  107.7 0.0 copy-done.3
  107.7 0.0 copy-done.4
  107.7 0.6 fusion.68
  108.3 24.0 %all_to_all.37 = bf16[8,4,768]{2,1,0:T(4,128)(2,1)S(1)} all-to-all(bf16[8,4,768]{2,1,0:T(4,128)(2,1)S(1)} %broadcast_in_dim.11), channel_id=1, replica_groups=mesh['xl'=2,'zh'=8,'zl'=4,'c'=2,'y'=4,'xh'=2] {'zh'}, dimensions={0} | all-to-all | bytes 98304 | tf_op jit(solution)/shard_map/all_to_all | solution.py:24
  132.3 8.3 %all_to_all.38 = bf16[4,32,768]{2,1,0:T(8,128)(2,1)S(1)} all-to-all(bf16[4,32,768]{2,1,0:T(8,128)(2,1)S(1)} %broadcast_in_dim.13), channel_id=1, replica_groups=mesh['xl'=2,'zh'=8,'zl'=4,'c'=2,'y'=4,'xh'=2] {'zl'}, dimensions={0} | all-to-all | bytes 393216 | tf_op jit(solution)/shard_map/all_to_all | solution.py:24
  140.7 13.0 %all_gather.3 = bf16[512,768]{1,0:T(8,128)(2,1)S(1)} all-gather(bf16[128,768]{1,0:T(8,128)(2,1)S(1)} %bitcast.54), channel_id=1, replica_groups=mesh['xl'=2,'zh'=8,'zl'=4,'c'=2,'y'=4,'xh'=2] {'xl','c'}, dimensions={0}, use_global_device_ids=true | all-gather | bytes 983040 | tf_op jit(solution)/shard_map/all_gather | solution.py:127
  153.6 0.0 copy-done.1
  153.6 0.2 fusion.2
  153.9 15.8 %all_to_all.39 = f16[8,32,768]{2,1,0:T(8,128)(2,1)S(1)} all-to-all(f16[8,32,768]{2,1,0:T(8,128)(2,1)S(1)} %broadcast_in_dim.14), channel_id=1, replica_groups=mesh['xl'=2,'zh'=8,'zl'=4,'c'=2,'y'=4,'xh'=2] {'y','xh'}, dimensions={0} | all-to-all | bytes 786432 | tf_op jit(solution)/shard_map/all_to_all | solution.py:24
  169.9 0.0 copy-start.2
  169.9 0.9 copy-done.2
  (24 shorter events, 0.3 us)
Async XLA Ops:
  0.6 21.4 %all-to-all-start = ((bf16[8,32,512]{2,1,0:T(8,128)(2,1)}), bf16[8,32,512]{2,1,0:T(8,128)(2,1)S(1)}, u32[]{:S(2)}, u32[]{:S(2)}) async-start(bf16[8,32,512]{2,1,0:T(8,128)(2,1)} %bitcast.55), calls=%async_computation | async-start | bytes 524288 | tf_op jit(solution)/shard_map/all_to_all | solution.py:24
  8.1 29.9 %collective-permute-start = (bf16[256,768]{1,0:T(8,128)(2,1)}, bf16[256,768]{1,0:T(8,128)(2,1)S(1)}, u32[]{:S(2)}, u32[]{:S(2)}) collective-permute-start(bf16[256,768]{1,0:T(8,128)(2,1)} %param.8), channel_id=1, source_target_pairs={{0,8},{8,0},{1,9},{9,1},{2,10},{10,2},{3,11},{11,3},{4,12},{12,4},... | collective-permute-start | bytes 1179656 | tf_op jit(solution)/shard_map/ppermute | solution.py:20
  22.0 12.6 %copy-start = (bf16[256,768]{1,0:T(8,128)(2,1)S(1)}, bf16[256,768]{1,0:T(8,128)(2,1)}, u32[]{:S(2)}) copy-start(bf16[256,768]{1,0:T(8,128)(2,1)} %param.8) | copy-start | bytes 1179652
  25.3 82.3 %copy-start.3 = (f32[4,768]{1,0:T(4,128)S(1)}, f32[4,768]{1,0:T(4,128)}, u32[]{:S(2)}) copy-start(f32[4,768]{1,0:T(4,128)} %param.10) | copy-start | bytes 36868
  25.4 82.3 %copy-start.4 = (f32[4,768]{1,0:T(4,128)S(1)}, f32[4,768]{1,0:T(4,128)}, u32[]{:S(2)}) copy-start(f32[4,768]{1,0:T(4,128)} %param.11) | copy-start | bytes 36868
  25.4 128.3 %copy-start.1 = (f32[32,768]{1,0:T(8,128)S(1)}, f32[32,768]{1,0:T(8,128)}, u32[]{:S(2)}) copy-start(f32[32,768]{1,0:T(8,128)} %param.9) | copy-start | bytes 294916
  26.2 17.2 %all-to-all-start.1 = ((bf16[32,32,128]{2,1,0:T(8,128)(2,1)}), bf16[32,32,128]{2,1,0:T(8,128)(2,1)S(1)}, u32[]{:S(2)}, u32[]{:S(2)}) async-start(bf16[32,32,128]{2,1,0:T(8,128)(2,1)} %bitcast.4), calls=%async_computation.1 | async-start | bytes 524288 | tf_op jit(solution)/shard_map/all_to_all | solution.py:24
  34.7 13.6 %collective-permute-start.1 = (bf16[256,768]{1,0:T(8,128)(2,1)S(1)}, bf16[256,768]{1,0:T(8,128)(2,1)S(1)}, u32[]{:S(2)}, u32[]{:S(2)}) collective-permute-start(bf16[256,768]{1,0:T(8,128)(2,1)S(1)} %copy-done), channel_id=1, source_target_pairs={{0,512},{512,0},{1,513},{513,1},{2,514},{514,2},{3,515},{515,3},{4... | collective-permute-start | bytes 1179656 | tf_op jit(solution)/shard_map/ppermute | solution.py:20
  38.0 18.7 %collective-permute-start.2 = (bf16[256,768]{1,0:T(8,128)(2,1)S(1)}, bf16[256,768]{1,0:T(8,128)(2,1)S(1)}, u32[]{:S(2)}, u32[]{:S(2)}) collective-permute-start(bf16[256,768]{1,0:T(8,128)(2,1)S(1)} %collective-permute-done), channel_id=1, source_target_pairs={{0,512},{512,0},{1,513},{513,1},{2,514},{514,2},{3,515},{515,3},{4... | collective-permute-start | bytes 1179656 | tf_op jit(solution)/shard_map/ppermute | solution.py:20
  169.9 0.9 copy-start.2
